TPU v7x, 128 devices: a whole 4x4x4 slice. The times are simulated.
128 devices in a mesh: band: 16 (over y, x), obs: 8 (over z, core).
Axes of the slice: x: 4, y: 4, z: 4, core: 2. Of those that a mesh axis runs over, the one named last changes fastest.
Arguments:
- obs_values: bfloat16 [24, 262144], P(None, ('band', 'obs')), may hold values from -6 to 6
- obs_tile: int32 [262144], P(('band', 'obs')), may hold values from 0 to 255, as said below
- obs_row: int32 [262144], P(('band', 'obs')), may hold values from 0 to 31
- obs_col: int32 [262144], P(('band', 'obs')), may hold values from 0 to 89
- obs_frac: float32 [2, 262144], P(None, ('band', 'obs')), may hold values from 0 to 1
- tile_place: int32 [256], replicated, may hold values from 0 to 255, as said below
- length_scale: float32 [2], replicated, may hold values from 0.8 to 1.4
- conv_weight: bfloat16 [5, 5, 25, 256], replicated, may hold values from -0.25 to 0.25
- conv_bias: float32 [256], replicated, may hold values from -1.5 to 1.5
Outputs:
- encoded: bfloat16 [256, 720, 256], P(('band', 'obs'))
Inputs may be any that keep to these rules, and one draw needn't show every extreme that they name: `obs_tile`: the owner of tile t is t mod 16. Among the 2048 observations of one device, at most 512 lie in tiles of one owner; one owner, the same for all devices, has exactly 512 from every device. tile_place is a permutation; the tiles d + 16 k of one owner d lie in 16 different latitude bands.
All inputs are finite; a program needn't handle non-finite values.
Results may differ from a plain program's by a relative error of at most 0.0057.
Values may be sent and summed in bfloat16 or wider, within the bound.
No kernel may reach another device: no remote copies, remote signals or barrier semaphores. Data moves between devices by JAX's collectives and lax.ppermute only.
A program may use at most 128 MiB of HBM per device.

v0:
```python
import jax
import jax.numpy as jnp
from jax import lax
from jax.sharding import PartitionSpec as P

LON = 1440
ROWS_DEV = 4


def from_behind(value, axis, steps):
    count = lax.axis_size(axis)
    first, last = (max(0, -steps), min(count, count - steps))
    return lax.ppermute(value, axis, [(source, source + steps) for source in range(first, last)])


def body(
    obs_values,
    obs_tile,
    obs_row,
    obs_col,
    obs_frac,
    tile_place,
    length_scale,
    conv_weight,
    conv_bias,
):
    band_count = lax.axis_size("band")
    obs_count = lax.axis_size("obs")
    arrivals = obs_tile.shape[0]
    capacity = arrivals // 4
    channels = obs_values.shape[0]
    lat_dev = ROWS_DEV * obs_count
    tile_width = LON // band_count
    band_ids = jnp.arange(band_count, dtype=jnp.int32)
    owner_band = obs_tile % band_count
    within = obs_tile // band_count
    member = (owner_band[:, None] == band_ids[None, :]).astype(jnp.int32)
    slot_rank = jnp.sum(jnp.cumsum(member, axis=0) * member, axis=1) - 1
    target = owner_band * capacity + slot_rank
    payload = jnp.concatenate(
        [
            obs_values.astype(jnp.float32),
            (obs_row.astype(jnp.float32) + obs_frac[0])[None],
            (obs_col.astype(jnp.float32) + obs_frac[1])[None],
            within.astype(jnp.float32)[None],
        ],
        axis=0,
    )
    outbox = (
        jnp.zeros((channels + 3, band_count * capacity), jnp.float32).at[channels + 2].set(-1.0)
    )
    outbox = outbox.at[:, target].set(payload)
    arrived_obs = lax.all_to_all(
        outbox.reshape(channels + 3, band_count, capacity),
        "band",
        split_axis=1,
        concat_axis=1,
        tiled=True,
    )
    inv_lat = 0.5 / (length_scale[0] * length_scale[0])
    inv_lon = 0.5 / (length_scale[1] * length_scale[1])
    row_mid = jnp.arange(lat_dev, dtype=jnp.float32) + 0.5
    col_mid = jnp.arange(tile_width, dtype=jnp.float32) + 0.5
    tile_codes = band_ids.astype(jnp.float32)

    def accumulate(source, running):
        source_block = lax.dynamic_index_in_dim(arrived_obs, source, 1, keepdims=False)
        lat_at = source_block[channels]
        lon_at = source_block[channels + 1]
        slot_at = source_block[channels + 2]
        lat_diff = row_mid[:, None] - lat_at[None, :]
        lon_diff = col_mid[:, None] - lon_at[None, :]
        lat_weight = jnp.exp(-(lat_diff * lat_diff) * inv_lat)
        lon_weight = jnp.exp(-(lon_diff * lon_diff) * inv_lon)
        extended = jnp.concatenate(
            [source_block[:channels], jnp.ones((1, capacity), jnp.float32)], axis=0
        )
        left_factor = (
            (extended[:, None, :] * lat_weight[None])
            .astype(jnp.bfloat16)
            .reshape((channels + 1) * lat_dev, capacity)
        )
        tile_pick = (slot_at[None, :] == tile_codes[:, None]).astype(jnp.float32)
        right_factor = (
            (tile_pick[:, None, :] * lon_weight[None])
            .astype(jnp.bfloat16)
            .reshape(band_count * tile_width, capacity)
        )
        return running + lax.dot_general(
            left_factor, right_factor, (((1,), (1,)), ((), ())), preferred_element_type=jnp.float32
        )

    grid_sums = lax.fori_loop(
        0, band_count, accumulate, jnp.zeros(((channels + 1) * lat_dev, LON), jnp.float32)
    )
    grid_sums = grid_sums.reshape(channels + 1, lat_dev, band_count, tile_width)
    my_band = lax.axis_index("band")
    place_table = tile_place.reshape(band_count, band_count)
    bands_of = place_table // band_count
    blocks_of = place_table % band_count
    my_bands = lax.dynamic_index_in_dim(bands_of, my_band, 1, keepdims=False)
    send_order = jnp.sum(
        (my_bands[None, :] == band_ids[:, None]).astype(jnp.int32) * band_ids[None, :], axis=1
    )
    outgoing = jnp.take(grid_sums, send_order, axis=2)
    matched = (bands_of == my_band).astype(jnp.int32)
    block_of_source = jnp.sum(matched * blocks_of, axis=0)
    source_of_block = jnp.sum(
        (block_of_source[None, :] == band_ids[:, None]).astype(jnp.int32) * band_ids[None, :],
        axis=1,
    )
    arrived = lax.all_to_all(outgoing, "band", split_axis=2, concat_axis=2, tiled=True)
    placed = jnp.take(arrived, source_of_block, axis=2).reshape(channels + 1, lat_dev, LON)
    band_rows = lax.psum_scatter(placed, "obs", scatter_dimension=1, tiled=True)
    density = band_rows[channels]
    feature = jnp.concatenate(
        [band_rows[:channels] / jnp.maximum(density, 1.0)[None], jnp.log(1.0 + density)[None]],
        axis=0,
    ).astype(jnp.bfloat16)
    rim_lower = from_behind(feature[:, -2:, :], ("band", "obs"), 1)
    rim_upper = from_behind(feature[:, :1, :], ("band", "obs"), -1)
    stacked = jnp.concatenate([rim_lower, feature, rim_upper], axis=1)
    wrapped = jnp.concatenate([stacked[:, :, -2:], stacked, stacked[:, :, :2]], axis=2)
    conv_out = lax.conv_general_dilated(
        wrapped[None],
        conv_weight,
        (2, 2),
        "VALID",
        dimension_numbers=("NCHW", "HWIO", "NHWC"),
        preferred_element_type=jnp.float32,
    )[0]
    return (conv_out + conv_bias).astype(jnp.bfloat16)


def solution(mesh):
    placed = (
        P(None, ("band", "obs")),
        P(("band", "obs")),
        P(("band", "obs")),
        P(("band", "obs")),
        P(None, ("band", "obs")),
        P(),
        P(),
        P(),
        P(),
    )
    return jax.shard_map(
        body, mesh=mesh, in_specs=placed, out_specs=P(("band", "obs"), None, None), check_vma=False
    )
```

profile of v0, /device:TPU:8, one launch (start us, length us, event | category | flops | bytes accessed | tf_op | source)
XLA Modules:
  0.0 478.7 jit_solution(16508290142636141292)
XLA Ops:
  7.3 4.5 reduce-window.6
  14.2 0.9 convert_element_type.73
  16.9 4.4 copy.63
  21.3 9.6 %scatter_fusion = f32[27,8192]{0,1:T(8,128)} fusion(f32[27,8192]{0,1:T(8,128)} %copy.63, s32[2048]{0:T(1024)S(1)} %get-tuple-element.214, f32[2048,27]{1,0:T(8,128)S(1)} %copy.36), kind=kCustom, calls=%fused_computation.2 | custom fusion | bytes 671744 | tf_op jit(solution)/shard_map/scatter | solution.py:52
  30.9 3.7 copy.37
  34.6 7.4 %all-to-all-start = ((f32[27,16,512]{2,0,1:T(8,128)}), f32[27,16,512]{2,0,1:T(8,128)S(1)}, u32[]{:S(2)}, u32[]{:S(2)}) async-start(f32[27,16,512]{2,0,1:T(8,128)} %copy.37), calls=%async_computation | async-start | bytes 2097152 | tf_op jit(solution)/shard_map/all_to_all | solution.py:53
  45.7 10.9 %all-to-all-done = f32[27,16,512]{2,0,1:T(8,128)S(1)} async-done(((f32[27,16,512]{2,0,1:T(8,128)}), f32[27,16,512]{2,0,1:T(8,128)S(1)}, u32[]{:S(2)}, u32[]{:S(2)}) %all-to-all-start) | async-done | bytes 884768 | tf_op jit(solution)/shard_map/all_to_all | solution.py:53
  56.6 1.5 copy.38
  58.1 145.0 %while.15 = (s32[]{:T(128)}, f32[800,1440]{1,0:T(8,128)}, f32[27,16,512]{2,1,0:T(8,128)}, f32[]{:T(128)}, f32[]{:T(128)}, /*index=5*/s32[]{:T(128)}, s32[]{:T(128)}, s32[]{}, s32[]{}, s32[]{}, /*index=10*/f32[]{:T(128)}) while((s32[]{:T(128)}, f32[800,1440]{1,0:T(8,128)}, f32[27,16,512]{2,1,0:T(8,128)}, f32[]{:T(128)}, f32[]{:T(128)}, ...), condition=%wide.region_5.6_spmd.clone, body=%wide.region_4.5_spmd.clone.sunk | while | flops 1184512128 | bytes 17685772 | solution.py:93
  60.0 1.0 constant_dynamic-slice_fusion.7
  61.2 3.7 select_add_fusion.2
  66.8 1.0 constant_dynamic-slice_fusion.7
  68.0 6.1 %select_add_fusion.2 = f32[800,1440]{1,0:T(8,128)} fusion(f32[800,1440]{1,0:T(8,128)} %get-tuple-element.268, bf16[800,512]{1,0:T(8,128)(2,1)S(1)} %bitcast.75, bf16[1440,512]{1,0:T(8,128)(2,1)S(1)} %convert_element_type.106, pred[]{:T(512)S(6)} %compare.26), kind=kOutput, calls=%fused_computation.6.clone.1 | convolution fusion | flops 1181952000 | bytes 11509761 | tf_op jit(solution)/shard_map/while/body/eval_jaxpr/dot_general | solution.py:89
  76.0 1.0 constant_dynamic-slice_fusion.7
  77.3 6.1 %select_add_fusion.2 = f32[800,1440]{1,0:T(8,128)} fusion(f32[800,1440]{1,0:T(8,128)} %get-tuple-element.268, bf16[800,512]{1,0:T(8,128)(2,1)S(1)} %bitcast.75, bf16[1440,512]{1,0:T(8,128)(2,1)S(1)} %convert_element_type.106, pred[]{:T(512)S(6)} %compare.26), kind=kOutput, calls=%fused_computation.6.clone.1 | convolution fusion | flops 1181952000 | bytes 11509761 | tf_op jit(solution)/shard_map/while/body/eval_jaxpr/dot_general | solution.py:89
  85.2 1.0 constant_dynamic-slice_fusion.7
  86.5 6.1 %select_add_fusion.2 = f32[800,1440]{1,0:T(8,128)} fusion(f32[800,1440]{1,0:T(8,128)} %get-tuple-element.268, bf16[800,512]{1,0:T(8,128)(2,1)S(1)} %bitcast.75, bf16[1440,512]{1,0:T(8,128)(2,1)S(1)} %convert_element_type.106, pred[]{:T(512)S(6)} %compare.26), kind=kOutput, calls=%fused_computation.6.clone.1 | convolution fusion | flops 1181952000 | bytes 11509761 | tf_op jit(solution)/shard_map/while/body/eval_jaxpr/dot_general | solution.py:89
  94.4 1.0 constant_dynamic-slice_fusion.7
  95.7 6.1 %select_add_fusion.2 = f32[800,1440]{1,0:T(8,128)} fusion(f32[800,1440]{1,0:T(8,128)} %get-tuple-element.268, bf16[800,512]{1,0:T(8,128)(2,1)S(1)} %bitcast.75, bf16[1440,512]{1,0:T(8,128)(2,1)S(1)} %convert_element_type.106, pred[]{:T(512)S(6)} %compare.26), kind=kOutput, calls=%fused_computation.6.clone.1 | convolution fusion | flops 1181952000 | bytes 11509761 | tf_op jit(solution)/shard_map/while/body/eval_jaxpr/dot_general | solution.py:89
  103.6 1.0 constant_dynamic-slice_fusion.7
  104.9 6.1 %select_add_fusion.2 = f32[800,1440]{1,0:T(8,128)} fusion(f32[800,1440]{1,0:T(8,128)} %get-tuple-element.268, bf16[800,512]{1,0:T(8,128)(2,1)S(1)} %bitcast.75, bf16[1440,512]{1,0:T(8,128)(2,1)S(1)} %convert_element_type.106, pred[]{:T(512)S(6)} %compare.26), kind=kOutput, calls=%fused_computation.6.clone.1 | convolution fusion | flops 1181952000 | bytes 11509761 | tf_op jit(solution)/shard_map/while/body/eval_jaxpr/dot_general | solution.py:89
  112.8 1.0 constant_dynamic-slice_fusion.7
  114.1 6.1 %select_add_fusion.2 = f32[800,1440]{1,0:T(8,128)} fusion(f32[800,1440]{1,0:T(8,128)} %get-tuple-element.268, bf16[800,512]{1,0:T(8,128)(2,1)S(1)} %bitcast.75, bf16[1440,512]{1,0:T(8,128)(2,1)S(1)} %convert_element_type.106, pred[]{:T(512)S(6)} %compare.26), kind=kOutput, calls=%fused_computation.6.clone.1 | convolution fusion | flops 1181952000 | bytes 11509761 | tf_op jit(solution)/shard_map/while/body/eval_jaxpr/dot_general | solution.py:89
  122.1 1.0 constant_dynamic-slice_fusion.7
  123.3 6.1 %select_add_fusion.2 = f32[800,1440]{1,0:T(8,128)} fusion(f32[800,1440]{1,0:T(8,128)} %get-tuple-element.268, bf16[800,512]{1,0:T(8,128)(2,1)S(1)} %bitcast.75, bf16[1440,512]{1,0:T(8,128)(2,1)S(1)} %convert_element_type.106, pred[]{:T(512)S(6)} %compare.26), kind=kOutput, calls=%fused_computation.6.clone.1 | convolution fusion | flops 1181952000 | bytes 11509761 | tf_op jit(solution)/shard_map/while/body/eval_jaxpr/dot_general | solution.py:89
  131.3 1.0 constant_dynamic-slice_fusion.7
  132.5 6.1 %select_add_fusion.2 = f32[800,1440]{1,0:T(8,128)} fusion(f32[800,1440]{1,0:T(8,128)} %get-tuple-element.268, bf16[800,512]{1,0:T(8,128)(2,1)S(1)} %bitcast.75, bf16[1440,512]{1,0:T(8,128)(2,1)S(1)} %convert_element_type.106, pred[]{:T(512)S(6)} %compare.26), kind=kOutput, calls=%fused_computation.6.clone.1 | convolution fusion | flops 1181952000 | bytes 11509761 | tf_op jit(solution)/shard_map/while/body/eval_jaxpr/dot_general | solution.py:89
  140.5 1.0 constant_dynamic-slice_fusion.7
  141.7 6.1 %select_add_fusion.2 = f32[800,1440]{1,0:T(8,128)} fusion(f32[800,1440]{1,0:T(8,128)} %get-tuple-element.268, bf16[800,512]{1,0:T(8,128)(2,1)S(1)} %bitcast.75, bf16[1440,512]{1,0:T(8,128)(2,1)S(1)} %convert_element_type.106, pred[]{:T(512)S(6)} %compare.26), kind=kOutput, calls=%fused_computation.6.clone.1 | convolution fusion | flops 1181952000 | bytes 11509761 | tf_op jit(solution)/shard_map/while/body/eval_jaxpr/dot_general | solution.py:89
  149.7 1.0 constant_dynamic-slice_fusion.7
  150.9 6.1 %select_add_fusion.2 = f32[800,1440]{1,0:T(8,128)} fusion(f32[800,1440]{1,0:T(8,128)} %get-tuple-element.268, bf16[800,512]{1,0:T(8,128)(2,1)S(1)} %bitcast.75, bf16[1440,512]{1,0:T(8,128)(2,1)S(1)} %convert_element_type.106, pred[]{:T(512)S(6)} %compare.26), kind=kOutput, calls=%fused_computation.6.clone.1 | convolution fusion | flops 1181952000 | bytes 11509761 | tf_op jit(solution)/shard_map/while/body/eval_jaxpr/dot_general | solution.py:89
  158.9 1.0 constant_dynamic-slice_fusion.7
  160.2 6.1 %select_add_fusion.2 = f32[800,1440]{1,0:T(8,128)} fusion(f32[800,1440]{1,0:T(8,128)} %get-tuple-element.268, bf16[800,512]{1,0:T(8,128)(2,1)S(1)} %bitcast.75, bf16[1440,512]{1,0:T(8,128)(2,1)S(1)} %convert_element_type.106, pred[]{:T(512)S(6)} %compare.26), kind=kOutput, calls=%fused_computation.6.clone.1 | convolution fusion | flops 1181952000 | bytes 11509761 | tf_op jit(solution)/shard_map/while/body/eval_jaxpr/dot_general | solution.py:89
  168.1 1.0 constant_dynamic-slice_fusion.7
  169.4 6.1 %select_add_fusion.2 = f32[800,1440]{1,0:T(8,128)} fusion(f32[800,1440]{1,0:T(8,128)} %get-tuple-element.268, bf16[800,512]{1,0:T(8,128)(2,1)S(1)} %bitcast.75, bf16[1440,512]{1,0:T(8,128)(2,1)S(1)} %convert_element_type.106, pred[]{:T(512)S(6)} %compare.26), kind=kOutput, calls=%fused_computation.6.clone.1 | convolution fusion | flops 1181952000 | bytes 11509761 | tf_op jit(solution)/shard_map/while/body/eval_jaxpr/dot_general | solution.py:89
  177.3 1.0 constant_dynamic-slice_fusion.7
  178.6 6.1 %select_add_fusion.2 = f32[800,1440]{1,0:T(8,128)} fusion(f32[800,1440]{1,0:T(8,128)} %get-tuple-element.268, bf16[800,512]{1,0:T(8,128)(2,1)S(1)} %bitcast.75, bf16[1440,512]{1,0:T(8,128)(2,1)S(1)} %convert_element_type.106, pred[]{:T(512)S(6)} %compare.26), kind=kOutput, calls=%fused_computation.6.clone.1 | convolution fusion | flops 1181952000 | bytes 11509761 | tf_op jit(solution)/shard_map/while/body/eval_jaxpr/dot_general | solution.py:89
  186.5 1.0 constant_dynamic-slice_fusion.7
  187.8 6.1 %select_add_fusion.2 = f32[800,1440]{1,0:T(8,128)} fusion(f32[800,1440]{1,0:T(8,128)} %get-tuple-element.268, bf16[800,512]{1,0:T(8,128)(2,1)S(1)} %bitcast.75, bf16[1440,512]{1,0:T(8,128)(2,1)S(1)} %convert_element_type.106, pred[]{:T(512)S(6)} %compare.26), kind=kOutput, calls=%fused_computation.6.clone.1 | convolution fusion | flops 1181952000 | bytes 11509761 | tf_op jit(solution)/shard_map/while/body/eval_jaxpr/dot_general | solution.py:89
  195.7 1.0 constant_dynamic-slice_fusion.7
  197.0 6.1 %select_add_fusion.2 = f32[800,1440]{1,0:T(8,128)} fusion(f32[800,1440]{1,0:T(8,128)} %get-tuple-element.268, bf16[800,512]{1,0:T(8,128)(2,1)S(1)} %bitcast.75, bf16[1440,512]{1,0:T(8,128)(2,1)S(1)} %convert_element_type.106, pred[]{:T(512)S(6)} %compare.26), kind=kOutput, calls=%fused_computation.6.clone.1 | convolution fusion | flops 1181952000 | bytes 11509761 | tf_op jit(solution)/shard_map/while/body/eval_jaxpr/dot_general | solution.py:89
  203.1 9.1 %reshape.209 = f32[25,32,16,90]{3,2,1,0:T(8,128)} reshape(f32[800,1440]{1,0:T(8,128)} %get-tuple-element.157) | data formatting | bytes 9216000 | tf_op jit(solution)/shard_map/reshape | solution.py:96
  212.2 8.1 %copy.39 = f32[25,32,16,90]{3,1,2,0:T(8,128)} copy(f32[25,32,16,90]{3,2,1,0:T(8,128)} %reshape.209) | data formatting | bytes 9216000 | tf_op jit(solution)/shard_map/reshape | solution.py:96
  220.3 6.6 %gather_fusion = f32[16,25,32,90]{3,2,1,0:T(8,128)} fusion(f32[25,32,16,90]{3,1,2,0:T(8,128)} %copy.39, s32[1024]{0:T(1024)S(1)} %pad_clamp_fusion.1), kind=kCustom, calls=%fused_computation.clone | custom fusion | bytes 9216064 | tf_op jit(solution)/shard_map/jit(_take)/gather | solution.py:105
  226.8 6.6 %select_bitcast_fusion.1 = f32[25,32,16,90]{3,1,0,2:T(8,128)} fusion(f32[16,25,32,90]{3,2,1,0:T(8,128)} %gather_fusion, pred[16]{0:T(512)(128)(4,1)S(1)} %compare_and_fusion.1), kind=kLoop, calls=%fused_computation.21 | loop fusion | flops 1152000 | bytes 9216016 | tf_op jit(solution)/shard_map/jit(_take)/select_n | solution.py:105
  233.4 7.6 %all-to-all-start.1 = ((f32[25,32,16,90]{3,1,0,2:T(8,128)}), f32[25,32,16,90]{3,1,0,2:T(8,128)}, u32[]{:S(2)}, u32[]{:S(2)}) async-start(f32[25,32,16,90]{3,1,0,2:T(8,128)} %select_bitcast_fusion.1), calls=%async_computation.1 | async-start | bytes 13107200 | tf_op jit(solution)/shard_map/all_to_all | solution.py:112
  241.4 92.5 %all-to-all-done.1 = f32[25,32,16,90]{3,1,0,2:T(8,128)} async-done(((f32[25,32,16,90]{3,1,0,2:T(8,128)}), f32[25,32,16,90]{3,1,0,2:T(8,128)}, u32[]{:S(2)}, u32[]{:S(2)}) %all-to-all-start.1) | async-done | bytes 4608032 | tf_op jit(solution)/shard_map/all_to_all | solution.py:112
  333.9 6.7 %copy.40 = f32[25,32,16,90]{3,1,2,0:T(8,128)} copy(f32[25,32,16,90]{3,1,0,2:T(8,128)} %all-to-all-done.1) | data formatting | bytes 9216000 | tf_op jit(solution)/shard_map/all_to_all | solution.py:112
  340.6 6.5 %gather_fusion.1 = f32[16,25,32,90]{3,2,1,0:T(8,128)} fusion(f32[25,32,16,90]{3,1,2,0:T(8,128)} %copy.40, s32[1024]{0:T(1024)S(1)} %pad_clamp_fusion), kind=kCustom, calls=%fused_computation.1.clone | custom fusion | bytes 9216064 | tf_op jit(solution)/shard_map/jit(_take)/gather | solution.py:113
  347.1 3.7 select_bitcast_fusion
  350.8 8.5 %copy.41 = f32[25,32,16,90]{3,2,1,0:T(8,128)} copy(f32[25,32,16,90]{3,1,0,2:T(8,128)S(1)} %select_bitcast_fusion) | data formatting | bytes 9216000 | tf_op jit(solution)/shard_map/jit(_take)/select_n | solution.py:113
  359.3 7.9 %reshape.211 = f32[25,32,1440]{2,1,0:T(8,128)} reshape(f32[25,32,16,90]{3,2,1,0:T(8,128)} %copy.41) | data formatting | bytes 9216000 | tf_op jit(solution)/shard_map/reshape | solution.py:113
  369.1 74.9 %all-reduce.4.cloned.1.call-done = f32[25,32,1440]{2,1,0:T(8,128)} async-done(((f32[25,32,1440]{2,1,0:T(8,128)}), f32[25,32,1440]{2,1,0:T(8,128)}) %all-reduce.4.cloned.1.call-update) | async-done | bytes 4608016
  444.0 0.8 maximum_bitcast_fusion.1
  444.8 1.4 fusion.20
  446.6 1.9 collective-permute-start
  448.7 8.1 %collective-permute-start.1 = (bf16[25,1,1440]{2,1,0:T(2,128)(2,1)S(1)}, bf16[25,1,1440]{2,1,0:T(2,128)(2,1)S(1)}, u32[]{:S(2)}, u32[]{:S(2)}) collective-permute-start(bf16[25,1,1440]{2,1,0:T(2,128)(2,1)S(1)} %pad_maximum_fusion.1), channel_id=1, source_target_pairs={{1,0},{2,1},{3,2},{4,3},{5,4},{6,5},{7,6},{8,7},{9,8},{10,9},{11,1... | collective-permute-start | bytes 216008 | tf_op jit(solution)/shard_map/ppermute | solution.py:13
  456.8 2.5 collective-permute-done.1
  459.9 0.9 concatenate.23
  460.9 1.2 reshape.214
  462.1 3.3 copy.43
  465.4 0.8 slice.115
  466.3 4.0 fusion.16
  470.9 1.0 fusion.15
  (240 shorter events, 41.7 us)
Async XLA Ops:
  6.5 459.7 %copy-start = (bf16[5,5,25,256]{3,2,1,0:T(8,128)(2,1)S(1)}, bf16[5,5,25,256]{3,2,1,0:T(8,128)(2,1)}, u32[]{:S(2)}) copy-start(bf16[5,5,25,256]{3,2,1,0:T(8,128)(2,1)} %param.22) | copy-start | bytes 960004
  30.9 11.1 %copy-start.1 = (f32[2]{0:T(128)S(1)}, f32[2]{0:T(128)}, u32[]{:S(2)}) copy-start(f32[2]{0:T(128)} %param.21) | copy-start | bytes 28
  30.9 14.3 %copy-start.3 = (s32[256]{0:T(256)S(1)}, s32[256]{0:T(256)}, u32[]{:S(2)}) copy-start(s32[256]{0:T(256)} %param.20) | copy-start | bytes 3076
  34.6 22.0 %all-to-all-start = ((f32[27,16,512]{2,0,1:T(8,128)}), f32[27,16,512]{2,0,1:T(8,128)S(1)}, u32[]{:S(2)}, u32[]{:S(2)}) async-start(f32[27,16,512]{2,0,1:T(8,128)} %copy.37), calls=%async_computation | async-start | bytes 2097152 | tf_op jit(solution)/shard_map/all_to_all | solution.py:53
  233.4 100.4 %all-to-all-start.1 = ((f32[25,32,16,90]{3,1,0,2:T(8,128)}), f32[25,32,16,90]{3,1,0,2:T(8,128)}, u32[]{:S(2)}, u32[]{:S(2)}) async-start(f32[25,32,16,90]{3,1,0,2:T(8,128)} %select_bitcast_fusion.1), calls=%async_computation.1 | async-start | bytes 13107200 | tf_op jit(solution)/shard_map/all_to_all | solution.py:112
  241.0 203.0 %all-reduce.4.cloned.1.call-start = ((), (), s32[]{:S(2)}) async-start(), calls=%async_computation.2 | async-start | bytes 9830400
  367.2 0.7 copy-start.5
  446.6 12.7 %collective-permute-start = (bf16[25,2,1440]{2,1,0:T(2,128)(2,1)S(1)}, bf16[25,2,1440]{2,1,0:T(2,128)(2,1)S(1)}, u32[]{:S(2)}, u32[]{:S(2)}) collective-permute-start(bf16[25,2,1440]{2,1,0:T(2,128)(2,1)S(1)} %fusion.21), channel_id=1, source_target_pairs={{0,1},{1,2},{2,3},{3,4},{4,5},{5,6},{6,7},{7,8},{8,9},{9,10},{10,1... | collective-permute-start | bytes 432008 | tf_op jit(solution)/shard_map/ppermute | solution.py:13
  448.7 17.6 %copy-start.4 = (pred[8,91]{0,1:T(8,128)(4,1)S(1)}, pred[8,91]{0,1:T(8,128)(4,1)}, u32[]{:S(2)}) copy-start(pred[8,91]{0,1:T(8,128)(4,1)} %constant.158) | copy-start | bytes 2188
  448.7 10.6 %collective-permute-start.1 = (bf16[25,1,1440]{2,1,0:T(2,128)(2,1)S(1)}, bf16[25,1,1440]{2,1,0:T(2,128)(2,1)S(1)}, u32[]{:S(2)}, u32[]{:S(2)}) collective-permute-start(bf16[25,1,1440]{2,1,0:T(2,128)(2,1)S(1)} %pad_maximum_fusion.1), channel_id=1, source_target_pairs={{1,0},{2,1},{3,2},{4,3},{5,4},{6,5},{7,6},{8,7},{9,8},{10,9},{11,1... | collective-permute-start | bytes 216008 | tf_op jit(solution)/shard_map/ppermute | solution.py:13
  470.2 0.7 copy-start.2
Sparse Core Ops, SparseCore 0:
  367.4 76.6 all-reduce.3
where the time goes:
time: 483 us; the launch traced here: 479 us
  waiting for transfers between devices  181 us (37%)
  local copies, waits for them, and re-layouts  119 us (25%)
  matrix products  98.7 us (20%)
  other arithmetic  36.6 us (8%)
  starting transfers between devices  25.2 us (5%)
  between operations  16.8 us (3%)
    dot_general x16, matrix products, accumulate(): lax.dot_general(left_factor, right_factor, (((1,), (1,)), ((), ())), pref...  94.7 us
    all_to_all x1, waiting for transfers between devices, body(): lax.all_to_all(outgoing, 'band', split_axis=2, concat_axis=2, tiled=True)  92.5 us
    unnamed x2, waiting for transfers between devices  74.9 us
    reshape x2, local copies, waits for them, and re-layouts, body(): grid_sums = grid_sums.reshape(channels + 1, lat_dev, band_count, tile_width)  17.2 us
    slice x16, local copies, waits for them, and re-layouts, accumulate(): source_block[:channels]  16.7 us
    slice x16, local copies, waits for them, and re-layouts, accumulate(): slot_at = source_block[channels + 2]  12.1 us
    all_to_all x1, waiting for transfers between devices, body(): lax.all_to_all(outbox.reshape(channels + 3, band_count, capacity), 'band'...  10.9 us
    ppermute x2, starting transfers between devices, from_behind(): lax.ppermute(value, axis, [(source, source + steps) for source in range(f...  10 us
  transfers between devices with their start and end apart: 5, of which 4 were waited for; matrix products, arithmetic and copies ran while one was open for 0% of the time, Pallas kernels for 0%

commit v1 on v0

--- a/solution.py
+++ b/solution.py
@@ -1,10 +1,389 @@
+import functools
+
 import jax
 import jax.numpy as jnp
 from jax import lax
+from jax.experimental import pallas as pl
+from jax.experimental.pallas import tpu as pltpu
 from jax.sharding import PartitionSpec as P
 
 LON = 1440
 ROWS_DEV = 4
+BANDS = 16
+TQ = 90
+HALF = TQ // 2
+HALF_PAD = 48
+BOX = 256
+EXTRA = 8
+ROW_CODE = 24
+ROW_LAT = 25
+ROW_LON = 28
+ROW_NOTE = 31
+PAY = 32
+F32 = jnp.float32
+BF16 = jnp.bfloat16
+
+
+def dot_nt(left, right):
+    return lax.dot_general(left, right, (((1,), (1,)), ((), ())), preferred_element_type=F32)
+
+
+def iota(shape, dim):
+    return lax.broadcasted_iota(jnp.int32, shape, dim)
+
+
+def ones_where(mask):
+    return jnp.where(mask, 1.0, 0.0)
+
+
+def ranks(member):
+    chunks = len(member)
+    rows = chunks * BANDS
+    stacked = jnp.concatenate(member, axis=0).astype(BF16)
+    before = ones_where(iota((BOX, BOX), 0) < iota((BOX, BOX), 1)).astype(BF16)
+    at, of = iota((rows, rows), 0), iota((rows, rows), 1)
+    earlier = ones_where(((of & 15) == (at & 15)) & ((of >> 4) < (at >> 4))).astype(BF16)
+    inside = jnp.dot(stacked, before, preferred_element_type=F32)
+    base = jnp.sum(jnp.dot(earlier, stacked, preferred_element_type=F32), axis=1, keepdims=True)
+    place = inside + base
+    return [
+        jnp.sum(member[k] * place[k * BANDS : (k + 1) * BANDS], axis=0, keepdims=True)
+        for k in range(chunks)
+    ]
+
+
+def bucket(payload, group, position, left_ref, right_ref, k):
+    lanes = slice(k * BOX, (k + 1) * BOX)
+    for g in range(left_ref.shape[0] // PAY):
+        left_ref[g * PAY : (g + 1) * PAY, lanes] = jnp.where(group == g, payload, 0.0).astype(BF16)
+    right_ref[:, lanes] = ones_where(iota((right_ref.shape[0], BOX), 0) == position).astype(BF16)
+
+
+def split3(value):
+    high = value.astype(BF16).astype(F32)
+    rest = value - high
+    middle = rest.astype(BF16).astype(F32)
+    return high, middle, rest - middle
+
+
+def pack_kernel(values_ref, tile_ref, row_ref, col_ref, frac_ref, place_ref, out_ref, left_ref, right_ref):
+    chunks = tile_ref.shape[0] * 128 // BOX
+
+    def wide(ref, k):
+        return jnp.concatenate([ref[2 * k : 2 * k + 1, :], ref[2 * k + 1 : 2 * k + 2, :]], axis=1)
+
+    table = jnp.broadcast_to(wide(place_ref, 0).astype(F32), (8, BOX)).astype(BF16)
+    ones = jnp.ones((8, BOX), BF16)
+    lines = iota((BOX, BOX), 0)
+    eight = iota((8, BOX), 0)
+    counts = jnp.zeros((8, BOX), F32)
+    bands, blocks, member = [], [], []
+    for k in range(chunks):
+        tile_pick = ones_where(lines == wide(tile_ref, k)).astype(BF16)
+        place = jnp.dot(table, tile_pick, preferred_element_type=F32)[0:1].astype(jnp.int32)
+        counts = counts + dot_nt(ones, ones_where(lines == place).astype(BF16))
+        bands.append(place >> 4)
+        blocks.append(place & 15)
+        member.append(ones_where(iota((BANDS, BOX), 0) == bands[k]))
+    rank = ranks(member)
+    for k in range(chunks):
+        lanes = slice(k * BOX, (k + 1) * BOX)
+        lat = split3(wide(row_ref, k).astype(F32) + frac_ref[0:1, lanes])
+        lon = split3(wide(col_ref, k).astype(F32) + frac_ref[1:2, lanes])
+        tail = jnp.zeros((8, BOX), F32)
+        for at, line in enumerate([blocks[k].astype(F32) + 1.0, *lat, *lon]):
+            tail = jnp.where(eight == at, line, tail)
+        payload = jnp.concatenate([values_ref[:, lanes].astype(F32), tail], axis=0)
+        bucket(payload, bands[k], rank[k].astype(jnp.int32), left_ref, right_ref, k)
+    packed = dot_nt(left_ref[...], right_ref[...])
+    line_of = iota((PAY, BOX), 0)
+    for g in range(BANDS):
+        rows = slice(g * PAY, (g + 1) * PAY)
+        out_ref[rows, :] = jnp.where(line_of == ROW_NOTE, counts[0:1], packed[rows]).astype(BF16)
+
+
+def regroup_kernel(in_ref, out_ref, left_ref, right_ref):
+    chunks = in_ref.shape[0] // PAY
+    codes, member, notes = [], [], []
+    line_of = iota((PAY, BOX), 0)
+    total = jnp.zeros((BANDS, 1), F32)
+    for k in range(chunks):
+        tail = in_ref[k * PAY + 16 : (k + 1) * PAY, :].astype(F32)
+        codes.append(tail[ROW_CODE - 16 : ROW_CODE - 15].astype(jnp.int32) - 1)
+        notes.append(tail[ROW_NOTE - 16 : ROW_NOTE - 15])
+        member.append(ones_where(iota((BANDS, BOX), 0) == codes[k]))
+        total = total + jnp.sum(member[k], axis=1, keepdims=True)
+    rank = ranks(member)
+
+    more = jnp.maximum(jnp.broadcast_to(total, (BANDS, 128)).astype(jnp.int32) - 1, 0) >> 7
+    lower = ones_where(iota((BANDS, BANDS), 1) < iota((BANDS, BANDS), 0)).astype(BF16)
+    first = jnp.dot(lower, more.astype(F32).astype(BF16), preferred_element_type=F32)
+    last = first + more.astype(F32)
+    first_wide = jnp.concatenate([first, first], axis=1)
+
+    for k in range(chunks):
+        payload = in_ref[k * PAY : (k + 1) * PAY, :].astype(F32)
+        payload = jnp.where(line_of == ROW_CODE, 1.0, jnp.where(line_of == ROW_NOTE, 0.0, payload))
+        place = rank[k].astype(jnp.int32)
+        over = jnp.sum(member[k] * first_wide, axis=0, keepdims=True).astype(jnp.int32)
+        group = jnp.where(place < 128, codes[k], BANDS - 1 + over + (place >> 7))
+        group = jnp.where(codes[k] < 0, -1, group)
+        bucket(payload, group, place & 127, left_ref, right_ref, k)
+    moved = dot_nt(left_ref[...], right_ref[...])
+
+    note = jnp.concatenate(notes, axis=0)
+    of_band = ones_where((iota((BOX, 128), 0) >> 4) == iota((BOX, 128), 1)).astype(BF16)
+    band_sums = jnp.dot(note.astype(BF16), of_band, preferred_element_type=F32)
+    tile_sums = jnp.broadcast_to(jnp.sum(note, axis=0, keepdims=True), (8, BOX)).astype(jnp.int32)
+    tile_more = (jnp.maximum(tile_sums - 1, 0) >> 7).astype(F32).astype(BF16)
+    more_sums = jnp.dot(tile_more, of_band, preferred_element_type=F32)
+    band_most = jnp.max(jnp.max(band_sums, axis=1, keepdims=True), axis=0, keepdims=True)
+    more_most = jnp.max(jnp.max(more_sums, axis=1, keepdims=True), axis=0, keepdims=True)
+    over = jnp.where((band_most > BOX - 1) | (more_most > EXTRA), 1.0, 0.0)
+
+    narrow = iota((PAY, 128), 0)
+    out_ref[0:PAY, :] = jnp.where(narrow == ROW_NOTE, over, moved[0:PAY]).astype(BF16)
+    out_ref[PAY : BANDS * PAY, :] = moved[PAY : BANDS * PAY].astype(BF16)
+    block_code = iota((BANDS, 128), 0).astype(F32) + 1.0
+    for e in range(EXTRA):
+        rows = slice((BANDS + e) * PAY, (BANDS + e + 1) * PAY)
+        code = jnp.where((first <= e) & (last > e), block_code, 0.0)
+        code = jnp.sum(code, axis=0, keepdims=True)
+        out_ref[rows, :] = jnp.where(narrow == ROW_NOTE, code, moved[rows]).astype(BF16)
+
+
+def sums_kernel(scale_ref, *refs):
+    (
+        *block_refs,
+        feature_ref,
+        lower_ref,
+        upper_ref,
+        over_ref,
+        left_ref,
+        right_ref,
+        sums_ref,
+        wide_ref,
+        codes_ref,
+        codes_smem,
+        sem,
+    ) = refs
+    first_row = (lax.axis_index("obs") * ROWS_DEV).astype(F32)
+    scale = jnp.full((8, 128), 1.0, F32)
+    inv_lat = 0.5 / (scale * scale_ref[0] * scale_ref[0])
+    inv_lon = 0.5 / (scale * scale_ref[1] * scale_ref[1])
+    inv_lat, inv_lon = inv_lat[0:1], inv_lon[0:1]
+    row_mid = iota((8, 128), 0).astype(F32) + 0.5 + first_row
+    line = iota((2 * HALF_PAD, 128), 0)
+    past = (line >= HALF_PAD).astype(jnp.int32)
+    col_mid = (2 * (line - HALF_PAD * past) + past).astype(F32) + 0.5
+    keep = iota((PAY, 128), 0) <= ROW_CODE
+    blocks = len(block_refs)
+    tall = 2 * HALF_PAD
+
+    lane = iota((8, 128), 1)
+    sub = iota((8, 128), 0)
+    codes = jnp.zeros((8, 128), F32)
+    for k in range(blocks):
+        for e in range(EXTRA):
+            at = (BANDS + e) * PAY + 16
+            note = block_refs[k][at : at + 16, :].astype(F32)[15:16]
+            codes = jnp.where((lane == e) & (sub == k), note, codes)
+    codes_ref[...] = codes.astype(jnp.int32)
+    copy = pltpu.make_async_copy(codes_ref, codes_smem, sem)
+    copy.start()
+
+    def factors(start):
+        for k in range(blocks):
+            lanes = slice(k * 128, (k + 1) * 128)
+            block = block_refs[k][pl.ds(start, PAY), :].astype(F32)
+            lat_at = block[ROW_LAT : ROW_LAT + 1] + block[ROW_LAT + 1 : ROW_LAT + 2]
+            lat_at = lat_at + block[ROW_LAT + 2 : ROW_LAT + 3]
+            lon_at = block[ROW_LON : ROW_LON + 1] + block[ROW_LON + 1 : ROW_LON + 2]
+            lon_at = lon_at + block[ROW_LON + 2 : ROW_LON + 3]
+            lat_diff = row_mid - lat_at
+            lat_weight = jnp.exp(-(lat_diff * lat_diff) * inv_lat)
+            lon_diff = col_mid - lon_at
+            lon_weight = jnp.exp(-(lon_diff * lon_diff) * inv_lon)
+            value = jnp.where(keep, block, 0.0)
+            present = block[ROW_CODE : ROW_CODE + 1]
+            for r in range(ROWS_DEV):
+                weight = lat_weight[r : r + 1]
+                left_ref[r * PAY : (r + 1) * PAY, lanes] = (value * weight).astype(BF16)
+                left_ref[(ROWS_DEV + r) * PAY : (ROWS_DEV + r + 1) * PAY, lanes] = jnp.broadcast_to(
+                    present * weight, (PAY, 128)
+                ).astype(BF16)
+            right_ref[:, lanes] = lon_weight.astype(BF16)
+
+    def main(p, carry):
+        factors(pl.multiple_of(p * PAY, PAY))
+        start = pl.multiple_of((p + 1) * tall, tall)
+        sums_ref[pl.ds(start, tall), :] = dot_nt(right_ref[...], left_ref[...])
+        return carry
+
+    sums_ref[0:tall, :] = jnp.zeros((tall, 256), F32)
+    lax.fori_loop(0, BANDS, main, 0)
+    copy.wait()
+    used = jnp.int32(0)
+    for e in range(EXTRA):
+        for k in range(blocks):
+            used = jnp.where(codes_smem[k, e] > 0, e + 1, used)
+
+    def extra(e, carry):
+        factors(pl.multiple_of((BANDS + e) * PAY, PAY))
+        for k in range(blocks):
+            lanes = slice(k * 128, (k + 1) * 128)
+            start = pl.multiple_of(codes_smem[k, e] * tall, tall)
+            sums_ref[pl.ds(start, tall), :] += dot_nt(right_ref[:, lanes], left_ref[:, lanes])
+        return carry
+
+    lax.fori_loop(0, used, extra, 0)
+
+    channel = iota((HALF_PAD, 128), 1) & (PAY - 1)
+    for block in range(BANDS):
+        for odd in range(2):
+            start = (2 * (block + 1) + odd) * HALF_PAD
+            total = sums_ref[start : start + HALF_PAD, 0:128]
+            density = sums_ref[start : start + HALF_PAD, 128:256]
+            feature = jnp.where(
+                channel < 24,
+                total / jnp.maximum(density, 1.0),
+                jnp.where(channel == 24, jnp.log(1.0 + density), 0.0),
+            )
+            wide_ref[block * HALF : (block + 1) * HALF, odd * 128 : (odd + 1) * 128] = feature[:HALF]
+    feature_ref[...] = wide_ref[...].astype(BF16)
+    lower_ref[...] = jnp.concatenate([wide_ref[:, 64:128], wide_ref[:, 192:256]], axis=1).astype(BF16)
+    top = jnp.concatenate([wide_ref[0:368, 0:32], wide_ref[0:368, 128:160]], axis=1)
+    rest = jnp.concatenate([wide_ref[368:720, 0:32], wide_ref[368:720, 128:160]], axis=1)
+    rest = jnp.concatenate([rest, jnp.zeros((16, 64), F32)], axis=0)
+    upper_ref[...] = jnp.concatenate([top, rest], axis=1).astype(BF16)
+    over = block_refs[0][0:PAY, :].astype(F32)[ROW_NOTE:PAY]
+    for k in range(1, blocks):
+        over = jnp.maximum(over, block_refs[k][0:PAY, :].astype(F32)[ROW_NOTE:PAY])
+    over_ref[...] = jnp.broadcast_to(over, (8, 128))
+
+
+def conv_kernel(feature_ref, lower_ref, upper_ref, weight_ref, bias_ref, out_ref, wide_ref, w_ref):
+    columns = feature_ref.shape[0]
+    w_ref[...] = jnp.zeros(w_ref.shape, BF16)
+    channels = weight_ref.shape[2]
+    zero = jnp.zeros((PAY - channels, 256), BF16)
+
+    def put(shift, at, out_row, tap, odd):
+        e = 2 * (shift + 1) + odd
+        if e < 5:
+            part = jnp.concatenate([weight_ref[tap, e].astype(F32), zero.astype(F32)], axis=0)
+            w_ref[shift + 1, at : at + PAY, out_row * 256 : (out_row + 1) * 256] = part.astype(BF16)
+
+    for shift in (-1, 0, 1):
+        for odd in range(2):
+            for row in range(ROWS_DEV):
+                for out_row in range(2):
+                    tap = row - 2 * out_row + 2
+                    if 0 <= tap < 5:
+                        put(shift, odd * 128 + row * PAY, out_row, tap, odd)
+            for row in range(2):
+                put(shift, 256 + odd * 64 + row * PAY, 0, row, odd)
+            put(shift, 384 + odd * 32, 1, 4, odd)
+
+    edge = 8
+    wide_ref[edge : edge + columns, 0:256] = feature_ref[...].astype(F32)
+    wide_ref[edge : edge + columns, 256:384] = lower_ref[...].astype(F32)
+    upper = upper_ref[...].astype(F32)
+    wide_ref[edge : edge + 368, 384:448] = upper[:, 0:64]
+    wide_ref[edge + 368 : edge + columns, 384:448] = upper[: columns - 368, 64:128]
+    wide_ref[edge : edge + columns, 448:512] = jnp.zeros((columns, 64), F32)
+    wide_ref[edge - 1 : edge, :] = wide_ref[edge + columns - 1 : edge + columns, :]
+    wide_ref[edge + columns : edge + columns + 1, :] = wide_ref[edge : edge + 1, :]
+
+    total = None
+    for shift in (-1, 0, 1):
+        moved = wide_ref[edge + shift : edge + shift + columns, :].astype(BF16)
+        part = jnp.dot(moved, w_ref[shift + 1], preferred_element_type=F32)
+        total = part if total is None else total + part
+    bias = bias_ref[...]
+    out_ref[0] = (total[:, 0:256] + bias).astype(BF16)
+    out_ref[1] = (total[:, 256:512] + bias).astype(BF16)
+
+
+def params(mib):
+    return pltpu.CompilerParams(vmem_limit_bytes=mib * 2**20)
+
+
+def vmem():
+    return pl.BlockSpec(memory_space=pltpu.VMEM)
+
+
+def fast_features(values, tile, row, col, frac, place, scale):
+    arrivals = tile.shape[0]
+    sent = pl.pallas_call(
+        pack_kernel,
+        out_shape=jax.ShapeDtypeStruct((BANDS * PAY, BOX), BF16),
+        in_specs=[vmem()] * 6,
+        out_specs=vmem(),
+        scratch_shapes=[
+            pltpu.VMEM((BANDS * PAY, arrivals), BF16),
+            pltpu.VMEM((BOX, arrivals), BF16),
+        ],
+        compiler_params=params(32),
+        name="pack",
+    )(
+        values,
+        tile.reshape(-1, 128),
+        row.reshape(-1, 128),
+        col.reshape(-1, 128),
+        frac,
+        place.reshape(2, 128),
+    )
+    came = lax.all_to_all(sent, "band", split_axis=0, concat_axis=0, tiled=True)
+    groups = BANDS + EXTRA
+    own = pl.pallas_call(
+        regroup_kernel,
+        out_shape=jax.ShapeDtypeStruct((groups * PAY, 128), BF16),
+        in_specs=[vmem()],
+        out_specs=vmem(),
+        scratch_shapes=[
+            pltpu.VMEM((groups * PAY, BANDS * BOX), BF16),
+            pltpu.VMEM((128, BANDS * BOX), BF16),
+        ],
+        compiler_params=params(32),
+        name="regroup",
+    )(came)
+    count = lax.axis_size("obs")
+    chips = count // 2
+
+    def along(value, steps):
+        order = [(s, ((s // 2 + steps) % chips) * 2 + s % 2) for s in range(count)]
+        return lax.ppermute(value, "obs", order)
+
+    def across(value):
+        return lax.ppermute(value, "obs", [(s, s ^ 1) for s in range(count)])
+
+    mine = [own] + [along(own, steps) for steps in range(1, chips)]
+    blocks = mine + [across(value) for value in mine]
+    columns = LON // 2
+    shape = jax.ShapeDtypeStruct
+    return pl.pallas_call(
+        sums_kernel,
+        out_shape=(
+            shape((columns, 256), BF16),
+            shape((columns, 128), BF16),
+            shape((368, 128), BF16),
+            shape((8, 128), F32),
+        ),
+        in_specs=[pl.BlockSpec(memory_space=pltpu.SMEM)] + [vmem()] * len(blocks),
+        out_specs=(vmem(),) * 4,
+        scratch_shapes=[
+            pltpu.VMEM((256, len(blocks) * 128), BF16),
+            pltpu.VMEM((2 * HALF_PAD, len(blocks) * 128), BF16),
+            pltpu.VMEM((2 * HALF_PAD * (BANDS + 1), 256), F32),
+            pltpu.VMEM((columns, 256), F32),
+            pltpu.VMEM((8, 128), jnp.int32),
+            pltpu.SMEM((8, 128), jnp.int32),
+            pltpu.SemaphoreType.DMA,
+        ],
+        compiler_params=params(32),
+        name="sums",
+    )(scale, *blocks)
 
 
 def from_behind(value, axis, steps):
@@ -13,7 +392,7 @@
     return lax.ppermute(value, axis, [(source, source + steps) for source in range(first, last)])
 
 
-def body(
+def general(
     obs_values,
     obs_tile,
     obs_row,
@@ -132,6 +511,34 @@
     return (conv_out + conv_bias).astype(jnp.bfloat16)
 
 
+def body(*args):
+    *_, conv_weight, conv_bias = args
+    feature, lower, upper, over = fast_features(*args[:7])
+    lower = from_behind(lower, ("band", "obs"), 1)
+    upper = from_behind(upper, ("band", "obs"), -1)
+
+    def finish(feature, lower, upper, *args):
+        *_, conv_weight, conv_bias = args
+        columns = LON // 2
+        return pl.pallas_call(
+            conv_kernel,
+            out_shape=jax.ShapeDtypeStruct((2, columns, 256), BF16),
+            in_specs=[vmem()] * 5,
+            out_specs=vmem(),
+            scratch_shapes=[
+                pltpu.VMEM((columns + 16, 512), F32),
+                pltpu.VMEM((3, 512, 512), BF16),
+            ],
+            compiler_params=params(32),
+            name="conv",
+        )(feature, lower, upper, conv_weight, conv_bias.reshape(1, -1))
+
+    def whole(feature, lower, upper, *args):
+        return general(*args)
+
+    return lax.cond(over[0, 0] > 0.0, whole, finish, feature, lower, upper, *args)
+
+
 def solution(mesh):
     placed = (
         P(None, ("band", "obs")),

time: 483 us -> 72.9 us (0.15)
  waiting for transfers between devices: 181 us -> 8.27 us
  local copies, waits for them, and re-layouts: 119 us -> 1.37 us
  matrix products: 98.7 us -> 0 us
  other arithmetic: 36.6 us -> 0 us
  Pallas kernels: 0 us -> 17.2 us
  blocking collectives: 0 us -> 14.2 us
  starting transfers between devices: 25.2 us -> 16.9 us
    all_to_all x2 -> x0, waiting for transfers between devices: 103 us -> none  [the longest x1 92.5 us: body(): lax.all_to_all(outgoing, 'band', split_axis=2, concat_axis=2, tiled=True)]
    dot_general x16 -> x0, matrix products: 94.7 us -> none  [accumulate(): lax.dot_general(left_factor, right_factor, (((1,), (1,)), ((), ())), pref...]
    unnamed x2 -> x0, waiting for transfers between devices: 74.9 us -> none
    slice x35 -> x1, local copies, waits for them, and re-layouts: 30.3 us -> 0.51 us  [body(): over[0, 0] > 0.0]
    reshape x5 -> x0, local copies, waits for them, and re-layouts: 28.9 us -> none  [the longest x2 17.2 us: body(): grid_sums = grid_sums.reshape(channels + 1, lat_dev, band_count, tile_width)]
    pallas_call x0 -> x4, Pallas kernels: none -> 17.2 us  [the longest x1 10.2 us: fast_features(): pl.pallas_call(sums_kernel, out_shape=(shape((columns, 256), BF16), shape...]
    all_to_all x2 -> x0, starting transfers between devices: 15 us -> none  [the longest x1 7.59 us: body(): lax.all_to_all(outgoing, 'band', split_axis=2, concat_axis=2, tiled=True)]
    all_to_all x0 -> x1, blocking collectives: none -> 14.2 us  [fast_features(): came = lax.all_to_all(sent, 'band', split_axis=0, concat_axis=0, tiled=True)]
  transfers between devices with their start and end apart: 5 -> 9, of which waited for: 4 -> 5; matrix products, arithmetic and copies ran while one was open for 0% -> 1% of each run, Pallas kernels for 0% -> 0%
where the time goes in v1:
time: 72.9 us; the launch traced here: 72.2 us
  Pallas kernels  17.2 us (24%)
  starting transfers between devices  16.9 us (23%)
  blocking collectives  14.2 us (19%)
  between operations  14.1 us (19%)
  waiting for transfers between devices  8.27 us (11%)
  local copies, waits for them, and re-layouts  1.37 us (2%)
    all_to_all x1, blocking collectives, fast_features(): came = lax.all_to_all(sent, 'band', split_axis=0, concat_axis=0, tiled=True)  14.2 us
    pallas_call x1, Pallas kernels, fast_features(): pl.pallas_call(sums_kernel, out_shape=(shape((columns, 256), BF16), shape...  10.2 us
    ppermute x2, starting transfers between devices, from_behind(): lax.ppermute(value, axis, [(source, source + steps) for source in range(f...  9.78 us
    ppermute x3, starting transfers between devices, along(): return lax.ppermute(value, 'obs', order)  6.58 us
    ppermute x3, waiting for transfers between devices, along(): return lax.ppermute(value, 'obs', order)  6.07 us
    pallas_call x1, Pallas kernels, fast_features(): pl.pallas_call(pack_kernel, out_shape=jax.ShapeDtypeStruct((BANDS * PAY,...  2.39 us
    pallas_call x1, Pallas kernels, finish(): pl.pallas_call(conv_kernel, out_shape=jax.ShapeDtypeStruct((2, columns, 2...  2.39 us
    pallas_call x1, Pallas kernels, fast_features(): pl.pallas_call(regroup_kernel, out_shape=jax.ShapeDtypeStruct((groups * P...  2.22 us
  transfers between devices with their start and end apart: 9, of which 5 were waited for; matrix products, arithmetic and copies ran while one was open for 1% of the time, Pallas kernels for 0%

profile of v1, /device:TPU:8, one launch (start us, length us, event | category | flops | bytes accessed | tf_op | source)
XLA Modules:
  0.0 72.2 jit_solution(11700733720088298512)
XLA Ops:
  6.5 2.4 %pack.1 = bf16[512,256]{1,0:T(8,128)(2,1)S(1)} custom-call(bf16[24,2048]{1,0:T(8,128)(2,1)} %values_ref.1, s32[16,128]{1,0:T(8,128)} %bitcast.93, s32[16,128]{1,0:T(8,128)} %bitcast.98, s32[16,128]{1,0:T(8,128)} %bitcast.99, f32[2,2048]{1,0:T(2,128)} %frac_ref.1, s32[2,128]{1,0:T(2,128)} %bitcast.103), custom_call_target="tpu_custom_call" | custom-call | tf_op jit(solution)/shard_map/pack/pallas_call | solution.py:318
  8.9 14.2 %all_to_all.19 = bf16[16,32,256]{2,1,0:T(8,128)(2,1)S(1)} all-to-all(bf16[16,32,256]{2,1,0:T(8,128)(2,1)S(1)} %bitcast.84), channel_id=1, replica_groups=mesh['band'=16,'obs'=8] {'band'}, dimensions={0} | all-to-all | bytes 524288 | tf_op jit(solution)/shard_map/all_to_all | solution.py:337
  23.1 2.2 %regroup.1.refs_0_ = bf16[768,128]{1,0:T(8,128)(2,1)S(1)} custom-call(bf16[512,256]{1,0:T(8,128)(2,1)S(1)} %bitcast.83), custom_call_target="tpu_custom_call" | custom-call | tf_op jit(solution)/shard_map/regroup/pallas_call | solution.py:339
  25.3 2.0 %collective-permute-start.2 = (bf16[768,128]{1,0:T(8,128)(2,1)S(1)}, bf16[768,128]{1,0:T(8,128)(2,1)S(1)}, u32[]{:S(2)}, u32[]{:S(2)}) collective-permute-start(bf16[768,128]{1,0:T(8,128)(2,1)S(1)} %regroup.1.refs_0_), channel_id=1, source_target_pairs={{0,2},{1,3},{2,4},{3,5},{4,6},{5,7},{6,0},{7,1},{8,10},{9,11},{10,... | collective-permute-start | bytes 589832 | tf_op jit(solution)/shard_map/ppermute | solution.py:356
  27.3 3.6 %collective-permute-start.3 = (bf16[768,128]{1,0:T(8,128)(2,1)S(1)}, bf16[768,128]{1,0:T(8,128)(2,1)S(1)}, u32[]{:S(2)}, u32[]{:S(2)}) collective-permute-start(bf16[768,128]{1,0:T(8,128)(2,1)S(1)} %regroup.1.refs_0_), channel_id=1, source_target_pairs={{0,4},{1,5},{2,6},{3,7},{4,0},{5,1},{6,2},{7,3},{8,12},{9,13},{10,... | collective-permute-start | bytes 589832 | tf_op jit(solution)/shard_map/ppermute | solution.py:356
  30.9 1.0 %collective-permute-start.4 = (bf16[768,128]{1,0:T(8,128)(2,1)S(1)}, bf16[768,128]{1,0:T(8,128)(2,1)S(1)}, u32[]{:S(2)}, u32[]{:S(2)}) collective-permute-start(bf16[768,128]{1,0:T(8,128)(2,1)S(1)} %regroup.1.refs_0_), channel_id=1, source_target_pairs={{0,6},{1,7},{2,0},{3,1},{4,2},{5,3},{6,4},{7,5},{8,14},{9,15},{10,... | collective-permute-start | bytes 589832 | tf_op jit(solution)/shard_map/ppermute | solution.py:356
  31.9 0.0 collective-permute-start.5
  31.9 3.3 %collective-permute-done.2.refs_1_ = bf16[768,128]{1,0:T(8,128)(2,1)S(1)} collective-permute-done((bf16[768,128]{1,0:T(8,128)(2,1)S(1)}, bf16[768,128]{1,0:T(8,128)(2,1)S(1)}, u32[]{:S(2)}, u32[]{:S(2)}) %collective-permute-start.2) | collective-permute-done | bytes 196640 | tf_op jit(solution)/shard_map/ppermute | solution.py:356
  35.2 0.0 collective-permute-start.6
  35.2 2.8 %collective-permute-done.3.refs_2_ = bf16[768,128]{1,0:T(8,128)(2,1)S(1)} collective-permute-done((bf16[768,128]{1,0:T(8,128)(2,1)S(1)}, bf16[768,128]{1,0:T(8,128)(2,1)S(1)}, u32[]{:S(2)}, u32[]{:S(2)}) %collective-permute-start.3) | collective-permute-done | bytes 196640 | tf_op jit(solution)/shard_map/ppermute | solution.py:356
  38.0 0.0 collective-permute-start.7
  38.0 0.0 collective-permute-done.4.refs_3_
  38.0 0.5 collective-permute-start.8
  38.5 0.0 collective-permute-done.5.refs_4_
  38.5 0.0 collective-permute-done.6.refs_5_
  38.5 0.9 %collective-permute-done.7.refs_6_ = bf16[768,128]{1,0:T(8,128)(2,1)S(1)} collective-permute-done((bf16[768,128]{1,0:T(8,128)(2,1)S(1)}, bf16[768,128]{1,0:T(8,128)(2,1)S(1)}, u32[]{:S(2)}, u32[]{:S(2)}) %collective-permute-start.7) | collective-permute-done | bytes 196640 | tf_op jit(solution)/shard_map/ppermute | solution.py:359
  39.4 0.3 collective-permute-done.8.refs_7_
  39.7 10.2 %sums.1 = (bf16[720,256]{1,0:T(8,128)(2,1)S(1)}, bf16[720,128]{1,0:T(8,128)(2,1)S(1)}, bf16[368,128]{1,0:T(8,128)(2,1)S(1)}, f32[8,128]{1,0:T(8,128)S(1)}) custom-call(f32[2]{0:T(128)} %scale_ref.1, bf16[768,128]{1,0:T(8,128)(2,1)S(1)} %regroup.1.refs_0_, bf16[768,128]{1,0:T(8,128)(2,1)S(1)} %collective-permute-done.2.refs_1_, ...), custom_call_target="tpu_custom_call" | custom-call | tf_op jit(solution)/shard_map/sums/pallas_call | solution.py:365
  49.9 2.1 %collective-permute-start.9 = (bf16[720,128]{1,0:T(8,128)(2,1)S(1)}, bf16[720,128]{1,0:T(8,128)(2,1)S(1)}, u32[]{:S(2)}, u32[]{:S(2)}) collective-permute-start(bf16[720,128]{1,0:T(8,128)(2,1)S(1)} %get-tuple-element.208), channel_id=1, source_target_pairs={{0,1},{1,2},{2,3},{3,4},{4,5},{5,6},{6,7},{7,8},{8,9},{9,10},{10,1... | collective-permute-start | bytes 552968 | tf_op jit(solution)/shard_map/ppermute | solution.py:392
  52.0 7.6 %collective-permute-start.10 = (bf16[368,128]{1,0:T(8,128)(2,1)S(1)}, bf16[368,128]{1,0:T(8,128)(2,1)S(1)}, u32[]{:S(2)}, u32[]{:S(2)}) collective-permute-start(bf16[368,128]{1,0:T(8,128)(2,1)S(1)} %get-tuple-element.209), channel_id=1, source_target_pairs={{1,0},{2,1},{3,2},{4,3},{5,4},{6,5},{7,6},{8,7},{9,8},{10,9},{11,1... | collective-permute-start | bytes 282632 | tf_op jit(solution)/shard_map/ppermute | solution.py:392
  59.7 0.5 slice.89
  60.9 1.0 %collective-permute-done.10 = bf16[368,128]{1,0:T(8,128)(2,1)S(1)} collective-permute-done((bf16[368,128]{1,0:T(8,128)(2,1)S(1)}, bf16[368,128]{1,0:T(8,128)(2,1)S(1)}, u32[]{:S(2)}, u32[]{:S(2)}) %collective-permute-start.10) | collective-permute-done | bytes 94240 | tf_op jit(solution)/shard_map/ppermute | solution.py:392
  61.8 0.0 collective-permute-done.9
  61.8 2.6 %conditional.1 = (bf16[2,720,256]{2,1,0:T(8,128)(2,1)S(1)}) conditional(s32[]{:T(128)} %bitcast.24, (f32[256]{0:T(256)}, bf16[720,256]{1,0:T(8,128)(2,1)S(1)}, bf16[720,128]{1,0:T(8,128)(2,1)S(1)}, bf16[368,128]{1,0:T(8,128)(2,1)S(1)}, bf16[5,5,25,256]{3,2,1,0:T(8,128)(2,1)}) %tuple.30, (s32[2048]{0:T(1024)}, bf16[24,2048]{1,0:T(8,128)(2,1)}, ...), branch_computations={%region_0.0_spmd, %region_1.13_spmd} | conditional | flops 1663755008 | bytes 175900160 | solution.py:539
  61.8 2.4 %conv.1 = bf16[2,720,256]{2,1,0:T(8,128)(2,1)S(1)} custom-call(bf16[720,256]{1,0:T(8,128)(2,1)S(1)} %get-tuple-element.178.feature_ref, bf16[720,128]{1,0:T(8,128)(2,1)S(1)} %get-tuple-element.179.lower_ref, bf16[368,128]{1,0:T(8,128)(2,1)S(1)} %get-tuple-element.180.upper_ref, bf16[5,5,25,256]{3,2,1,0:T(8,128)(2,1)} %get-tuple-element.181.weight_ref, ...), custom_call_target="tpu_custom_call" | custom-call | tf_op jit(solution)/shard_map/cond/branch_0_fun/conv/pallas_call | solution.py:523
  64.5 0.0 copy-start
  64.5 0.9 %copy-done = bf16[2,720,256]{2,1,0:T(8,128)(2,1)} copy-done((bf16[2,720,256]{2,1,0:T(8,128)(2,1)}, bf16[2,720,256]{2,1,0:T(8,128)(2,1)S(1)}, u32[]{:S(2)}) %copy-start) | copy-done | bytes 737304
Async XLA Ops:
  25.3 9.9 %collective-permute-start.2 = (bf16[768,128]{1,0:T(8,128)(2,1)S(1)}, bf16[768,128]{1,0:T(8,128)(2,1)S(1)}, u32[]{:S(2)}, u32[]{:S(2)}) collective-permute-start(bf16[768,128]{1,0:T(8,128)(2,1)S(1)} %regroup.1.refs_0_), channel_id=1, source_target_pairs={{0,2},{1,3},{2,4},{3,5},{4,6},{5,7},{6,0},{7,1},{8,10},{9,11},{10,... | collective-permute-start | bytes 589832 | tf_op jit(solution)/shard_map/ppermute | solution.py:356
  27.3 10.7 %collective-permute-start.3 = (bf16[768,128]{1,0:T(8,128)(2,1)S(1)}, bf16[768,128]{1,0:T(8,128)(2,1)S(1)}, u32[]{:S(2)}, u32[]{:S(2)}) collective-permute-start(bf16[768,128]{1,0:T(8,128)(2,1)S(1)} %regroup.1.refs_0_), channel_id=1, source_target_pairs={{0,4},{1,5},{2,6},{3,7},{4,0},{5,1},{6,2},{7,3},{8,12},{9,13},{10,... | collective-permute-start | bytes 589832 | tf_op jit(solution)/shard_map/ppermute | solution.py:356
  30.9 7.1 %collective-permute-start.4 = (bf16[768,128]{1,0:T(8,128)(2,1)S(1)}, bf16[768,128]{1,0:T(8,128)(2,1)S(1)}, u32[]{:S(2)}, u32[]{:S(2)}) collective-permute-start(bf16[768,128]{1,0:T(8,128)(2,1)S(1)} %regroup.1.refs_0_), channel_id=1, source_target_pairs={{0,6},{1,7},{2,0},{3,1},{4,2},{5,3},{6,4},{7,5},{8,14},{9,15},{10,... | collective-permute-start | bytes 589832 | tf_op jit(solution)/shard_map/ppermute | solution.py:356
  31.9 6.6 %collective-permute-start.5 = (bf16[768,128]{1,0:T(8,128)(2,1)S(1)}, bf16[768,128]{1,0:T(8,128)(2,1)S(1)}, u32[]{:S(2)}, u32[]{:S(2)}) collective-permute-start(bf16[768,128]{1,0:T(8,128)(2,1)S(1)} %regroup.1.refs_0_), channel_id=1, source_target_pairs={{0,1},{1,0},{2,3},{3,2},{4,5},{5,4},{6,7},{7,6},{8,9},{9,8},{10,11... | collective-permute-start | bytes 589832 | tf_op jit(solution)/shard_map/ppermute | solution.py:359
  35.2 3.3 %collective-permute-start.6 = (bf16[768,128]{1,0:T(8,128)(2,1)S(1)}, bf16[768,128]{1,0:T(8,128)(2,1)S(1)}, u32[]{:S(2)}, u32[]{:S(2)}) collective-permute-start(bf16[768,128]{1,0:T(8,128)(2,1)S(1)} %collective-permute-done.2.refs_1_), channel_id=1, source_target_pairs={{0,1},{1,0},{2,3},{3,2},{4,5},{5,4},{6,7},{7,6},{8,9},{9,8},{10,11... | collective-permute-start | bytes 589832 | tf_op jit(solution)/shard_map/ppermute | solution.py:359
  38.0 1.4 %collective-permute-start.7 = (bf16[768,128]{1,0:T(8,128)(2,1)S(1)}, bf16[768,128]{1,0:T(8,128)(2,1)S(1)}, u32[]{:S(2)}, u32[]{:S(2)}) collective-permute-start(bf16[768,128]{1,0:T(8,128)(2,1)S(1)} %collective-permute-done.3.refs_2_), channel_id=1, source_target_pairs={{0,1},{1,0},{2,3},{3,2},{4,5},{5,4},{6,7},{7,6},{8,9},{9,8},{10,11... | collective-permute-start | bytes 589832 | tf_op jit(solution)/shard_map/ppermute | solution.py:359
  38.0 1.7 %collective-permute-start.8 = (bf16[768,128]{1,0:T(8,128)(2,1)S(1)}, bf16[768,128]{1,0:T(8,128)(2,1)S(1)}, u32[]{:S(2)}, u32[]{:S(2)}) collective-permute-start(bf16[768,128]{1,0:T(8,128)(2,1)S(1)} %collective-permute-done.4.refs_3_), channel_id=1, source_target_pairs={{0,1},{1,0},{2,3},{3,2},{4,5},{5,4},{6,7},{7,6},{8,9},{9,8},{10,11... | collective-permute-start | bytes 589832 | tf_op jit(solution)/shard_map/ppermute | solution.py:359
  49.9 12.0 %collective-permute-start.9 = (bf16[720,128]{1,0:T(8,128)(2,1)S(1)}, bf16[720,128]{1,0:T(8,128)(2,1)S(1)}, u32[]{:S(2)}, u32[]{:S(2)}) collective-permute-start(bf16[720,128]{1,0:T(8,128)(2,1)S(1)} %get-tuple-element.208), channel_id=1, source_target_pairs={{0,1},{1,2},{2,3},{3,4},{4,5},{5,6},{6,7},{7,8},{8,9},{9,10},{10,1... | collective-permute-start | bytes 552968 | tf_op jit(solution)/shard_map/ppermute | solution.py:392
  52.0 9.8 %collective-permute-start.10 = (bf16[368,128]{1,0:T(8,128)(2,1)S(1)}, bf16[368,128]{1,0:T(8,128)(2,1)S(1)}, u32[]{:S(2)}, u32[]{:S(2)}) collective-permute-start(bf16[368,128]{1,0:T(8,128)(2,1)S(1)} %get-tuple-element.209), channel_id=1, source_target_pairs={{1,0},{2,1},{3,2},{4,3},{5,4},{6,5},{7,6},{8,7},{9,8},{10,9},{11,1... | collective-permute-start | bytes 282632 | tf_op jit(solution)/shard_map/ppermute | solution.py:392
  64.5 0.9 %copy-start = (bf16[2,720,256]{2,1,0:T(8,128)(2,1)}, bf16[2,720,256]{2,1,0:T(8,128)(2,1)S(1)}, u32[]{:S(2)}) copy-start(bf16[2,720,256]{2,1,0:T(8,128)(2,1)S(1)} %get-tuple-element.395) | copy-start | bytes 2211844

commit v2 on v1

--- a/solution.py
+++ b/solution.py
@@ -15,11 +15,17 @@
 HALF_PAD = 48
 BOX = 256
 EXTRA = 8
+HEAD = 4
 ROW_CODE = 24
 ROW_LAT = 25
 ROW_LON = 28
 ROW_NOTE = 31
 PAY = 32
+SLOTS = 8
+LAT_BAND = 32
+ROWS_IN = 7
+TALL = 2 * HALF_PAD
+LOG2E = 1.4426950408889634
 F32 = jnp.float32
 BF16 = jnp.bfloat16
 
@@ -116,9 +122,16 @@
     rank = ranks(member)
 
     more = jnp.maximum(jnp.broadcast_to(total, (BANDS, 128)).astype(jnp.int32) - 1, 0) >> 7
-    lower = ones_where(iota((BANDS, BANDS), 1) < iota((BANDS, BANDS), 0)).astype(BF16)
-    first = jnp.dot(lower, more.astype(F32).astype(BF16), preferred_element_type=F32)
-    last = first + more.astype(F32)
+    key = more * BANDS + (BANDS - 1 - iota((BANDS, 128), 0))
+    leads = key == jnp.max(key, axis=0, keepdims=True)
+    more = jnp.where(leads, jnp.maximum(more, HEAD), more)
+    key = more * BANDS + (BANDS - 1 - iota((BANDS, 128), 0))
+    more = more.astype(F32)
+    first = jnp.zeros((BANDS, 128), F32)
+    for g in range(BANDS):
+        first = first + jnp.where(key[g : g + 1] > key, more[g : g + 1], 0.0)
+    first = jnp.where(leads, 0.0, first)
+    last = first + more
     first_wide = jnp.concatenate([first, first], axis=1)
 
     for k in range(chunks):
@@ -134,11 +147,13 @@
     note = jnp.concatenate(notes, axis=0)
     of_band = ones_where((iota((BOX, 128), 0) >> 4) == iota((BOX, 128), 1)).astype(BF16)
     band_sums = jnp.dot(note.astype(BF16), of_band, preferred_element_type=F32)
-    tile_sums = jnp.broadcast_to(jnp.sum(note, axis=0, keepdims=True), (8, BOX)).astype(jnp.int32)
-    tile_more = (jnp.maximum(tile_sums - 1, 0) >> 7).astype(F32).astype(BF16)
-    more_sums = jnp.dot(tile_more, of_band, preferred_element_type=F32)
+    tile_sums = jnp.broadcast_to(jnp.sum(note, axis=0, keepdims=True), (BANDS, BOX)).astype(jnp.int32)
+    tile_more = jnp.maximum(tile_sums - 1, 0) >> 7
+    tile_more = jnp.where((iota((BANDS, BOX), 1) >> 4) == iota((BANDS, BOX), 0), tile_more, 0).astype(F32)
+    most = jnp.max(tile_more, axis=1, keepdims=True)
+    more_sums = jnp.sum(tile_more, axis=1, keepdims=True) + jnp.maximum(HEAD - most, 0.0)
     band_most = jnp.max(jnp.max(band_sums, axis=1, keepdims=True), axis=0, keepdims=True)
-    more_most = jnp.max(jnp.max(more_sums, axis=1, keepdims=True), axis=0, keepdims=True)
+    more_most = jnp.max(more_sums, axis=0, keepdims=True)
     over = jnp.where((band_most > BOX - 1) | (more_most > EXTRA), 1.0, 0.0)
 
     narrow = iota((PAY, 128), 0)
@@ -152,38 +167,27 @@
         out_ref[rows, :] = jnp.where(narrow == ROW_NOTE, code, moved[rows]).astype(BF16)
 
 
-def sums_kernel(scale_ref, *refs):
-    (
-        *block_refs,
-        feature_ref,
-        lower_ref,
-        upper_ref,
-        over_ref,
-        left_ref,
-        right_ref,
-        sums_ref,
-        wide_ref,
-        codes_ref,
-        codes_smem,
-        sem,
-    ) = refs
-    first_row = (lax.axis_index("obs") * ROWS_DEV).astype(F32)
+def sums_kernel(count, last, scale_ref, *refs):
+    block_refs, refs = refs[:count], refs[count:]
+    if last:
+        *before_refs, feature_ref, edge_ref, over_ref = refs[:-7]
+        left_ref, right_ref, codes_ref, codes_smem, sem, sums_ref, wide_ref = refs[-7:]
+    else:
+        sums_ref, over_ref, left_ref, right_ref, codes_ref, codes_smem, sem = refs
+    shard = lax.axis_index("obs")
     scale = jnp.full((8, 128), 1.0, F32)
-    inv_lat = 0.5 / (scale * scale_ref[0] * scale_ref[0])
-    inv_lon = 0.5 / (scale * scale_ref[1] * scale_ref[1])
-    inv_lat, inv_lon = inv_lat[0:1], inv_lon[0:1]
-    row_mid = iota((8, 128), 0).astype(F32) + 0.5 + first_row
+    lat_scale = (-0.5 * LOG2E) / (scale * scale_ref[0] * scale_ref[0])
+    lon_scale = (-0.5 * LOG2E) / (scale * scale_ref[1] * scale_ref[1])
+    lat_scale, lon_scale = lat_scale[0:1], lon_scale[0:1]
+    row_mid = ((iota((8, 128), 0) + (shard * ROWS_DEV - 2)) & (LAT_BAND - 1)).astype(F32) + 0.5
     line = iota((2 * HALF_PAD, 128), 0)
     past = (line >= HALF_PAD).astype(jnp.int32)
     col_mid = (2 * (line - HALF_PAD * past) + past).astype(F32) + 0.5
-    keep = iota((PAY, 128), 0) <= ROW_CODE
-    blocks = len(block_refs)
-    tall = 2 * HALF_PAD
-
     lane = iota((8, 128), 1)
     sub = iota((8, 128), 0)
+
     codes = jnp.zeros((8, 128), F32)
-    for k in range(blocks):
+    for k in range(count):
         for e in range(EXTRA):
             at = (BANDS + e) * PAY + 16
             note = block_refs[k][at : at + 16, :].astype(F32)[15:16]
@@ -192,113 +196,138 @@
     copy = pltpu.make_async_copy(codes_ref, codes_smem, sem)
     copy.start()
 
-    def factors(start):
-        for k in range(blocks):
+    def factors(start, slot):
+        for k in range(count):
             lanes = slice(k * 128, (k + 1) * 128)
-            block = block_refs[k][pl.ds(start, PAY), :].astype(F32)
-            lat_at = block[ROW_LAT : ROW_LAT + 1] + block[ROW_LAT + 1 : ROW_LAT + 2]
-            lat_at = lat_at + block[ROW_LAT + 2 : ROW_LAT + 3]
-            lon_at = block[ROW_LON : ROW_LON + 1] + block[ROW_LON + 1 : ROW_LON + 2]
-            lon_at = lon_at + block[ROW_LON + 2 : ROW_LON + 3]
+            value = block_refs[k][pl.ds(start, PAY), :].astype(F32)
+            tail = value[24:32]
+            lat_at = tail[1:2] + tail[2:3] + tail[3:4]
+            lon_at = tail[4:5] + tail[5:6] + tail[6:7]
             lat_diff = row_mid - lat_at
-            lat_weight = jnp.exp(-(lat_diff * lat_diff) * inv_lat)
+            lat_weight = jnp.exp2(lat_diff * lat_diff * lat_scale)
             lon_diff = col_mid - lon_at
-            lon_weight = jnp.exp(-(lon_diff * lon_diff) * inv_lon)
-            value = jnp.where(keep, block, 0.0)
-            present = block[ROW_CODE : ROW_CODE + 1]
-            for r in range(ROWS_DEV):
-                weight = lat_weight[r : r + 1]
-                left_ref[r * PAY : (r + 1) * PAY, lanes] = (value * weight).astype(BF16)
-                left_ref[(ROWS_DEV + r) * PAY : (ROWS_DEV + r + 1) * PAY, lanes] = jnp.broadcast_to(
-                    present * weight, (PAY, 128)
-                ).astype(BF16)
-            right_ref[:, lanes] = lon_weight.astype(BF16)
+            lon_weight = jnp.exp2(lon_diff * lon_diff * lon_scale)
+            for r in range(ROWS_IN):
+                left_ref[slot, r * PAY : (r + 1) * PAY, lanes] = (value * lat_weight[r : r + 1]).astype(BF16)
+            right_ref[slot, :, lanes] = lon_weight.astype(BF16)
+
+    slots = left_ref.shape[0]
+    for slot in range(slots):
+        left_ref[slot, ROWS_IN * PAY :, :] = jnp.zeros((PAY, count * 128), BF16)
 
     def main(p, carry):
-        factors(pl.multiple_of(p * PAY, PAY))
-        start = pl.multiple_of((p + 1) * tall, tall)
-        sums_ref[pl.ds(start, tall), :] = dot_nt(right_ref[...], left_ref[...])
+        for slot in range(slots):
+            at = p * slots + slot
+            factors(pl.multiple_of(at * PAY, PAY), slot)
+            start = pl.multiple_of((at + 1) * TALL, TALL)
+            sums_ref[pl.ds(start, TALL), :] = dot_nt(right_ref[slot], left_ref[slot])
         return carry
 
-    sums_ref[0:tall, :] = jnp.zeros((tall, 256), F32)
-    lax.fori_loop(0, BANDS, main, 0)
+    sums_ref[0:TALL, :] = jnp.zeros((TALL, 256), F32)
+    lax.fori_loop(0, BANDS // slots, main, 0)
+
     copy.wait()
     used = jnp.int32(0)
-    for e in range(EXTRA):
-        for k in range(blocks):
-            used = jnp.where(codes_smem[k, e] > 0, e + 1, used)
+    for e in range(HEAD, EXTRA):
+        for k in range(count):
+            used = jnp.where(codes_smem[k, e] > 0, e + 1 - HEAD, used)
+    for e in range(HEAD):
+        factors((BANDS + e) * PAY, e)
+    for k in range(count):
+        lanes = slice(k * 128, (k + 1) * 128)
+        right = jnp.concatenate([right_ref[e, :, lanes] for e in range(HEAD)], axis=1)
+        left = jnp.concatenate([left_ref[e, :, lanes] for e in range(HEAD)], axis=1)
+        start = pl.multiple_of(codes_smem[k, 0] * TALL, TALL)
+        sums_ref[pl.ds(start, TALL), :] += dot_nt(right, left)
 
     def extra(e, carry):
-        factors(pl.multiple_of((BANDS + e) * PAY, PAY))
-        for k in range(blocks):
+        factors(pl.multiple_of((BANDS + HEAD + e) * PAY, PAY), 0)
+        for k in range(count):
             lanes = slice(k * 128, (k + 1) * 128)
-            start = pl.multiple_of(codes_smem[k, e] * tall, tall)
-            sums_ref[pl.ds(start, tall), :] += dot_nt(right_ref[:, lanes], left_ref[:, lanes])
+            start = pl.multiple_of(codes_smem[k, HEAD + e] * TALL, TALL)
+            sums_ref[pl.ds(start, TALL), :] += dot_nt(right_ref[0, :, lanes], left_ref[0, :, lanes])
         return carry
 
     lax.fori_loop(0, used, extra, 0)
 
-    channel = iota((HALF_PAD, 128), 1) & (PAY - 1)
+    over = block_refs[0][16:PAY, :].astype(F32)[15:16]
+    for k in range(1, count):
+        over = jnp.maximum(over, block_refs[k][16:PAY, :].astype(F32)[15:16])
+    over = jnp.broadcast_to(over, (8, 128))
+    if not last:
+        over_ref[...] = over
+        return
+    sums_before, overs_before = before_refs[0::2], before_refs[1::2]
+    for ref in overs_before:
+        over = jnp.maximum(over, ref[...])
+    over_ref[...] = over
+
+    channel = iota((TALL, 128), 1) & (PAY - 1)
+    dense = iota((TALL, 128), 1) - channel + ROW_CODE
     for block in range(BANDS):
-        for odd in range(2):
-            start = (2 * (block + 1) + odd) * HALF_PAD
-            total = sums_ref[start : start + HALF_PAD, 0:128]
-            density = sums_ref[start : start + HALF_PAD, 128:256]
-            feature = jnp.where(
-                channel < 24,
-                total / jnp.maximum(density, 1.0),
-                jnp.where(channel == 24, jnp.log(1.0 + density), 0.0),
-            )
-            wide_ref[block * HALF : (block + 1) * HALF, odd * 128 : (odd + 1) * 128] = feature[:HALF]
+        rows = slice(block * HALF, (block + 1) * HALF)
+        at = slice((block + 1) * TALL, (block + 2) * TALL)
+        for half in range(2):
+            lanes = slice(half * 128, (half + 1) * 128)
+            total = sums_ref[at, lanes]
+            for ref in sums_before:
+                total = total + ref[at, lanes]
+            density = jnp.take_along_axis(total, dense, axis=1)
+            feature = total * (1.0 / jnp.maximum(density, 1.0))
+            feature = jnp.where(channel < 24, feature, jnp.where(channel == 24, jnp.log(1.0 + density), 0.0))
+            wide_ref[rows, lanes] = feature[0:HALF]
+            wide_ref[rows, 256 + half * 128 : 256 + (half + 1) * 128] = feature[HALF_PAD : HALF_PAD + HALF]
     feature_ref[...] = wide_ref[...].astype(BF16)
-    lower_ref[...] = jnp.concatenate([wide_ref[:, 64:128], wide_ref[:, 192:256]], axis=1).astype(BF16)
-    top = jnp.concatenate([wide_ref[0:368, 0:32], wide_ref[0:368, 128:160]], axis=1)
-    rest = jnp.concatenate([wide_ref[368:720, 0:32], wide_ref[368:720, 128:160]], axis=1)
-    rest = jnp.concatenate([rest, jnp.zeros((16, 64), F32)], axis=0)
-    upper_ref[...] = jnp.concatenate([top, rest], axis=1).astype(BF16)
-    over = block_refs[0][0:PAY, :].astype(F32)[ROW_NOTE:PAY]
-    for k in range(1, blocks):
-        over = jnp.maximum(over, block_refs[k][0:PAY, :].astype(F32)[ROW_NOTE:PAY])
-    over_ref[...] = jnp.broadcast_to(over, (8, 128))
-
-
-def conv_kernel(feature_ref, lower_ref, upper_ref, weight_ref, bias_ref, out_ref, wide_ref, w_ref):
+
+    @pl.when(shard == 0)
+    def _():
+        edge_ref[...] = jnp.concatenate([wide_ref[:, 0:64], wide_ref[:, 256:320]], axis=1).astype(BF16)
+
+    @pl.when(shard != 0)
+    def _():
+        edge_ref[...] = jnp.concatenate([wide_ref[:, 192:256], wide_ref[:, 448:512]], axis=1).astype(BF16)
+
+
+def conv_kernel(feature_ref, edge_ref, weight_ref, bias_ref, out_ref, wide_ref, w_ref):
     columns = feature_ref.shape[0]
+    shard = lax.axis_index("obs")
     w_ref[...] = jnp.zeros(w_ref.shape, BF16)
     channels = weight_ref.shape[2]
-    zero = jnp.zeros((PAY - channels, 256), BF16)
-
-    def put(shift, at, out_row, tap, odd):
-        e = 2 * (shift + 1) + odd
-        if e < 5:
-            part = jnp.concatenate([weight_ref[tap, e].astype(F32), zero.astype(F32)], axis=0)
-            w_ref[shift + 1, at : at + PAY, out_row * 256 : (out_row + 1) * 256] = part.astype(BF16)
-
-    for shift in (-1, 0, 1):
+    zero = jnp.zeros((PAY - channels, 256), F32)
+    for shift in range(3):
         for odd in range(2):
-            for row in range(ROWS_DEV):
-                for out_row in range(2):
-                    tap = row - 2 * out_row + 2
-                    if 0 <= tap < 5:
-                        put(shift, odd * 128 + row * PAY, out_row, tap, odd)
-            for row in range(2):
-                put(shift, 256 + odd * 64 + row * PAY, 0, row, odd)
-            put(shift, 384 + odd * 32, 1, 4, odd)
-
-    edge = 8
-    wide_ref[edge : edge + columns, 0:256] = feature_ref[...].astype(F32)
-    wide_ref[edge : edge + columns, 256:384] = lower_ref[...].astype(F32)
-    upper = upper_ref[...].astype(F32)
-    wide_ref[edge : edge + 368, 384:448] = upper[:, 0:64]
-    wide_ref[edge + 368 : edge + columns, 384:448] = upper[: columns - 368, 64:128]
-    wide_ref[edge : edge + columns, 448:512] = jnp.zeros((columns, 64), F32)
-    wide_ref[edge - 1 : edge, :] = wide_ref[edge + columns - 1 : edge + columns, :]
-    wide_ref[edge + columns : edge + columns + 1, :] = wide_ref[edge : edge + 1, :]
+            if 2 * shift + odd < 5:
+                for tap in range(5):
+                    part = weight_ref[tap, 2 * shift + odd].astype(F32)
+                    part = jnp.concatenate([part, zero], axis=0).astype(BF16)
+                    for out_row in range(2):
+                        at = odd * 256 + (tap + 2 * out_row) * PAY
+                        w_ref[shift, at : at + PAY, out_row * 256 : (out_row + 1) * 256] = part
+
+    border = 8
+    inner = slice(border, border + columns)
+    wide_ref[inner, :] = feature_ref[...].astype(F32)
+
+    @pl.when(shard == 0)
+    def _():
+        edge = edge_ref[...].astype(F32)
+        wide_ref[inner, 0:64] = edge[:, 0:64]
+        wide_ref[inner, 256:320] = edge[:, 64:128]
+
+    @pl.when(shard == lax.axis_size("obs") - 1)
+    def _():
+        edge = edge_ref[...].astype(F32)
+        wide_ref[inner, 192:256] = edge[:, 0:64]
+        wide_ref[inner, 448:512] = edge[:, 64:128]
+
+    wide_ref[border - 1 : border, :] = wide_ref[border + columns - 1 : border + columns, :]
+    wide_ref[border + columns : border + columns + 1, :] = wide_ref[border : border + 1, :]
 
     total = None
-    for shift in (-1, 0, 1):
-        moved = wide_ref[edge + shift : edge + shift + columns, :].astype(BF16)
-        part = jnp.dot(moved, w_ref[shift + 1], preferred_element_type=F32)
+    for shift in range(3):
+        start = border + shift - 1
+        moved = wide_ref[start : start + columns, :].astype(BF16)
+        part = jnp.dot(moved, w_ref[shift], preferred_element_type=F32)
         total = part if total is None else total + part
     bias = bias_ref[...]
     out_ref[0] = (total[:, 0:256] + bias).astype(BF16)
@@ -358,32 +387,49 @@
     def across(value):
         return lax.ppermute(value, "obs", [(s, s ^ 1) for s in range(count)])
 
-    mine = [own] + [along(own, steps) for steps in range(1, chips)]
-    blocks = mine + [across(value) for value in mine]
     columns = LON // 2
     shape = jax.ShapeDtypeStruct
-    return pl.pallas_call(
-        sums_kernel,
-        out_shape=(
-            shape((columns, 256), BF16),
-            shape((columns, 128), BF16),
-            shape((368, 128), BF16),
-            shape((8, 128), F32),
-        ),
-        in_specs=[pl.BlockSpec(memory_space=pltpu.SMEM)] + [vmem()] * len(blocks),
-        out_specs=(vmem(),) * 4,
-        scratch_shapes=[
-            pltpu.VMEM((256, len(blocks) * 128), BF16),
-            pltpu.VMEM((2 * HALF_PAD, len(blocks) * 128), BF16),
-            pltpu.VMEM((2 * HALF_PAD * (BANDS + 1), 256), F32),
-            pltpu.VMEM((columns, 256), F32),
+
+    def sums(blocks, before):
+        last = before is not None
+        tall = TALL * (BANDS + 1)
+        if last:
+            out_shape = (
+                shape((columns, 512), BF16),
+                shape((columns, 128), BF16),
+                shape((8, 128), F32),
+            )
+        else:
+            out_shape = (shape((tall, 256), F32), shape((8, 128), F32))
+            before = ()
+        slots = SLOTS
+        scratch = [
+            pltpu.VMEM((slots, 256, len(blocks) * 128), BF16),
+            pltpu.VMEM((slots, TALL, len(blocks) * 128), BF16),
             pltpu.VMEM((8, 128), jnp.int32),
             pltpu.SMEM((8, 128), jnp.int32),
             pltpu.SemaphoreType.DMA,
-        ],
-        compiler_params=params(32),
-        name="sums",
-    )(scale, *blocks)
+        ]
+        if last:
+            scratch += [pltpu.VMEM((tall, 256), F32), pltpu.VMEM((columns, 512), F32)]
+        return pl.pallas_call(
+            functools.partial(sums_kernel, len(blocks), last),
+            out_shape=out_shape,
+            in_specs=[pl.BlockSpec(memory_space=pltpu.SMEM)] + [vmem()] * (len(blocks) + len(before)),
+            out_specs=(vmem(),) * len(out_shape),
+            scratch_shapes=scratch,
+            compiler_params=params(32),
+            cost_estimate=pl.CostEstimate(
+                flops=len(blocks) * 1_200_000_000, bytes_accessed=len(blocks) * 200_000, transcendentals=0
+            ),
+            name="sums_last" if last else "sums",
+        )(scale, *blocks, *before)
+
+    far, after, ahead = (along(own, steps) for steps in (2, 1, -1))
+    before = sums([own, across(own)], None)
+    after, ahead, far, *before = lax.optimization_barrier((after, ahead, far, *before))
+    there = [across(value) for value in (after, ahead, far)]
+    return sums([after, ahead, far, *there], before)
 
 
 def from_behind(value, axis, steps):
@@ -490,7 +536,10 @@
     )
     arrived = lax.all_to_all(outgoing, "band", split_axis=2, concat_axis=2, tiled=True)
     placed = jnp.take(arrived, source_of_block, axis=2).reshape(channels + 1, lat_dev, LON)
-    band_rows = lax.psum_scatter(placed, "obs", scatter_dimension=1, tiled=True)
+    spread = lax.all_to_all(
+        placed.reshape(channels + 1, obs_count, ROWS_DEV, LON), "obs", split_axis=1, concat_axis=1, tiled=True
+    )
+    band_rows = jnp.sum(spread, axis=1)
     density = band_rows[channels]
     feature = jnp.concatenate(
         [band_rows[:channels] / jnp.maximum(density, 1.0)[None], jnp.log(1.0 + density)[None]],
@@ -512,18 +561,19 @@
 
 
 def body(*args):
-    *_, conv_weight, conv_bias = args
-    feature, lower, upper, over = fast_features(*args[:7])
-    lower = from_behind(lower, ("band", "obs"), 1)
-    upper = from_behind(upper, ("band", "obs"), -1)
-
-    def finish(feature, lower, upper, *args):
+    feature, edge, over = fast_features(*args[:7])
+    bands, shards = lax.axis_size("band"), lax.axis_size("obs")
+    down = [(band * shards, (band + 1) * shards) for band in range(bands - 1)]
+    up = [(band * shards + shards - 1, band * shards - 1) for band in range(1, bands)]
+    edge = lax.ppermute(edge, ("band", "obs"), down + up)
+
+    def finish(feature, edge, *args):
         *_, conv_weight, conv_bias = args
         columns = LON // 2
         return pl.pallas_call(
             conv_kernel,
             out_shape=jax.ShapeDtypeStruct((2, columns, 256), BF16),
-            in_specs=[vmem()] * 5,
+            in_specs=[vmem()] * 4,
             out_specs=vmem(),
             scratch_shapes=[
                 pltpu.VMEM((columns + 16, 512), F32),
@@ -531,12 +581,12 @@
             ],
             compiler_params=params(32),
             name="conv",
-        )(feature, lower, upper, conv_weight, conv_bias.reshape(1, -1))
-
-    def whole(feature, lower, upper, *args):
+        )(feature, edge, conv_weight, conv_bias.reshape(1, -1))
+
+    def whole(feature, edge, *args):
         return general(*args)
 
-    return lax.cond(over[0, 0] > 0.0, whole, finish, feature, lower, upper, *args)
+    return lax.cond(over[0, 0] > 0.0, whole, finish, feature, edge, *args)
 
 
 def solution(mesh):

time: 72.9 us -> 53.7 us (0.74)
  between operations: 14.1 us -> 0.81 us
  starting transfers between devices: 16.9 us -> 8.71 us
  waiting for transfers between devices: 8.27 us -> 14.7 us
  Pallas kernels: 17.2 us -> 13.7 us
    ppermute x2 -> x1, starting transfers between devices: 9.78 us -> 1.97 us  [body(): edge = lax.ppermute(edge, ('band', 'obs'), down + up)]
    ppermute x2 -> x1, waiting for transfers between devices: 0.99 us -> 6.39 us  [body(): edge = lax.ppermute(edge, ('band', 'obs'), down + up)]
    pallas_call x1 -> x2, Pallas kernels: 10.2 us -> 7.47 us  [sums(): pl.pallas_call(functools.partial(sums_kernel, len(blocks), last), out_sha...]
    ppermute x3, waiting for transfers between devices: 6.07 us -> 6.86 us  [along(): return lax.ppermute(value, 'obs', order)]
  transfers between devices with their start and end apart: 9 -> 8, of which waited for: 5 -> 7; matrix products, arithmetic and copies ran while one was open for 1% -> 1% of each run, Pallas kernels for 0% -> 4%
where the time goes in v2:
time: 53.7 us
  waiting for transfers between devices  14.7 us (27%)
  blocking collectives  14.2 us (26%)
  Pallas kernels  13.7 us (26%)
  starting transfers between devices  8.71 us (16%)
  local copies, waits for them, and re-layouts  1.41 us (3%)
  between operations  0.81 us (2%)
    all_to_all x1, blocking collectives, fast_features(): came = lax.all_to_all(sent, 'band', split_axis=0, concat_axis=0, tiled=True)  14.2 us
    pallas_call x2, Pallas kernels, sums(): pl.pallas_call(functools.partial(sums_kernel, len(blocks), last), out_sha...  7.47 us
    ppermute x3, waiting for transfers between devices, along(): return lax.ppermute(value, 'obs', order)  6.86 us
    ppermute x1, waiting for transfers between devices, body(): edge = lax.ppermute(edge, ('band', 'obs'), down + up)  6.39 us
    ppermute x3, starting transfers between devices, along(): return lax.ppermute(value, 'obs', order)  5.97 us
    pallas_call x1, Pallas kernels, fast_features(): pl.pallas_call(pack_kernel, out_shape=jax.ShapeDtypeStruct((BANDS * PAY,...  2.39 us
    pallas_call x1, Pallas kernels, fast_features(): pl.pallas_call(regroup_kernel, out_shape=jax.ShapeDtypeStruct((groups * P...  2.18 us
    ppermute x1, starting transfers between devices, body(): edge = lax.ppermute(edge, ('band', 'obs'), down + up)  1.97 us
  transfers between devices with their start and end apart: 8, of which 7 were waited for; matrix products, arithmetic and copies ran while one was open for 1% of the time, Pallas kernels for 4%

profile of v2, /device:TPU:8, one launch (start us, length us, event | category | flops | bytes accessed | tf_op | source)
XLA Modules:
  0.0 53.7 jit_solution(10438911480807906602)
XLA Ops:
  0.0 2.4 %pack.1 = bf16[512,256]{1,0:T(8,128)(2,1)S(1)} custom-call(bf16[24,2048]{1,0:T(8,128)(2,1)} %values_ref.1, s32[16,128]{1,0:T(8,128)} %bitcast.90, s32[16,128]{1,0:T(8,128)} %bitcast.95, s32[16,128]{1,0:T(8,128)} %bitcast.96, f32[2,2048]{1,0:T(2,128)} %frac_ref.1, s32[2,128]{1,0:T(2,128)} %bitcast.100), custom_call_target="tpu_custom_call" | custom-call | tf_op jit(solution)/shard_map/pack/pallas_call | solution.py:347
  2.4 14.2 %all_to_all.24 = bf16[16,32,256]{2,1,0:T(8,128)(2,1)S(1)} all-to-all(bf16[16,32,256]{2,1,0:T(8,128)(2,1)S(1)} %bitcast.81), channel_id=1, replica_groups=mesh['band'=16,'obs'=8] {'band'}, dimensions={0} | all-to-all | bytes 524288 | tf_op jit(solution)/shard_map/all_to_all | solution.py:366
  16.6 2.2 %regroup.1.refs_0_ = bf16[768,128]{1,0:T(8,128)(2,1)S(1)} custom-call(bf16[512,256]{1,0:T(8,128)(2,1)S(1)} %bitcast.80), custom_call_target="tpu_custom_call" | custom-call | tf_op jit(solution)/shard_map/regroup/pallas_call | solution.py:368
  18.7 0.0 copy-start.10
  18.7 0.1 collective-permute-start.5
  18.8 2.0 %collective-permute-start.2 = (bf16[768,128]{1,0:T(8,128)(2,1)S(1)}, bf16[768,128]{1,0:T(8,128)(2,1)S(1)}, u32[]{:S(2)}, u32[]{:S(2)}) collective-permute-start(bf16[768,128]{1,0:T(8,128)(2,1)S(1)} %regroup.1.refs_0_), channel_id=1, source_target_pairs={{0,2},{1,3},{2,4},{3,5},{4,6},{5,7},{6,0},{7,1},{8,10},{9,11},{10,... | collective-permute-start | bytes 589832 | tf_op jit(solution)/shard_map/ppermute | solution.py:385
  20.8 2.2 %collective-permute-start.3 = (bf16[768,128]{1,0:T(8,128)(2,1)S(1)}, bf16[768,128]{1,0:T(8,128)(2,1)S(1)}, u32[]{:S(2)}, u32[]{:S(2)}) collective-permute-start(bf16[768,128]{1,0:T(8,128)(2,1)S(1)} %regroup.1.refs_0_), channel_id=1, source_target_pairs={{0,6},{1,7},{2,0},{3,1},{4,2},{5,3},{6,4},{7,5},{8,14},{9,15},{10,... | collective-permute-start | bytes 589832 | tf_op jit(solution)/shard_map/ppermute | solution.py:385
  23.0 1.8 %collective-permute-start.4 = (bf16[768,128]{1,0:T(8,128)(2,1)S(1)}, bf16[768,128]{1,0:T(8,128)(2,1)S(1)}, u32[]{:S(2)}, u32[]{:S(2)}) collective-permute-start(bf16[768,128]{1,0:T(8,128)(2,1)S(1)} %regroup.1.refs_0_), channel_id=1, source_target_pairs={{0,4},{1,5},{2,6},{3,7},{4,0},{5,1},{6,2},{7,3},{8,12},{9,13},{10,... | collective-permute-start | bytes 589832 | tf_op jit(solution)/shard_map/ppermute | solution.py:385
  24.8 0.0 collective-permute-done.5.refs_1_
  24.8 2.2 %sums.1 = (f32[1632,256]{1,0:T(8,128)S(1)}, f32[8,128]{1,0:T(8,128)S(1)}) custom-call(f32[2]{0:T(128)} %scale_ref.3, bf16[768,128]{1,0:T(8,128)(2,1)S(1)} %regroup.1.refs_0_, bf16[768,128]{1,0:T(8,128)(2,1)S(1)} %collective-permute-done.5.refs_1_), custom_call_target="tpu_custom_call" | custom-call | flops 2400000000 | bytes 400000 | tf_op jit(solution)/shard_map/sums/pallas_call | solution.py:415
  27.0 1.5 %collective-permute-done.2.refs_0_ = bf16[768,128]{1,0:T(8,128)(2,1)S(1)} collective-permute-done((bf16[768,128]{1,0:T(8,128)(2,1)S(1)}, bf16[768,128]{1,0:T(8,128)(2,1)S(1)}, u32[]{:S(2)}, u32[]{:S(2)}) %collective-permute-start.2) | collective-permute-done | bytes 196640 | tf_op jit(solution)/shard_map/ppermute | solution.py:385
  28.4 3.5 %collective-permute-done.3.refs_1_ = bf16[768,128]{1,0:T(8,128)(2,1)S(1)} collective-permute-done((bf16[768,128]{1,0:T(8,128)(2,1)S(1)}, bf16[768,128]{1,0:T(8,128)(2,1)S(1)}, u32[]{:S(2)}, u32[]{:S(2)}) %collective-permute-start.3) | collective-permute-done | bytes 196640 | tf_op jit(solution)/shard_map/ppermute | solution.py:385
  32.0 1.9 %collective-permute-done.4.refs_2_ = bf16[768,128]{1,0:T(8,128)(2,1)S(1)} collective-permute-done((bf16[768,128]{1,0:T(8,128)(2,1)S(1)}, bf16[768,128]{1,0:T(8,128)(2,1)S(1)}, u32[]{:S(2)}, u32[]{:S(2)}) %collective-permute-start.4) | collective-permute-done | bytes 196640 | tf_op jit(solution)/shard_map/ppermute | solution.py:385
  33.8 0.0 copy-start.1
  33.9 0.0 copy-start.3
  33.9 0.0 copy-start.4
  33.9 0.0 copy-start.5
  33.9 0.0 copy-start.6
  33.9 0.0 copy-start.7
  33.9 0.0 copy-start.8
  33.9 0.0 copy-start.9
  33.9 0.1 collective-permute-start.6
  34.0 0.5 collective-permute-start.7
  34.5 0.1 collective-permute-start.8
  34.6 0.8 %collective-permute-done.6.refs_3_ = bf16[768,128]{1,0:T(8,128)(2,1)S(1)} collective-permute-done((bf16[768,128]{1,0:T(8,128)(2,1)S(1)}, bf16[768,128]{1,0:T(8,128)(2,1)S(1)}, u32[]{:S(2)}, u32[]{:S(2)}) %collective-permute-start.6) | collective-permute-done | bytes 196640 | tf_op jit(solution)/shard_map/ppermute | solution.py:388
  35.4 0.3 collective-permute-done.7.refs_4_
  35.7 0.3 collective-permute-done.8.refs_5_
  36.0 0.0 copy-done.10
  36.0 5.3 %sums_last.1 = (bf16[720,512]{1,0:T(8,128)(2,1)S(1)}, bf16[720,128]{1,0:T(8,128)(2,1)S(1)}, f32[8,128]{1,0:T(8,128)S(1)}) custom-call(f32[2]{0:T(128)S(1)} %copy-done.10, bf16[768,128]{1,0:T(8,128)(2,1)S(1)} %collective-permute-done.2.refs_0_, bf16[768,128]{1,0:T(8,128)(2,1)S(1)} %collective-permute-done.3.refs_1_, ...), custom_call_target="tpu_custom_call" | custom-call | flops 7200000000 | bytes 1200000 | tf_op jit(solution)/shard_map/sums_last/pallas_call | solution.py:415
  41.3 2.0 %collective-permute-start.9 = (bf16[720,128]{1,0:T(8,128)(2,1)S(1)}, bf16[720,128]{1,0:T(8,128)(2,1)S(1)}, u32[]{:S(2)}, u32[]{:S(2)}) collective-permute-start(bf16[720,128]{1,0:T(8,128)(2,1)S(1)} %get-tuple-element.218), channel_id=1, source_target_pairs={{0,8},{8,16},{16,24},{24,32},{32,40},{40,48},{48,56},{56,64},{64,7... | collective-permute-start | bytes 552968 | tf_op jit(solution)/shard_map/ppermute | solution.py:568
  43.3 0.5 slice.89
  44.5 6.4 %collective-permute-done.9 = bf16[720,128]{1,0:T(8,128)(2,1)S(1)} collective-permute-done((bf16[720,128]{1,0:T(8,128)(2,1)S(1)}, bf16[720,128]{1,0:T(8,128)(2,1)S(1)}, u32[]{:S(2)}, u32[]{:S(2)}) %collective-permute-start.9) | collective-permute-done | bytes 184352 | tf_op jit(solution)/shard_map/ppermute | solution.py:568
  50.9 0.0 copy-done.1
  50.9 0.0 copy-done.3
  50.9 0.0 copy-done.4
  50.9 0.0 copy-done.5
  50.9 0.0 copy-done.6
  50.9 0.0 copy-done.7
  50.9 0.0 copy-done.8
  50.9 0.0 copy-done.9
  50.9 1.9 %conditional.1 = (bf16[2,720,256]{2,1,0:T(8,128)(2,1)S(1)}) conditional(s32[]{:T(128)} %bitcast.24, (f32[256]{0:T(256)S(1)}, bf16[720,512]{1,0:T(8,128)(2,1)S(1)}, bf16[720,128]{1,0:T(8,128)(2,1)S(1)}, bf16[5,5,25,256]{3,2,1,0:T(8,128)(2,1)S(1)}) %tuple.78, (s32[2048]{0:T(1024)S(1)}, bf16[24,2048]{1,0:T(8,128)(2,1)S(1)}, s32[2048]{0:T(1024)S(1)}, ...), branch_computations={%region_0.0_spmd, %region_1.13_spmd} | conditional | flops 1663610880 | bytes 172523328 | solution.py:589
  50.9 1.7 %conv.1 = bf16[2,720,256]{2,1,0:T(8,128)(2,1)S(1)} custom-call(bf16[720,512]{1,0:T(8,128)(2,1)S(1)} %get-tuple-element.176.feature_ref, bf16[720,128]{1,0:T(8,128)(2,1)S(1)} %get-tuple-element.177.edge_ref, bf16[5,5,25,256]{3,2,1,0:T(8,128)(2,1)S(1)} %get-tuple-element.178.weight_ref, f32[1,256]{1,0:T(1,128)S(1)} %bitcast.99), custom_call_target="tpu_custom_call" | custom-call | tf_op jit(solution)/shard_map/cond/branch_0_fun/conv/pallas_call | solution.py:573
  52.8 0.0 copy-start
  52.8 0.9 %copy-done = bf16[2,720,256]{2,1,0:T(8,128)(2,1)} copy-done((bf16[2,720,256]{2,1,0:T(8,128)(2,1)}, bf16[2,720,256]{2,1,0:T(8,128)(2,1)S(1)}, u32[]{:S(2)}) %copy-start) | copy-done | bytes 737304
Async XLA Ops:
  18.7 17.2 %copy-start.10 = (f32[2]{0:T(128)S(1)}, f32[2]{0:T(128)}, u32[]{:S(2)}) copy-start(f32[2]{0:T(128)} %scale_ref.3) | copy-start | bytes 28
  18.7 6.1 %collective-permute-start.5 = (bf16[768,128]{1,0:T(8,128)(2,1)S(1)}, bf16[768,128]{1,0:T(8,128)(2,1)S(1)}, u32[]{:S(2)}, u32[]{:S(2)}) collective-permute-start(bf16[768,128]{1,0:T(8,128)(2,1)S(1)} %regroup.1.refs_0_), channel_id=1, source_target_pairs={{0,1},{1,0},{2,3},{3,2},{4,5},{5,4},{6,7},{7,6},{8,9},{9,8},{10,11... | collective-permute-start | bytes 589832 | tf_op jit(solution)/shard_map/ppermute | solution.py:388
  18.8 9.6 %collective-permute-start.2 = (bf16[768,128]{1,0:T(8,128)(2,1)S(1)}, bf16[768,128]{1,0:T(8,128)(2,1)S(1)}, u32[]{:S(2)}, u32[]{:S(2)}) collective-permute-start(bf16[768,128]{1,0:T(8,128)(2,1)S(1)} %regroup.1.refs_0_), channel_id=1, source_target_pairs={{0,2},{1,3},{2,4},{3,5},{4,6},{5,7},{6,0},{7,1},{8,10},{9,11},{10,... | collective-permute-start | bytes 589832 | tf_op jit(solution)/shard_map/ppermute | solution.py:385
  20.8 11.1 %collective-permute-start.3 = (bf16[768,128]{1,0:T(8,128)(2,1)S(1)}, bf16[768,128]{1,0:T(8,128)(2,1)S(1)}, u32[]{:S(2)}, u32[]{:S(2)}) collective-permute-start(bf16[768,128]{1,0:T(8,128)(2,1)S(1)} %regroup.1.refs_0_), channel_id=1, source_target_pairs={{0,6},{1,7},{2,0},{3,1},{4,2},{5,3},{6,4},{7,5},{8,14},{9,15},{10,... | collective-permute-start | bytes 589832 | tf_op jit(solution)/shard_map/ppermute | solution.py:385
  23.0 10.8 %collective-permute-start.4 = (bf16[768,128]{1,0:T(8,128)(2,1)S(1)}, bf16[768,128]{1,0:T(8,128)(2,1)S(1)}, u32[]{:S(2)}, u32[]{:S(2)}) collective-permute-start(bf16[768,128]{1,0:T(8,128)(2,1)S(1)} %regroup.1.refs_0_), channel_id=1, source_target_pairs={{0,4},{1,5},{2,6},{3,7},{4,0},{5,1},{6,2},{7,3},{8,12},{9,13},{10,... | collective-permute-start | bytes 589832 | tf_op jit(solution)/shard_map/ppermute | solution.py:385
  33.8 17.0 %copy-start.1 = (bf16[5,5,25,256]{3,2,1,0:T(8,128)(2,1)S(1)}, bf16[5,5,25,256]{3,2,1,0:T(8,128)(2,1)}, u32[]{:S(2)}) copy-start(bf16[5,5,25,256]{3,2,1,0:T(8,128)(2,1)} %param.24) | copy-start | bytes 960004
  33.9 17.0 %copy-start.3 = (bf16[24,2048]{1,0:T(8,128)(2,1)S(1)}, bf16[24,2048]{1,0:T(8,128)(2,1)}, u32[]{:S(2)}) copy-start(bf16[24,2048]{1,0:T(8,128)(2,1)} %values_ref.1) | copy-start | bytes 294916
  33.9 17.0 %copy-start.4 = (s32[2048]{0:T(1024)S(1)}, s32[2048]{0:T(1024)}, u32[]{:S(2)}) copy-start(s32[2048]{0:T(1024)} %param.18) | copy-start | bytes 24580
  33.9 17.0 %copy-start.5 = (f32[2,2048]{1,0:T(2,128)S(1)}, f32[2,2048]{1,0:T(2,128)}, u32[]{:S(2)}) copy-start(f32[2,2048]{1,0:T(2,128)} %frac_ref.1) | copy-start | bytes 49156
  33.9 17.0 %copy-start.6 = (s32[2048]{0:T(1024)S(1)}, s32[2048]{0:T(1024)}, u32[]{:S(2)}) copy-start(s32[2048]{0:T(1024)} %param.19) | copy-start | bytes 24580
  33.9 17.0 %copy-start.7 = (s32[2048]{0:T(1024)S(1)}, s32[2048]{0:T(1024)}, u32[]{:S(2)}) copy-start(s32[2048]{0:T(1024)} %param.20) | copy-start | bytes 24580
  33.9 17.0 %copy-start.8 = (f32[256]{0:T(256)S(1)}, f32[256]{0:T(256)}, u32[]{:S(2)}) copy-start(f32[256]{0:T(256)} %param.25) | copy-start | bytes 3076
  33.9 17.0 %copy-start.9 = (s32[256]{0:T(256)S(1)}, s32[256]{0:T(256)}, u32[]{:S(2)}) copy-start(s32[256]{0:T(256)} %param.22) | copy-start | bytes 3076
  33.9 1.5 %collective-permute-start.6 = (bf16[768,128]{1,0:T(8,128)(2,1)S(1)}, bf16[768,128]{1,0:T(8,128)(2,1)S(1)}, u32[]{:S(2)}, u32[]{:S(2)}) collective-permute-start(bf16[768,128]{1,0:T(8,128)(2,1)S(1)} %collective-permute-done.2.refs_0_), channel_id=1, source_target_pairs={{0,1},{1,0},{2,3},{3,2},{4,5},{5,4},{6,7},{7,6},{8,9},{9,8},{10,11... | collective-permute-start | bytes 589832 | tf_op jit(solution)/shard_map/ppermute | solution.py:388
  34.0 1.7 %collective-permute-start.7 = (bf16[768,128]{1,0:T(8,128)(2,1)S(1)}, bf16[768,128]{1,0:T(8,128)(2,1)S(1)}, u32[]{:S(2)}, u32[]{:S(2)}) collective-permute-start(bf16[768,128]{1,0:T(8,128)(2,1)S(1)} %collective-permute-done.3.refs_1_), channel_id=1, source_target_pairs={{0,1},{1,0},{2,3},{3,2},{4,5},{5,4},{6,7},{7,6},{8,9},{9,8},{10,11... | collective-permute-start | bytes 589832 | tf_op jit(solution)/shard_map/ppermute | solution.py:388
  34.5 1.5 %collective-permute-start.8 = (bf16[768,128]{1,0:T(8,128)(2,1)S(1)}, bf16[768,128]{1,0:T(8,128)(2,1)S(1)}, u32[]{:S(2)}, u32[]{:S(2)}) collective-permute-start(bf16[768,128]{1,0:T(8,128)(2,1)S(1)} %collective-permute-done.4.refs_2_), channel_id=1, source_target_pairs={{0,1},{1,0},{2,3},{3,2},{4,5},{5,4},{6,7},{7,6},{8,9},{9,8},{10,11... | collective-permute-start | bytes 589832 | tf_op jit(solution)/shard_map/ppermute | solution.py:388
  41.3 9.5 %collective-permute-start.9 = (bf16[720,128]{1,0:T(8,128)(2,1)S(1)}, bf16[720,128]{1,0:T(8,128)(2,1)S(1)}, u32[]{:S(2)}, u32[]{:S(2)}) collective-permute-start(bf16[720,128]{1,0:T(8,128)(2,1)S(1)} %get-tuple-element.218), channel_id=1, source_target_pairs={{0,8},{8,16},{16,24},{24,32},{32,40},{40,48},{48,56},{56,64},{64,7... | collective-permute-start | bytes 552968 | tf_op jit(solution)/shard_map/ppermute | solution.py:568
  52.8 0.9 %copy-start = (bf16[2,720,256]{2,1,0:T(8,128)(2,1)}, bf16[2,720,256]{2,1,0:T(8,128)(2,1)S(1)}, u32[]{:S(2)}) copy-start(bf16[2,720,256]{2,1,0:T(8,128)(2,1)S(1)} %get-tuple-element.400) | copy-start | bytes 2211844

commit v3 on v2

--- a/solution.py
+++ b/solution.py
@@ -14,7 +14,7 @@
 HALF = TQ // 2
 HALF_PAD = 48
 BOX = 256
-EXTRA = 8
+EXTRA = 7
 HEAD = 4
 ROW_CODE = 24
 ROW_LAT = 25
@@ -23,6 +23,8 @@
 PAY = 32
 SLOTS = 8
 LAT_BAND = 32
+SENDS_DOWN = 4
+SENDS_UP = 6
 ROWS_IN = 7
 TALL = 2 * HALF_PAD
 LOG2E = 1.4426950408889634
@@ -78,19 +80,27 @@
     def wide(ref, k):
         return jnp.concatenate([ref[2 * k : 2 * k + 1, :], ref[2 * k + 1 : 2 * k + 2, :]], axis=1)
 
-    table = jnp.broadcast_to(wide(place_ref, 0).astype(F32), (8, BOX)).astype(BF16)
-    ones = jnp.ones((8, BOX), BF16)
-    lines = iota((BOX, BOX), 0)
+    table = jnp.concatenate(
+        [jnp.broadcast_to(place_ref[h : h + 1, :].astype(F32), (128, 128)).T for h in range(2)], axis=0
+    )
+    lines = iota((BOX, 128), 0)
     eight = iota((8, BOX), 0)
-    counts = jnp.zeros((8, BOX), F32)
-    bands, blocks, member = [], [], []
+    sixteen = iota((BANDS, BOX), 0)
+    bands, blocks, member, within = [], [], [], []
     for k in range(chunks):
-        tile_pick = ones_where(lines == wide(tile_ref, k)).astype(BF16)
-        place = jnp.dot(table, tile_pick, preferred_element_type=F32)[0:1].astype(jnp.int32)
-        counts = counts + dot_nt(ones, ones_where(lines == place).astype(BF16))
+        place = [
+            jnp.sum(jnp.where(lines == tile_ref[at : at + 1, :], table, 0.0), axis=0, keepdims=True)
+            for at in (2 * k, 2 * k + 1)
+        ]
+        place = jnp.concatenate(place, axis=1).astype(jnp.int32)
         bands.append(place >> 4)
         blocks.append(place & 15)
-        member.append(ones_where(iota((BANDS, BOX), 0) == bands[k]))
+        member.append(ones_where(sixteen == bands[k]))
+        within.append(ones_where(sixteen == blocks[k]).astype(BF16))
+    counts = dot_nt(jnp.concatenate(member, axis=1).astype(BF16), jnp.concatenate(within, axis=1))
+    spread = ones_where((iota((BANDS, BOX), 1) & 15) == sixteen).astype(BF16)
+    counts = jnp.dot(counts.astype(BF16), spread, preferred_element_type=F32)
+    counts = jnp.sum(jnp.where((iota((BANDS, BOX), 1) >> 4) == sixteen, counts, 0.0), axis=0, keepdims=True)
     rank = ranks(member)
     for k in range(chunks):
         lanes = slice(k * BOX, (k + 1) * BOX)
@@ -105,7 +115,7 @@
     line_of = iota((PAY, BOX), 0)
     for g in range(BANDS):
         rows = slice(g * PAY, (g + 1) * PAY)
-        out_ref[rows, :] = jnp.where(line_of == ROW_NOTE, counts[0:1], packed[rows]).astype(BF16)
+        out_ref[rows, :] = jnp.where(line_of == ROW_NOTE, counts, packed[rows]).astype(BF16)
 
 
 def regroup_kernel(in_ref, out_ref, left_ref, right_ref):
@@ -141,8 +151,13 @@
         over = jnp.sum(member[k] * first_wide, axis=0, keepdims=True).astype(jnp.int32)
         group = jnp.where(place < 128, codes[k], BANDS - 1 + over + (place >> 7))
         group = jnp.where(codes[k] < 0, -1, group)
-        bucket(payload, group, place & 127, left_ref, right_ref, k)
-    moved = dot_nt(left_ref[...], right_ref[...])
+        bucket(payload, group >> 1, (place & 127) + ((group & 1) << 7), left_ref, right_ref, k)
+    both = dot_nt(left_ref[...], right_ref[...])
+
+    def moved(group):
+        rows = slice((group >> 1) * PAY, (group >> 1) * PAY + PAY)
+        return both[rows, 0:128] if group % 2 == 0 else both[rows, 128:256]
+
 
     note = jnp.concatenate(notes, axis=0)
     of_band = ones_where((iota((BOX, 128), 0) >> 4) == iota((BOX, 128), 1)).astype(BF16)
@@ -157,29 +172,51 @@
     over = jnp.where((band_most > BOX - 1) | (more_most > EXTRA), 1.0, 0.0)
 
     narrow = iota((PAY, 128), 0)
-    out_ref[0:PAY, :] = jnp.where(narrow == ROW_NOTE, over, moved[0:PAY]).astype(BF16)
-    out_ref[PAY : BANDS * PAY, :] = moved[PAY : BANDS * PAY].astype(BF16)
+    out_ref[0:PAY, :] = jnp.where(narrow == ROW_NOTE, over, moved(0)).astype(BF16)
+    for g in range(1, BANDS):
+        out_ref[g * PAY : (g + 1) * PAY, :] = moved(g).astype(BF16)
     block_code = iota((BANDS, 128), 0).astype(F32) + 1.0
     for e in range(EXTRA):
         rows = slice((BANDS + e) * PAY, (BANDS + e + 1) * PAY)
         code = jnp.where((first <= e) & (last > e), block_code, 0.0)
         code = jnp.sum(code, axis=0, keepdims=True)
-        out_ref[rows, :] = jnp.where(narrow == ROW_NOTE, code, moved[rows]).astype(BF16)
-
-
-def sums_kernel(count, last, scale_ref, *refs):
+        out_ref[rows, :] = jnp.where(narrow == ROW_NOTE, code, moved(BANDS + e)).astype(BF16)
+
+
+def sums_kernel(count, kind, scale_ref, *refs):
+    shard = lax.axis_index("obs")
+    if kind.startswith("edge"):
+
+        @pl.when((shard == SENDS_DOWN) | (shard == SENDS_UP))
+        def _():
+            sums_work(count, kind, shard, scale_ref, *refs)
+
+    else:
+        sums_work(count, kind, shard, scale_ref, *refs)
+
+
+def sums_work(count, kind, shard, scale_ref, *refs):
+    last = kind == "last"
     block_refs, refs = refs[:count], refs[count:]
     if last:
-        *before_refs, feature_ref, edge_ref, over_ref = refs[:-7]
+        *before_refs, feature_ref, over_ref = refs[:-7]
         left_ref, right_ref, codes_ref, codes_smem, sem, sums_ref, wide_ref = refs[-7:]
+    elif kind == "edge":
+        before_ref, edge_ref, left_ref, right_ref, codes_ref, codes_smem, sem, sums_ref, wide_ref = refs
+    elif kind == "edge_part":
+        sums_ref, left_ref, right_ref, codes_ref, codes_smem, sem = refs
     else:
         sums_ref, over_ref, left_ref, right_ref, codes_ref, codes_smem, sem = refs
-    shard = lax.axis_index("obs")
+    wide = sums_ref.shape[1]
+    if kind.startswith("edge"):
+        rows_in, first_row = 2, jnp.where(shard == SENDS_DOWN, LAT_BAND - 2, 0)
+    else:
+        rows_in, first_row = ROWS_IN, shard * ROWS_DEV - 2
     scale = jnp.full((8, 128), 1.0, F32)
     lat_scale = (-0.5 * LOG2E) / (scale * scale_ref[0] * scale_ref[0])
     lon_scale = (-0.5 * LOG2E) / (scale * scale_ref[1] * scale_ref[1])
     lat_scale, lon_scale = lat_scale[0:1], lon_scale[0:1]
-    row_mid = ((iota((8, 128), 0) + (shard * ROWS_DEV - 2)) & (LAT_BAND - 1)).astype(F32) + 0.5
+    row_mid = ((iota((8, 128), 0) + first_row) & (LAT_BAND - 1)).astype(F32) + 0.5
     line = iota((2 * HALF_PAD, 128), 0)
     past = (line >= HALF_PAD).astype(jnp.int32)
     col_mid = (2 * (line - HALF_PAD * past) + past).astype(F32) + 0.5
@@ -207,13 +244,13 @@
             lat_weight = jnp.exp2(lat_diff * lat_diff * lat_scale)
             lon_diff = col_mid - lon_at
             lon_weight = jnp.exp2(lon_diff * lon_diff * lon_scale)
-            for r in range(ROWS_IN):
+            for r in range(rows_in):
                 left_ref[slot, r * PAY : (r + 1) * PAY, lanes] = (value * lat_weight[r : r + 1]).astype(BF16)
             right_ref[slot, :, lanes] = lon_weight.astype(BF16)
 
     slots = left_ref.shape[0]
     for slot in range(slots):
-        left_ref[slot, ROWS_IN * PAY :, :] = jnp.zeros((PAY, count * 128), BF16)
+        left_ref[slot, rows_in * PAY :, :] = jnp.zeros((wide - rows_in * PAY, count * 128), BF16)
 
     def main(p, carry):
         for slot in range(slots):
@@ -223,7 +260,7 @@
             sums_ref[pl.ds(start, TALL), :] = dot_nt(right_ref[slot], left_ref[slot])
         return carry
 
-    sums_ref[0:TALL, :] = jnp.zeros((TALL, 256), F32)
+    sums_ref[0:TALL, :] = jnp.zeros((TALL, wide), F32)
     lax.fori_loop(0, BANDS // slots, main, 0)
 
     copy.wait()
@@ -250,6 +287,26 @@
 
     lax.fori_loop(0, used, extra, 0)
 
+    channel = iota((TALL, 128), 1) & (PAY - 1)
+    dense = iota((TALL, 128), 1) - channel + ROW_CODE
+
+    def feature_of(total):
+        density = jnp.take_along_axis(total, dense, axis=1)
+        feature = total * (1.0 / jnp.maximum(density, 1.0))
+        return jnp.where(channel < 24, feature, jnp.where(channel == 24, jnp.log(1.0 + density), 0.0))
+
+    if kind == "edge_part":
+        return
+    if kind == "edge":
+        for block in range(BANDS):
+            rows = slice(block * HALF, (block + 1) * HALF)
+            at = slice((block + 1) * TALL, (block + 2) * TALL)
+            feature = feature_of(sums_ref[at, :] + before_ref[at, :])
+            wide_ref[rows, 0:64] = feature[0:HALF, 0:64]
+            wide_ref[rows, 64:128] = feature[HALF_PAD : HALF_PAD + HALF, 0:64]
+        edge_ref[...] = wide_ref[...].astype(BF16)
+        return
+
     over = block_refs[0][16:PAY, :].astype(F32)[15:16]
     for k in range(1, count):
         over = jnp.maximum(over, block_refs[k][16:PAY, :].astype(F32)[15:16])
@@ -262,8 +319,6 @@
         over = jnp.maximum(over, ref[...])
     over_ref[...] = over
 
-    channel = iota((TALL, 128), 1) & (PAY - 1)
-    dense = iota((TALL, 128), 1) - channel + ROW_CODE
     for block in range(BANDS):
         rows = slice(block * HALF, (block + 1) * HALF)
         at = slice((block + 1) * TALL, (block + 2) * TALL)
@@ -272,20 +327,10 @@
             total = sums_ref[at, lanes]
             for ref in sums_before:
                 total = total + ref[at, lanes]
-            density = jnp.take_along_axis(total, dense, axis=1)
-            feature = total * (1.0 / jnp.maximum(density, 1.0))
-            feature = jnp.where(channel < 24, feature, jnp.where(channel == 24, jnp.log(1.0 + density), 0.0))
+            feature = feature_of(total)
             wide_ref[rows, lanes] = feature[0:HALF]
             wide_ref[rows, 256 + half * 128 : 256 + (half + 1) * 128] = feature[HALF_PAD : HALF_PAD + HALF]
     feature_ref[...] = wide_ref[...].astype(BF16)
-
-    @pl.when(shard == 0)
-    def _():
-        edge_ref[...] = jnp.concatenate([wide_ref[:, 0:64], wide_ref[:, 256:320]], axis=1).astype(BF16)
-
-    @pl.when(shard != 0)
-    def _():
-        edge_ref[...] = jnp.concatenate([wide_ref[:, 192:256], wide_ref[:, 448:512]], axis=1).astype(BF16)
 
 
 def conv_kernel(feature_ref, edge_ref, weight_ref, bias_ref, out_ref, wide_ref, w_ref):
@@ -371,8 +416,8 @@
         in_specs=[vmem()],
         out_specs=vmem(),
         scratch_shapes=[
-            pltpu.VMEM((groups * PAY, BANDS * BOX), BF16),
-            pltpu.VMEM((128, BANDS * BOX), BF16),
+            pltpu.VMEM(((groups + 1) // 2 * PAY, BANDS * BOX), BF16),
+            pltpu.VMEM((BOX, BANDS * BOX), BF16),
         ],
         compiler_params=params(32),
         name="regroup",
@@ -390,30 +435,30 @@
     columns = LON // 2
     shape = jax.ShapeDtypeStruct
 
-    def sums(blocks, before):
-        last = before is not None
+    def sums(kind, blocks, before=()):
         tall = TALL * (BANDS + 1)
-        if last:
-            out_shape = (
-                shape((columns, 512), BF16),
-                shape((columns, 128), BF16),
-                shape((8, 128), F32),
-            )
-        else:
-            out_shape = (shape((tall, 256), F32), shape((8, 128), F32))
-            before = ()
+        wide = 128 if kind.startswith("edge") else 256
         slots = SLOTS
         scratch = [
-            pltpu.VMEM((slots, 256, len(blocks) * 128), BF16),
+            pltpu.VMEM((slots, wide, len(blocks) * 128), BF16),
             pltpu.VMEM((slots, TALL, len(blocks) * 128), BF16),
             pltpu.VMEM((8, 128), jnp.int32),
             pltpu.SMEM((8, 128), jnp.int32),
             pltpu.SemaphoreType.DMA,
         ]
-        if last:
-            scratch += [pltpu.VMEM((tall, 256), F32), pltpu.VMEM((columns, 512), F32)]
+        over = shape((8, 128), F32)
+        if kind == "part":
+            out_shape = (shape((tall, wide), F32), over)
+        elif kind == "edge_part":
+            out_shape = (shape((tall, wide), F32),)
+        elif kind == "edge":
+            out_shape = (shape((columns, 128), BF16),)
+            scratch += [pltpu.VMEM((tall, wide), F32), pltpu.VMEM((columns, 128), F32)]
+        else:
+            out_shape = (shape((columns, 512), BF16), over)
+            scratch += [pltpu.VMEM((tall, wide), F32), pltpu.VMEM((columns, 512), F32)]
         return pl.pallas_call(
-            functools.partial(sums_kernel, len(blocks), last),
+            functools.partial(sums_kernel, len(blocks), kind),
             out_shape=out_shape,
             in_specs=[pl.BlockSpec(memory_space=pltpu.SMEM)] + [vmem()] * (len(blocks) + len(before)),
             out_specs=(vmem(),) * len(out_shape),
@@ -422,14 +467,23 @@
             cost_estimate=pl.CostEstimate(
                 flops=len(blocks) * 1_200_000_000, bytes_accessed=len(blocks) * 200_000, transcendentals=0
             ),
-            name="sums_last" if last else "sums",
+            name=kind + "_sums",
         )(scale, *blocks, *before)
 
     far, after, ahead = (along(own, steps) for steps in (2, 1, -1))
-    before = sums([own, across(own)], None)
+    near = [own, across(own)]
+    before = [*sums("part", near), *sums("edge_part", near)]
     after, ahead, far, *before = lax.optimization_barrier((after, ahead, far, *before))
-    there = [across(value) for value in (after, ahead, far)]
-    return sums([after, ahead, far, *there], before)
+    there = [after, ahead, far] + [across(value) for value in (after, ahead, far)]
+    *before, edge_before = before
+    (edge,) = sums("edge", there, [edge_before])
+    edge, *there = lax.optimization_barrier((edge, *there))
+    bands = lax.axis_size("band")
+    down = [(band * count + SENDS_DOWN, (band + 1) * count) for band in range(bands - 1)]
+    up = [(band * count + SENDS_UP, band * count - 1) for band in range(1, bands)]
+    edge = lax.ppermute(edge, ("band", "obs"), down + up)
+    feature, over = sums("last", there, before)
+    return feature, edge, over
 
 
 def from_behind(value, axis, steps):
@@ -562,11 +616,6 @@
 
 def body(*args):
     feature, edge, over = fast_features(*args[:7])
-    bands, shards = lax.axis_size("band"), lax.axis_size("obs")
-    down = [(band * shards, (band + 1) * shards) for band in range(bands - 1)]
-    up = [(band * shards + shards - 1, band * shards - 1) for band in range(1, bands)]
-    edge = lax.ppermute(edge, ("band", "obs"), down + up)
-
     def finish(feature, edge, *args):
         *_, conv_weight, conv_bias = args
         columns = LON // 2

time: 53.7 us -> 50.7 us (0.944)
  waiting for transfers between devices: 14.7 us -> 11.7 us
  starting transfers between devices: 8.71 us -> 8 us
    ppermute x1, waiting for transfers between devices: 6.39 us -> 4.27 us  [fast_features(): edge = lax.ppermute(edge, ('band', 'obs'), down + up)]
    pallas_call x2 -> x4, Pallas kernels: 7.47 us -> 8.49 us  [sums(): pl.pallas_call(functools.partial(sums_kernel, len(blocks), kind), out_sha...]
    ppermute x3, waiting for transfers between devices: 6.86 us -> 5.93 us  [along(): return lax.ppermute(value, 'obs', order)]
    pallas_call x1, Pallas kernels: 2.18 us -> 1.39 us  [fast_features(): pl.pallas_call(regroup_kernel, out_shape=jax.ShapeDtypeStruct((groups * P...]
    ppermute x1, starting transfers between devices: 1.97 us -> 1.42 us  [fast_features(): edge = lax.ppermute(edge, ('band', 'obs'), down + up)]
  transfers between devices with their start and end apart: 8 -> 8, of which waited for: 7 -> 7; matrix products, arithmetic and copies ran while one was open for 1% -> 1% of each run, Pallas kernels for 4% -> 16%
where the time goes in v3:
time: 50.7 us; the launch traced here: 50.5 us
  blocking collectives  14.2 us (28%)
  Pallas kernels  14 us (28%)
  waiting for transfers between devices  11.7 us (23%)
  starting transfers between devices  8 us (16%)
  local copies, waits for them, and re-layouts  1.43 us (3%)
  between operations  0.85 us (2%)
    all_to_all x1, blocking collectives, fast_features(): came = lax.all_to_all(sent, 'band', split_axis=0, concat_axis=0, tiled=True)  14.2 us
    pallas_call x4, Pallas kernels, sums(): pl.pallas_call(functools.partial(sums_kernel, len(blocks), kind), out_sha...  8.49 us
    ppermute x3, starting transfers between devices, along(): return lax.ppermute(value, 'obs', order)  5.97 us
    ppermute x3, waiting for transfers between devices, along(): return lax.ppermute(value, 'obs', order)  5.93 us
    ppermute x1, waiting for transfers between devices, fast_features(): edge = lax.ppermute(edge, ('band', 'obs'), down + up)  4.27 us
    pallas_call x1, Pallas kernels, fast_features(): pl.pallas_call(pack_kernel, out_shape=jax.ShapeDtypeStruct((BANDS * PAY,...  2.46 us
    pallas_call x1, Pallas kernels, finish(): pl.pallas_call(conv_kernel, out_shape=jax.ShapeDtypeStruct((2, columns, 2...  1.66 us
    ppermute x4, waiting for transfers between devices, across(): return lax.ppermute(value, 'obs', [(s, s ^ 1) for s in range(count)])  1.46 us
  transfers between devices with their start and end apart: 8, of which 7 were waited for; matrix products, arithmetic and copies ran while one was open for 1% of the time, Pallas kernels for 16%

profile of v3, /device:TPU:8, one launch (start us, length us, event | category | flops | bytes accessed | tf_op | source)
XLA Modules:
  0.0 50.5 jit_solution(15364873572488035764)
XLA Ops:
  0.0 2.5 %pack.1 = bf16[512,256]{1,0:T(8,128)(2,1)S(1)} custom-call(bf16[24,2048]{1,0:T(8,128)(2,1)} %values_ref.1, s32[16,128]{1,0:T(8,128)} %bitcast.90, s32[16,128]{1,0:T(8,128)} %bitcast.95, s32[16,128]{1,0:T(8,128)} %bitcast.96, f32[2,2048]{1,0:T(2,128)} %frac_ref.1, s32[2,128]{1,0:T(2,128)} %bitcast.100), custom_call_target="tpu_custom_call" | custom-call | tf_op jit(solution)/shard_map/pack/pallas_call | solution.py:392
  2.5 14.2 %all_to_all.24 = bf16[16,32,256]{2,1,0:T(8,128)(2,1)S(1)} all-to-all(bf16[16,32,256]{2,1,0:T(8,128)(2,1)S(1)} %bitcast.81), channel_id=1, replica_groups=mesh['band'=16,'obs'=8] {'band'}, dimensions={0} | all-to-all | bytes 524288 | tf_op jit(solution)/shard_map/all_to_all | solution.py:411
  16.6 1.4 %regroup.1.refs_0_ = bf16[736,128]{1,0:T(8,128)(2,1)S(1)} custom-call(bf16[512,256]{1,0:T(8,128)(2,1)S(1)} %bitcast.80), custom_call_target="tpu_custom_call" | custom-call | tf_op jit(solution)/shard_map/regroup/pallas_call | solution.py:413
  18.0 0.0 copy-start.10
  18.0 0.1 collective-permute-start.5
  18.1 2.0 %collective-permute-start.2 = (bf16[736,128]{1,0:T(8,128)(2,1)S(1)}, bf16[736,128]{1,0:T(8,128)(2,1)S(1)}, u32[]{:S(2)}, u32[]{:S(2)}) collective-permute-start(bf16[736,128]{1,0:T(8,128)(2,1)S(1)} %regroup.1.refs_0_), channel_id=1, source_target_pairs={{0,2},{1,3},{2,4},{3,5},{4,6},{5,7},{6,0},{7,1},{8,10},{9,11},{10,... | collective-permute-start | bytes 565256 | tf_op jit(solution)/shard_map/ppermute | solution.py:430
  20.1 2.2 %collective-permute-start.3 = (bf16[736,128]{1,0:T(8,128)(2,1)S(1)}, bf16[736,128]{1,0:T(8,128)(2,1)S(1)}, u32[]{:S(2)}, u32[]{:S(2)}) collective-permute-start(bf16[736,128]{1,0:T(8,128)(2,1)S(1)} %regroup.1.refs_0_), channel_id=1, source_target_pairs={{0,6},{1,7},{2,0},{3,1},{4,2},{5,3},{6,4},{7,5},{8,14},{9,15},{10,... | collective-permute-start | bytes 565256 | tf_op jit(solution)/shard_map/ppermute | solution.py:430
  22.3 1.8 %collective-permute-start.4 = (bf16[736,128]{1,0:T(8,128)(2,1)S(1)}, bf16[736,128]{1,0:T(8,128)(2,1)S(1)}, u32[]{:S(2)}, u32[]{:S(2)}) collective-permute-start(bf16[736,128]{1,0:T(8,128)(2,1)S(1)} %regroup.1.refs_0_), channel_id=1, source_target_pairs={{0,4},{1,5},{2,6},{3,7},{4,0},{5,1},{6,2},{7,3},{8,12},{9,13},{10,... | collective-permute-start | bytes 565256 | tf_op jit(solution)/shard_map/ppermute | solution.py:430
  24.1 0.0 collective-permute-done.5.refs_1_
  24.1 2.2 %part_sums.1 = (f32[1632,256]{1,0:T(8,128)S(1)}, f32[8,128]{1,0:T(8,128)S(1)}) custom-call(f32[2]{0:T(128)} %scale_ref.7, bf16[736,128]{1,0:T(8,128)(2,1)S(1)} %regroup.1.refs_0_, bf16[736,128]{1,0:T(8,128)(2,1)S(1)} %collective-permute-done.5.refs_1_), custom_call_target="tpu_custom_call" | custom-call | flops 2400000000 | bytes 400000 | tf_op jit(solution)/shard_map/part_sums/pallas_call | solution.py:460
  26.3 0.0 copy-done.10
  26.3 0.6 %edge_part_sums.1.refs_6_ = f32[1632,128]{1,0:T(8,128)S(1)} custom-call(f32[2]{0:T(128)S(1)} %copy-done.10, bf16[736,128]{1,0:T(8,128)(2,1)S(1)} %regroup.1.refs_0_, bf16[736,128]{1,0:T(8,128)(2,1)S(1)} %collective-permute-done.5.refs_1_), custom_call_target="tpu_custom_call" | custom-call | flops 2400000000 | bytes 400000 | tf_op jit(solution)/shard_map/edge_part_sums/pallas_call | solution.py:460
  26.8 0.7 %collective-permute-done.2.refs_0_ = bf16[736,128]{1,0:T(8,128)(2,1)S(1)} collective-permute-done((bf16[736,128]{1,0:T(8,128)(2,1)S(1)}, bf16[736,128]{1,0:T(8,128)(2,1)S(1)}, u32[]{:S(2)}, u32[]{:S(2)}) %collective-permute-start.2) | collective-permute-done | bytes 188448 | tf_op jit(solution)/shard_map/ppermute | solution.py:430
  27.5 3.3 %collective-permute-done.3.refs_1_ = bf16[736,128]{1,0:T(8,128)(2,1)S(1)} collective-permute-done((bf16[736,128]{1,0:T(8,128)(2,1)S(1)}, bf16[736,128]{1,0:T(8,128)(2,1)S(1)}, u32[]{:S(2)}, u32[]{:S(2)}) %collective-permute-start.3) | collective-permute-done | bytes 188448 | tf_op jit(solution)/shard_map/ppermute | solution.py:430
  30.9 1.9 %collective-permute-done.4.refs_2_ = bf16[736,128]{1,0:T(8,128)(2,1)S(1)} collective-permute-done((bf16[736,128]{1,0:T(8,128)(2,1)S(1)}, bf16[736,128]{1,0:T(8,128)(2,1)S(1)}, u32[]{:S(2)}, u32[]{:S(2)}) %collective-permute-start.4) | collective-permute-done | bytes 188448 | tf_op jit(solution)/shard_map/ppermute | solution.py:430
  32.8 0.0 collective-permute-start.6
  32.8 0.5 %collective-permute-start.7 = (bf16[736,128]{1,0:T(8,128)(2,1)S(1)}, bf16[736,128]{1,0:T(8,128)(2,1)S(1)}, u32[]{:S(2)}, u32[]{:S(2)}) collective-permute-start(bf16[736,128]{1,0:T(8,128)(2,1)S(1)} %collective-permute-done.3.refs_1_), channel_id=1, source_target_pairs={{0,1},{1,0},{2,3},{3,2},{4,5},{5,4},{6,7},{7,6},{8,9},{9,8},{10,11... | collective-permute-start | bytes 565256 | tf_op jit(solution)/shard_map/ppermute | solution.py:433
  33.3 0.0 collective-permute-start.8
  33.3 0.9 %collective-permute-done.6.refs_3_ = bf16[736,128]{1,0:T(8,128)(2,1)S(1)} collective-permute-done((bf16[736,128]{1,0:T(8,128)(2,1)S(1)}, bf16[736,128]{1,0:T(8,128)(2,1)S(1)}, u32[]{:S(2)}, u32[]{:S(2)}) %collective-permute-start.6) | collective-permute-done | bytes 188448 | tf_op jit(solution)/shard_map/ppermute | solution.py:433
  34.2 0.3 collective-permute-done.7.refs_4_
  34.5 0.3 collective-permute-done.8.refs_5_
  34.8 0.6 %edge_sums.1 = bf16[720,128]{1,0:T(8,128)(2,1)S(1)} custom-call(f32[2]{0:T(128)S(1)} %copy-done.10, bf16[736,128]{1,0:T(8,128)(2,1)S(1)} %collective-permute-done.2.refs_0_, bf16[736,128]{1,0:T(8,128)(2,1)S(1)} %collective-permute-done.3.refs_1_, bf16[736,128]{1,0:T(8,128)(2,1)S(1)} %collective-permute-done.4.refs_2_, ...), custom_call_target="tpu_custom_call" | custom-call | flops 7200000000 | bytes 1200000 | tf_op jit(solution)/shard_map/edge_sums/pallas_call | solution.py:460
  35.3 0.0 copy-start.1
  35.3 0.0 copy-start.3
  35.3 0.0 copy-start.4
  35.4 0.0 copy-start.5
  35.4 0.0 copy-start.6
  35.4 0.0 copy-start.7
  35.4 0.0 copy-start.8
  35.4 0.0 copy-start.9
  35.4 1.4 %collective-permute-start.9 = (bf16[720,128]{1,0:T(8,128)(2,1)S(1)}, bf16[720,128]{1,0:T(8,128)(2,1)S(1)}, u32[]{:S(2)}, u32[]{:S(2)}) collective-permute-start(bf16[720,128]{1,0:T(8,128)(2,1)S(1)} %edge_sums.1), channel_id=1, source_target_pairs={{4,8},{12,16},{20,24},{28,32},{36,40},{44,48},{52,56},{60,64},{68,... | collective-permute-start | bytes 552968 | tf_op jit(solution)/shard_map/ppermute | solution.py:484
  36.8 5.2 %last_sums.1 = (bf16[720,512]{1,0:T(8,128)(2,1)S(1)}, f32[8,128]{1,0:T(8,128)S(1)}) custom-call(f32[2]{0:T(128)S(1)} %copy-done.10, bf16[736,128]{1,0:T(8,128)(2,1)S(1)} %collective-permute-done.2.refs_0_, bf16[736,128]{1,0:T(8,128)(2,1)S(1)} %collective-permute-done.3.refs_1_, bf16[736,128]{1,0:T(8,128)(2,1)S(1)} %collective-permute-done.4.refs_2_, ...), custom_call_target="tpu_custom_call" | custom-call | flops 7200000000 | bytes 1200000 | tf_op jit(solution)/shard_map/last_sums/pallas_call | solution.py:460
  42.1 0.5 %slice.89 = f32[1,1]{1,0:T(1,128)} slice(f32[8,128]{1,0:T(8,128)S(1)} %get-tuple-element.230), slice={[0:1], [0:1]} | slice | bytes 8 | tf_op jit(solution)/shard_map/slice | solution.py:638
  43.2 4.3 %collective-permute-done.9 = bf16[720,128]{1,0:T(8,128)(2,1)S(1)} collective-permute-done((bf16[720,128]{1,0:T(8,128)(2,1)S(1)}, bf16[720,128]{1,0:T(8,128)(2,1)S(1)}, u32[]{:S(2)}, u32[]{:S(2)}) %collective-permute-start.9) | collective-permute-done | bytes 184352 | tf_op jit(solution)/shard_map/ppermute | solution.py:484
  47.5 0.0 copy-done.1
  47.5 0.0 copy-done.3
  47.5 0.0 copy-done.4
  47.5 0.0 copy-done.5
  47.5 0.0 copy-done.6
  47.5 0.0 copy-done.7
  47.5 0.0 copy-done.8
  47.5 0.0 copy-done.9
  47.6 2.1 %conditional.1 = (bf16[2,720,256]{2,1,0:T(8,128)(2,1)S(1)}) conditional(s32[]{:T(128)} %bitcast.24, (f32[256]{0:T(256)S(1)}, bf16[720,512]{1,0:T(8,128)(2,1)S(1)}, bf16[720,128]{1,0:T(8,128)(2,1)S(1)}, bf16[5,5,25,256]{3,2,1,0:T(8,128)(2,1)S(1)}) %tuple.80, (s32[2048]{0:T(1024)S(1)}, bf16[24,2048]{1,0:T(8,128)(2,1)S(1)}, s32[2048]{0:T(1024)S(1)}, ...), branch_computations={%region_0.0_spmd, %region_1.13_spmd} | conditional | flops 1663610880 | bytes 172523328 | solution.py:638
  47.6 1.7 %conv.1 = bf16[2,720,256]{2,1,0:T(8,128)(2,1)S(1)} custom-call(bf16[720,512]{1,0:T(8,128)(2,1)S(1)} %get-tuple-element.176.feature_ref, bf16[720,128]{1,0:T(8,128)(2,1)S(1)} %get-tuple-element.177.edge_ref, bf16[5,5,25,256]{3,2,1,0:T(8,128)(2,1)S(1)} %get-tuple-element.178.weight_ref, f32[1,256]{1,0:T(1,128)S(1)} %bitcast.99), custom_call_target="tpu_custom_call" | custom-call | tf_op jit(solution)/shard_map/cond/branch_0_fun/conv/pallas_call | solution.py:622
  49.7 0.0 copy-start
  49.7 0.9 %copy-done = bf16[2,720,256]{2,1,0:T(8,128)(2,1)} copy-done((bf16[2,720,256]{2,1,0:T(8,128)(2,1)}, bf16[2,720,256]{2,1,0:T(8,128)(2,1)S(1)}, u32[]{:S(2)}) %copy-start) | copy-done | bytes 737304
Async XLA Ops:
  18.0 8.2 %copy-start.10 = (f32[2]{0:T(128)S(1)}, f32[2]{0:T(128)}, u32[]{:S(2)}) copy-start(f32[2]{0:T(128)} %scale_ref.7) | copy-start | bytes 28
  18.0 6.1 %collective-permute-start.5 = (bf16[736,128]{1,0:T(8,128)(2,1)S(1)}, bf16[736,128]{1,0:T(8,128)(2,1)S(1)}, u32[]{:S(2)}, u32[]{:S(2)}) collective-permute-start(bf16[736,128]{1,0:T(8,128)(2,1)S(1)} %regroup.1.refs_0_), channel_id=1, source_target_pairs={{0,1},{1,0},{2,3},{3,2},{4,5},{5,4},{6,7},{7,6},{8,9},{9,8},{10,11... | collective-permute-start | bytes 565256 | tf_op jit(solution)/shard_map/ppermute | solution.py:433
  18.1 9.4 %collective-permute-start.2 = (bf16[736,128]{1,0:T(8,128)(2,1)S(1)}, bf16[736,128]{1,0:T(8,128)(2,1)S(1)}, u32[]{:S(2)}, u32[]{:S(2)}) collective-permute-start(bf16[736,128]{1,0:T(8,128)(2,1)S(1)} %regroup.1.refs_0_), channel_id=1, source_target_pairs={{0,2},{1,3},{2,4},{3,5},{4,6},{5,7},{6,0},{7,1},{8,10},{9,11},{10,... | collective-permute-start | bytes 565256 | tf_op jit(solution)/shard_map/ppermute | solution.py:430
  20.1 10.8 %collective-permute-start.3 = (bf16[736,128]{1,0:T(8,128)(2,1)S(1)}, bf16[736,128]{1,0:T(8,128)(2,1)S(1)}, u32[]{:S(2)}, u32[]{:S(2)}) collective-permute-start(bf16[736,128]{1,0:T(8,128)(2,1)S(1)} %regroup.1.refs_0_), channel_id=1, source_target_pairs={{0,6},{1,7},{2,0},{3,1},{4,2},{5,3},{6,4},{7,5},{8,14},{9,15},{10,... | collective-permute-start | bytes 565256 | tf_op jit(solution)/shard_map/ppermute | solution.py:430
  22.3 10.5 %collective-permute-start.4 = (bf16[736,128]{1,0:T(8,128)(2,1)S(1)}, bf16[736,128]{1,0:T(8,128)(2,1)S(1)}, u32[]{:S(2)}, u32[]{:S(2)}) collective-permute-start(bf16[736,128]{1,0:T(8,128)(2,1)S(1)} %regroup.1.refs_0_), channel_id=1, source_target_pairs={{0,4},{1,5},{2,6},{3,7},{4,0},{5,1},{6,2},{7,3},{8,12},{9,13},{10,... | collective-permute-start | bytes 565256 | tf_op jit(solution)/shard_map/ppermute | solution.py:430
  32.8 1.4 %collective-permute-start.6 = (bf16[736,128]{1,0:T(8,128)(2,1)S(1)}, bf16[736,128]{1,0:T(8,128)(2,1)S(1)}, u32[]{:S(2)}, u32[]{:S(2)}) collective-permute-start(bf16[736,128]{1,0:T(8,128)(2,1)S(1)} %collective-permute-done.2.refs_0_), channel_id=1, source_target_pairs={{0,1},{1,0},{2,3},{3,2},{4,5},{5,4},{6,7},{7,6},{8,9},{9,8},{10,11... | collective-permute-start | bytes 565256 | tf_op jit(solution)/shard_map/ppermute | solution.py:433
  32.8 1.7 %collective-permute-start.7 = (bf16[736,128]{1,0:T(8,128)(2,1)S(1)}, bf16[736,128]{1,0:T(8,128)(2,1)S(1)}, u32[]{:S(2)}, u32[]{:S(2)}) collective-permute-start(bf16[736,128]{1,0:T(8,128)(2,1)S(1)} %collective-permute-done.3.refs_1_), channel_id=1, source_target_pairs={{0,1},{1,0},{2,3},{3,2},{4,5},{5,4},{6,7},{7,6},{8,9},{9,8},{10,11... | collective-permute-start | bytes 565256 | tf_op jit(solution)/shard_map/ppermute | solution.py:433
  33.3 1.5 %collective-permute-start.8 = (bf16[736,128]{1,0:T(8,128)(2,1)S(1)}, bf16[736,128]{1,0:T(8,128)(2,1)S(1)}, u32[]{:S(2)}, u32[]{:S(2)}) collective-permute-start(bf16[736,128]{1,0:T(8,128)(2,1)S(1)} %collective-permute-done.4.refs_2_), channel_id=1, source_target_pairs={{0,1},{1,0},{2,3},{3,2},{4,5},{5,4},{6,7},{7,6},{8,9},{9,8},{10,11... | collective-permute-start | bytes 565256 | tf_op jit(solution)/shard_map/ppermute | solution.py:433
  35.3 12.2 %copy-start.1 = (bf16[5,5,25,256]{3,2,1,0:T(8,128)(2,1)S(1)}, bf16[5,5,25,256]{3,2,1,0:T(8,128)(2,1)}, u32[]{:S(2)}) copy-start(bf16[5,5,25,256]{3,2,1,0:T(8,128)(2,1)} %param.24) | copy-start | bytes 960004
  35.3 12.2 %copy-start.3 = (bf16[24,2048]{1,0:T(8,128)(2,1)S(1)}, bf16[24,2048]{1,0:T(8,128)(2,1)}, u32[]{:S(2)}) copy-start(bf16[24,2048]{1,0:T(8,128)(2,1)} %values_ref.1) | copy-start | bytes 294916
  35.3 12.2 %copy-start.4 = (s32[2048]{0:T(1024)S(1)}, s32[2048]{0:T(1024)}, u32[]{:S(2)}) copy-start(s32[2048]{0:T(1024)} %param.18) | copy-start | bytes 24580
  35.4 12.2 %copy-start.5 = (f32[2,2048]{1,0:T(2,128)S(1)}, f32[2,2048]{1,0:T(2,128)}, u32[]{:S(2)}) copy-start(f32[2,2048]{1,0:T(2,128)} %frac_ref.1) | copy-start | bytes 49156
  35.4 12.1 %copy-start.6 = (s32[2048]{0:T(1024)S(1)}, s32[2048]{0:T(1024)}, u32[]{:S(2)}) copy-start(s32[2048]{0:T(1024)} %param.19) | copy-start | bytes 24580
  35.4 12.1 %copy-start.7 = (s32[2048]{0:T(1024)S(1)}, s32[2048]{0:T(1024)}, u32[]{:S(2)}) copy-start(s32[2048]{0:T(1024)} %param.20) | copy-start | bytes 24580
  35.4 12.1 %copy-start.8 = (f32[256]{0:T(256)S(1)}, f32[256]{0:T(256)}, u32[]{:S(2)}) copy-start(f32[256]{0:T(256)} %param.25) | copy-start | bytes 3076
  35.4 12.1 %copy-start.9 = (s32[256]{0:T(256)S(1)}, s32[256]{0:T(256)}, u32[]{:S(2)}) copy-start(s32[256]{0:T(256)} %param.22) | copy-start | bytes 3076
  35.4 12.1 %collective-permute-start.9 = (bf16[720,128]{1,0:T(8,128)(2,1)S(1)}, bf16[720,128]{1,0:T(8,128)(2,1)S(1)}, u32[]{:S(2)}, u32[]{:S(2)}) collective-permute-start(bf16[720,128]{1,0:T(8,128)(2,1)S(1)} %edge_sums.1), channel_id=1, source_target_pairs={{4,8},{12,16},{20,24},{28,32},{36,40},{44,48},{52,56},{60,64},{68,... | collective-permute-start | bytes 552968 | tf_op jit(solution)/shard_map/ppermute | solution.py:484
  49.7 0.9 %copy-start = (bf16[2,720,256]{2,1,0:T(8,128)(2,1)}, bf16[2,720,256]{2,1,0:T(8,128)(2,1)S(1)}, u32[]{:S(2)}) copy-start(bf16[2,720,256]{2,1,0:T(8,128)(2,1)S(1)} %get-tuple-element.414) | copy-start | bytes 2211844

commit v4 on v3

--- a/solution.py
+++ b/solution.py
@@ -23,6 +23,7 @@
 PAY = 32
 SLOTS = 8
 LAT_BAND = 32
+BORDER = 8
 SENDS_DOWN = 4
 SENDS_UP = 6
 ROWS_IN = 7
@@ -333,12 +334,9 @@
     feature_ref[...] = wide_ref[...].astype(BF16)
 
 
-def conv_kernel(feature_ref, edge_ref, weight_ref, bias_ref, out_ref, wide_ref, w_ref):
-    columns = feature_ref.shape[0]
-    shard = lax.axis_index("obs")
+def weights_kernel(weight_ref, w_ref):
     w_ref[...] = jnp.zeros(w_ref.shape, BF16)
-    channels = weight_ref.shape[2]
-    zero = jnp.zeros((PAY - channels, 256), F32)
+    zero = jnp.zeros((PAY - weight_ref.shape[2], 256), F32)
     for shift in range(3):
         for odd in range(2):
             if 2 * shift + odd < 5:
@@ -349,34 +347,70 @@
                         at = odd * 256 + (tap + 2 * out_row) * PAY
                         w_ref[shift, at : at + PAY, out_row * 256 : (out_row + 1) * 256] = part
 
-    border = 8
-    inner = slice(border, border + columns)
+
+def shifted_dots(wide_ref, columns, weights):
+    wide_ref[BORDER - 1 : BORDER, :] = wide_ref[BORDER + columns - 1 : BORDER + columns, :]
+    wide_ref[BORDER + columns : BORDER + columns + 1, :] = wide_ref[BORDER : BORDER + 1, :]
+    total = None
+    for shift in range(3):
+        start = BORDER + shift - 1
+        moved = wide_ref[start : start + columns, :].astype(BF16)
+        part = jnp.dot(moved, weights(shift), preferred_element_type=F32)
+        total = part if total is None else total + part
+    return total
+
+
+def local_conv_kernel(feature_ref, w_ref, bias_ref, part_ref, wide_ref):
+    columns = feature_ref.shape[0]
+    shard = lax.axis_index("obs")
+    inner = slice(BORDER, BORDER + columns)
     wide_ref[inner, :] = feature_ref[...].astype(F32)
+    blank = jnp.zeros((columns, 64), F32)
 
     @pl.when(shard == 0)
     def _():
-        edge = edge_ref[...].astype(F32)
-        wide_ref[inner, 0:64] = edge[:, 0:64]
-        wide_ref[inner, 256:320] = edge[:, 64:128]
+        wide_ref[inner, 0:64] = blank
+        wide_ref[inner, 256:320] = blank
 
     @pl.when(shard == lax.axis_size("obs") - 1)
     def _():
-        edge = edge_ref[...].astype(F32)
-        wide_ref[inner, 192:256] = edge[:, 0:64]
-        wide_ref[inner, 448:512] = edge[:, 64:128]
-
-    wide_ref[border - 1 : border, :] = wide_ref[border + columns - 1 : border + columns, :]
-    wide_ref[border + columns : border + columns + 1, :] = wide_ref[border : border + 1, :]
-
-    total = None
-    for shift in range(3):
-        start = border + shift - 1
-        moved = wide_ref[start : start + columns, :].astype(BF16)
-        part = jnp.dot(moved, w_ref[shift], preferred_element_type=F32)
-        total = part if total is None else total + part
-    bias = bias_ref[...]
-    out_ref[0] = (total[:, 0:256] + bias).astype(BF16)
-    out_ref[1] = (total[:, 256:512] + bias).astype(BF16)
+        wide_ref[inner, 192:256] = blank
+        wide_ref[inner, 448:512] = blank
+
+    bias = jnp.concatenate([bias_ref[...], bias_ref[...]], axis=1)
+    part_ref[...] = shifted_dots(wide_ref, columns, lambda shift: w_ref[shift]) + bias
+
+
+def conv_kernel(part_ref, edge_ref, w_ref, out_ref, wide_ref):
+    columns = part_ref.shape[0]
+    shard = lax.axis_index("obs")
+
+    def finish(at, out_row):
+        wide_ref[BORDER : BORDER + columns, :] = edge_ref[...].astype(F32)
+        lanes = slice(out_row * 256, (out_row + 1) * 256)
+
+        def weights(shift):
+            rows = [w_ref[shift, odd * 256 + at : odd * 256 + at + 64, lanes] for odd in range(2)]
+            return jnp.concatenate(rows, axis=0)
+
+        rest = slice((1 - out_row) * 256, (2 - out_row) * 256)
+        out_ref[1 - out_row] = part_ref[:, rest].astype(BF16)
+        out_ref[out_row] = (part_ref[:, lanes] + shifted_dots(wide_ref, columns, weights)).astype(BF16)
+
+    first, last = shard == 0, shard == lax.axis_size("obs") - 1
+
+    @pl.when(first)
+    def _():
+        finish(0, 0)
+
+    @pl.when(last)
+    def _():
+        finish(192, 1)
+
+    @pl.when(jnp.logical_not(first | last))
+    def _():
+        out_ref[0] = part_ref[:, 0:256].astype(BF16)
+        out_ref[1] = part_ref[:, 256:512].astype(BF16)
 
 
 def params(mib):
@@ -387,7 +421,7 @@
     return pl.BlockSpec(memory_space=pltpu.VMEM)
 
 
-def fast_features(values, tile, row, col, frac, place, scale):
+def fast_features(values, tile, row, col, frac, place, scale, conv_weight):
     arrivals = tile.shape[0]
     sent = pl.pallas_call(
         pack_kernel,
@@ -473,7 +507,17 @@
     far, after, ahead = (along(own, steps) for steps in (2, 1, -1))
     near = [own, across(own)]
     before = [*sums("part", near), *sums("edge_part", near)]
-    after, ahead, far, *before = lax.optimization_barrier((after, ahead, far, *before))
+    conv_weight, *before = lax.optimization_barrier((conv_weight, *before))
+    w = pl.pallas_call(
+        weights_kernel,
+        out_shape=shape((3, 512, 512), BF16),
+        in_specs=[vmem()],
+        out_specs=vmem(),
+        compiler_params=params(32),
+        cost_estimate=pl.CostEstimate(flops=1_000_000_000, bytes_accessed=2_000_000, transcendentals=0),
+        name="weights",
+    )(conv_weight)
+    after, ahead, far, w, *before = lax.optimization_barrier((after, ahead, far, w, *before))
     there = [after, ahead, far] + [across(value) for value in (after, ahead, far)]
     *before, edge_before = before
     (edge,) = sums("edge", there, [edge_before])
@@ -483,7 +527,7 @@
     up = [(band * count + SENDS_UP, band * count - 1) for band in range(1, bands)]
     edge = lax.ppermute(edge, ("band", "obs"), down + up)
     feature, over = sums("last", there, before)
-    return feature, edge, over
+    return feature, edge, over, w
 
 
 def from_behind(value, axis, steps):
@@ -615,27 +659,36 @@
 
 
 def body(*args):
-    feature, edge, over = fast_features(*args[:7])
-    def finish(feature, edge, *args):
-        *_, conv_weight, conv_bias = args
-        columns = LON // 2
+    *_, conv_weight, conv_bias = args
+    feature, edge, over, w = fast_features(*args[:8])
+    columns = LON // 2
+    part = pl.pallas_call(
+        local_conv_kernel,
+        out_shape=jax.ShapeDtypeStruct((columns, 512), F32),
+        in_specs=[vmem()] * 3,
+        out_specs=vmem(),
+        scratch_shapes=[pltpu.VMEM((columns + 16, 512), F32)],
+        compiler_params=params(32),
+        cost_estimate=pl.CostEstimate(flops=2_000_000_000, bytes_accessed=4_000_000, transcendentals=0),
+        name="local_conv",
+    )(feature, w, conv_bias.reshape(1, -1))
+    edge, part = lax.optimization_barrier((edge, part))
+
+    def finish(part, edge, w, *args):
         return pl.pallas_call(
             conv_kernel,
             out_shape=jax.ShapeDtypeStruct((2, columns, 256), BF16),
-            in_specs=[vmem()] * 4,
+            in_specs=[vmem()] * 3,
             out_specs=vmem(),
-            scratch_shapes=[
-                pltpu.VMEM((columns + 16, 512), F32),
-                pltpu.VMEM((3, 512, 512), BF16),
-            ],
+            scratch_shapes=[pltpu.VMEM((columns + 16, 128), F32)],
             compiler_params=params(32),
             name="conv",
-        )(feature, edge, conv_weight, conv_bias.reshape(1, -1))
-
-    def whole(feature, edge, *args):
+        )(part, edge, w)
+
+    def whole(part, edge, w, *args):
         return general(*args)
 
-    return lax.cond(over[0, 0] > 0.0, whole, finish, feature, edge, *args)
+    return lax.cond(over[0, 0] > 0.0, whole, finish, part, edge, w, *args)
 
 
 def solution(mesh):

time: 50.7 us -> 49.2 us (0.970)
  waiting for transfers between devices: 11.7 us -> 9.36 us
  Pallas kernels: 14 us -> 14.6 us
    pallas_call x0 -> x2, Pallas kernels: none -> 1.77 us  [the longest x1 1.67 us: body(): pl.pallas_call(local_conv_kernel, out_shape=jax.ShapeDtypeStruct((columns...]
    ppermute x1, waiting for transfers between devices: 4.27 us -> 2.51 us  [fast_features(): edge = lax.ppermute(edge, ('band', 'obs'), down + up)]
    pallas_call x1, Pallas kernels: 1.66 us -> 0.52 us  [finish(): pl.pallas_call(conv_kernel, out_shape=jax.ShapeDtypeStruct((2, columns, 2...]
    ppermute x3, waiting for transfers between devices: 5.93 us -> 5.39 us  [along(): return lax.ppermute(value, 'obs', order)]
  transfers between devices with their start and end apart: 8 -> 8, of which waited for: 7 -> 7; matrix products, arithmetic and copies ran while one was open for 1% -> 1% of each run, Pallas kernels for 16% -> 20%
where the time goes in v4:
time: 49.2 us; the launch traced here: 49 us
  Pallas kernels  14.6 us (30%)
  blocking collectives  14.2 us (29%)
  waiting for transfers between devices  9.36 us (19%)
  starting transfers between devices  7.86 us (16%)
  local copies, waits for them, and re-layouts  1.85 us (4%)
  between operations  0.85 us (2%)
    all_to_all x1, blocking collectives, fast_features(): came = lax.all_to_all(sent, 'band', split_axis=0, concat_axis=0, tiled=True)  14.2 us
    pallas_call x4, Pallas kernels, sums(): pl.pallas_call(functools.partial(sums_kernel, len(blocks), kind), out_sha...  8.49 us
    ppermute x3, starting transfers between devices, along(): return lax.ppermute(value, 'obs', order)  5.97 us
    ppermute x3, waiting for transfers between devices, along(): return lax.ppermute(value, 'obs', order)  5.39 us
    ppermute x1, waiting for transfers between devices, fast_features(): edge = lax.ppermute(edge, ('band', 'obs'), down + up)  2.51 us
    pallas_call x1, Pallas kernels, fast_features(): pl.pallas_call(pack_kernel, out_shape=jax.ShapeDtypeStruct((BANDS * PAY,...  2.46 us
    pallas_call x1, Pallas kernels, body(): pl.pallas_call(local_conv_kernel, out_shape=jax.ShapeDtypeStruct((columns...  1.67 us
    ppermute x4, waiting for transfers between devices, across(): return lax.ppermute(value, 'obs', [(s, s ^ 1) for s in range(count)])  1.46 us
  transfers between devices with their start and end apart: 8, of which 7 were waited for; matrix products, arithmetic and copies ran while one was open for 1% of the time, Pallas kernels for 20%

profile of v4, /device:TPU:8, one launch (start us, length us, event | category | flops | bytes accessed | tf_op | source)
XLA Modules:
  0.0 49.0 jit_solution(3384586673047220547)
XLA Ops:
  0.0 2.5 %pack.1 = bf16[512,256]{1,0:T(8,128)(2,1)S(1)} custom-call(bf16[24,2048]{1,0:T(8,128)(2,1)} %values_ref.1, s32[16,128]{1,0:T(8,128)} %bitcast.90, s32[16,128]{1,0:T(8,128)} %bitcast.95, s32[16,128]{1,0:T(8,128)} %bitcast.96, f32[2,2048]{1,0:T(2,128)} %frac_ref.1, s32[2,128]{1,0:T(2,128)} %bitcast.99), custom_call_target="tpu_custom_call" | custom-call | tf_op jit(solution)/shard_map/pack/pallas_call | solution.py:426
  2.5 14.2 %all_to_all.24 = bf16[16,32,256]{2,1,0:T(8,128)(2,1)S(1)} all-to-all(bf16[16,32,256]{2,1,0:T(8,128)(2,1)S(1)} %bitcast.81), channel_id=1, replica_groups=mesh['band'=16,'obs'=8] {'band'}, dimensions={0} | all-to-all | bytes 524288 | tf_op jit(solution)/shard_map/all_to_all | solution.py:445
  16.6 1.4 %regroup.1.refs_0_ = bf16[736,128]{1,0:T(8,128)(2,1)S(1)} custom-call(bf16[512,256]{1,0:T(8,128)(2,1)S(1)} %bitcast.80), custom_call_target="tpu_custom_call" | custom-call | tf_op jit(solution)/shard_map/regroup/pallas_call | solution.py:447
  18.0 0.0 copy-start.7
  18.0 0.1 collective-permute-start.5
  18.1 2.0 %collective-permute-start.2 = (bf16[736,128]{1,0:T(8,128)(2,1)S(1)}, bf16[736,128]{1,0:T(8,128)(2,1)S(1)}, u32[]{:S(2)}, u32[]{:S(2)}) collective-permute-start(bf16[736,128]{1,0:T(8,128)(2,1)S(1)} %regroup.1.refs_0_), channel_id=1, source_target_pairs={{0,2},{1,3},{2,4},{3,5},{4,6},{5,7},{6,0},{7,1},{8,10},{9,11},{10,... | collective-permute-start | bytes 565256 | tf_op jit(solution)/shard_map/ppermute | solution.py:464
  20.1 2.2 %collective-permute-start.3 = (bf16[736,128]{1,0:T(8,128)(2,1)S(1)}, bf16[736,128]{1,0:T(8,128)(2,1)S(1)}, u32[]{:S(2)}, u32[]{:S(2)}) collective-permute-start(bf16[736,128]{1,0:T(8,128)(2,1)S(1)} %regroup.1.refs_0_), channel_id=1, source_target_pairs={{0,6},{1,7},{2,0},{3,1},{4,2},{5,3},{6,4},{7,5},{8,14},{9,15},{10,... | collective-permute-start | bytes 565256 | tf_op jit(solution)/shard_map/ppermute | solution.py:464
  22.3 1.8 %collective-permute-start.4 = (bf16[736,128]{1,0:T(8,128)(2,1)S(1)}, bf16[736,128]{1,0:T(8,128)(2,1)S(1)}, u32[]{:S(2)}, u32[]{:S(2)}) collective-permute-start(bf16[736,128]{1,0:T(8,128)(2,1)S(1)} %regroup.1.refs_0_), channel_id=1, source_target_pairs={{0,4},{1,5},{2,6},{3,7},{4,0},{5,1},{6,2},{7,3},{8,12},{9,13},{10,... | collective-permute-start | bytes 565256 | tf_op jit(solution)/shard_map/ppermute | solution.py:464
  24.1 0.0 collective-permute-done.5.refs_1_
  24.1 2.2 %part_sums.1 = (f32[1632,256]{1,0:T(8,128)S(1)}, f32[8,128]{1,0:T(8,128)S(1)}) custom-call(f32[2]{0:T(128)} %scale_ref.7, bf16[736,128]{1,0:T(8,128)(2,1)S(1)} %regroup.1.refs_0_, bf16[736,128]{1,0:T(8,128)(2,1)S(1)} %collective-permute-done.5.refs_1_), custom_call_target="tpu_custom_call" | custom-call | flops 2400000000 | bytes 400000 | tf_op jit(solution)/shard_map/part_sums/pallas_call | solution.py:494
  26.3 0.0 copy-done.7
  26.3 0.0 copy-start.9
  26.3 0.6 %edge_part_sums.1.refs_6_ = f32[1632,128]{1,0:T(8,128)S(1)} custom-call(f32[2]{0:T(128)S(1)} %copy-done.7, bf16[736,128]{1,0:T(8,128)(2,1)S(1)} %regroup.1.refs_0_, bf16[736,128]{1,0:T(8,128)(2,1)S(1)} %collective-permute-done.5.refs_1_), custom_call_target="tpu_custom_call" | custom-call | flops 2400000000 | bytes 400000 | tf_op jit(solution)/shard_map/edge_part_sums/pallas_call | solution.py:494
  26.9 0.4 copy-done.9
  27.3 0.1 weights.1.w_ref
  27.4 0.2 collective-permute-done.2.refs_0_
  27.5 3.3 %collective-permute-done.3.refs_1_ = bf16[736,128]{1,0:T(8,128)(2,1)S(1)} collective-permute-done((bf16[736,128]{1,0:T(8,128)(2,1)S(1)}, bf16[736,128]{1,0:T(8,128)(2,1)S(1)}, u32[]{:S(2)}, u32[]{:S(2)}) %collective-permute-start.3) | collective-permute-done | bytes 188448 | tf_op jit(solution)/shard_map/ppermute | solution.py:464
  30.9 1.9 %collective-permute-done.4.refs_2_ = bf16[736,128]{1,0:T(8,128)(2,1)S(1)} collective-permute-done((bf16[736,128]{1,0:T(8,128)(2,1)S(1)}, bf16[736,128]{1,0:T(8,128)(2,1)S(1)}, u32[]{:S(2)}, u32[]{:S(2)}) %collective-permute-start.4) | collective-permute-done | bytes 188448 | tf_op jit(solution)/shard_map/ppermute | solution.py:464
  32.8 0.0 collective-permute-start.6
  32.8 0.5 %collective-permute-start.7 = (bf16[736,128]{1,0:T(8,128)(2,1)S(1)}, bf16[736,128]{1,0:T(8,128)(2,1)S(1)}, u32[]{:S(2)}, u32[]{:S(2)}) collective-permute-start(bf16[736,128]{1,0:T(8,128)(2,1)S(1)} %collective-permute-done.3.refs_1_), channel_id=1, source_target_pairs={{0,1},{1,0},{2,3},{3,2},{4,5},{5,4},{6,7},{7,6},{8,9},{9,8},{10,11... | collective-permute-start | bytes 565256 | tf_op jit(solution)/shard_map/ppermute | solution.py:467
  33.3 0.0 collective-permute-start.8
  33.3 0.9 %collective-permute-done.6.refs_3_ = bf16[736,128]{1,0:T(8,128)(2,1)S(1)} collective-permute-done((bf16[736,128]{1,0:T(8,128)(2,1)S(1)}, bf16[736,128]{1,0:T(8,128)(2,1)S(1)}, u32[]{:S(2)}, u32[]{:S(2)}) %collective-permute-start.6) | collective-permute-done | bytes 188448 | tf_op jit(solution)/shard_map/ppermute | solution.py:467
  34.2 0.3 collective-permute-done.7.refs_4_
  34.5 0.3 collective-permute-done.8.refs_5_
  34.8 0.6 %edge_sums.1 = bf16[720,128]{1,0:T(8,128)(2,1)S(1)} custom-call(f32[2]{0:T(128)S(1)} %copy-done.7, bf16[736,128]{1,0:T(8,128)(2,1)S(1)} %collective-permute-done.2.refs_0_, bf16[736,128]{1,0:T(8,128)(2,1)S(1)} %collective-permute-done.3.refs_1_, bf16[736,128]{1,0:T(8,128)(2,1)S(1)} %collective-permute-done.4.refs_2_, ...), custom_call_target="tpu_custom_call" | custom-call | flops 7200000000 | bytes 1200000 | tf_op jit(solution)/shard_map/edge_sums/pallas_call | solution.py:494
  35.3 0.0 copy-start.8
  35.3 1.3 %collective-permute-start.9 = (bf16[720,128]{1,0:T(8,128)(2,1)S(1)}, bf16[720,128]{1,0:T(8,128)(2,1)S(1)}, u32[]{:S(2)}, u32[]{:S(2)}) collective-permute-start(bf16[720,128]{1,0:T(8,128)(2,1)S(1)} %edge_sums.1), channel_id=1, source_target_pairs={{4,8},{12,16},{20,24},{28,32},{36,40},{44,48},{52,56},{60,64},{68,... | collective-permute-start | bytes 552968 | tf_op jit(solution)/shard_map/ppermute | solution.py:528
  36.6 5.2 %last_sums.1 = (bf16[720,512]{1,0:T(8,128)(2,1)S(1)}, f32[8,128]{1,0:T(8,128)S(1)}) custom-call(f32[2]{0:T(128)S(1)} %copy-done.7, bf16[736,128]{1,0:T(8,128)(2,1)S(1)} %collective-permute-done.2.refs_0_, bf16[736,128]{1,0:T(8,128)(2,1)S(1)} %collective-permute-done.3.refs_1_, bf16[736,128]{1,0:T(8,128)(2,1)S(1)} %collective-permute-done.4.refs_2_, ...), custom_call_target="tpu_custom_call" | custom-call | flops 7200000000 | bytes 1200000 | tf_op jit(solution)/shard_map/last_sums/pallas_call | solution.py:494
  41.8 0.0 copy-start.1
  41.9 0.0 copy-start.2
  41.9 0.0 copy-start.3
  41.9 0.0 copy-start.4
  41.9 0.0 copy-start.5
  41.9 0.0 copy-start.6
  41.9 0.5 %slice.89 = f32[1,1]{1,0:T(1,128)} slice(f32[8,128]{1,0:T(8,128)S(1)} %get-tuple-element.238), slice={[0:1], [0:1]} | slice | bytes 8 | tf_op jit(solution)/shard_map/slice | solution.py:691
  43.1 0.0 copy-done.8
  43.1 1.7 %local_conv.1 = f32[720,512]{1,0:T(8,128)S(1)} custom-call(bf16[720,512]{1,0:T(8,128)(2,1)S(1)} %get-tuple-element.240.feature_ref, bf16[3,512,512]{2,1,0:T(8,128)(2,1)S(1)} %weights.1.w_ref, f32[1,256]{1,0:T(1,128)S(1)} %bitcast.100), custom_call_target="tpu_custom_call" | custom-call | flops 2000000000 | bytes 4000000 | tf_op jit(solution)/shard_map/local_conv/pallas_call | solution.py:665
  44.8 2.5 %collective-permute-done.9 = bf16[720,128]{1,0:T(8,128)(2,1)S(1)} collective-permute-done((bf16[720,128]{1,0:T(8,128)(2,1)S(1)}, bf16[720,128]{1,0:T(8,128)(2,1)S(1)}, u32[]{:S(2)}, u32[]{:S(2)}) %collective-permute-start.9) | collective-permute-done | bytes 184352 | tf_op jit(solution)/shard_map/ppermute | solution.py:528
  47.3 0.0 copy-done.1
  47.3 0.0 copy-done.2
  47.3 0.0 copy-done.3
  47.3 0.0 copy-done.4
  47.3 0.0 copy-done.5
  47.3 0.0 copy-done.6
  47.3 0.8 %conditional.1 = (bf16[2,720,256]{2,1,0:T(8,128)(2,1)S(1)}) conditional(s32[]{:T(128)} %bitcast.23, (f32[720,512]{1,0:T(8,128)S(1)}, bf16[720,128]{1,0:T(8,128)(2,1)S(1)}, bf16[3,512,512]{2,1,0:T(8,128)(2,1)S(1)}) %tuple.38, (s32[2048]{0:T(1024)S(1)}, bf16[24,2048]{1,0:T(8,128)(2,1)S(1)}, s32[2048]{0:T(1024)S(1)}, f32[2,2048]{1,0:T(2,128)S(1)}, ...), branch_computations={%region_0.0_spmd, %region_1.13_spmd} | conditional | flops 1663610880 | bytes 171243296 | solution.py:691
  47.3 0.5 %conv.1 = bf16[2,720,256]{2,1,0:T(8,128)(2,1)S(1)} custom-call(f32[720,512]{1,0:T(8,128)S(1)} %get-tuple-element.174.part_ref, bf16[720,128]{1,0:T(8,128)(2,1)S(1)} %get-tuple-element.175.edge_ref, bf16[3,512,512]{2,1,0:T(8,128)(2,1)S(1)} %get-tuple-element.176.w_ref), custom_call_target="tpu_custom_call" | custom-call | tf_op jit(solution)/shard_map/cond/branch_0_fun/conv/pallas_call | solution.py:678
  48.1 0.0 copy-start
  48.1 0.9 %copy-done = bf16[2,720,256]{2,1,0:T(8,128)(2,1)} copy-done((bf16[2,720,256]{2,1,0:T(8,128)(2,1)}, bf16[2,720,256]{2,1,0:T(8,128)(2,1)S(1)}, u32[]{:S(2)}) %copy-start) | copy-done | bytes 737304
Async XLA Ops:
  18.0 8.2 %copy-start.7 = (f32[2]{0:T(128)S(1)}, f32[2]{0:T(128)}, u32[]{:S(2)}) copy-start(f32[2]{0:T(128)} %scale_ref.7) | copy-start | bytes 28
  18.0 6.1 %collective-permute-start.5 = (bf16[736,128]{1,0:T(8,128)(2,1)S(1)}, bf16[736,128]{1,0:T(8,128)(2,1)S(1)}, u32[]{:S(2)}, u32[]{:S(2)}) collective-permute-start(bf16[736,128]{1,0:T(8,128)(2,1)S(1)} %regroup.1.refs_0_), channel_id=1, source_target_pairs={{0,1},{1,0},{2,3},{3,2},{4,5},{5,4},{6,7},{7,6},{8,9},{9,8},{10,11... | collective-permute-start | bytes 565256 | tf_op jit(solution)/shard_map/ppermute | solution.py:467
  18.1 9.4 %collective-permute-start.2 = (bf16[736,128]{1,0:T(8,128)(2,1)S(1)}, bf16[736,128]{1,0:T(8,128)(2,1)S(1)}, u32[]{:S(2)}, u32[]{:S(2)}) collective-permute-start(bf16[736,128]{1,0:T(8,128)(2,1)S(1)} %regroup.1.refs_0_), channel_id=1, source_target_pairs={{0,2},{1,3},{2,4},{3,5},{4,6},{5,7},{6,0},{7,1},{8,10},{9,11},{10,... | collective-permute-start | bytes 565256 | tf_op jit(solution)/shard_map/ppermute | solution.py:464
  20.1 10.8 %collective-permute-start.3 = (bf16[736,128]{1,0:T(8,128)(2,1)S(1)}, bf16[736,128]{1,0:T(8,128)(2,1)S(1)}, u32[]{:S(2)}, u32[]{:S(2)}) collective-permute-start(bf16[736,128]{1,0:T(8,128)(2,1)S(1)} %regroup.1.refs_0_), channel_id=1, source_target_pairs={{0,6},{1,7},{2,0},{3,1},{4,2},{5,3},{6,4},{7,5},{8,14},{9,15},{10,... | collective-permute-start | bytes 565256 | tf_op jit(solution)/shard_map/ppermute | solution.py:464
  22.3 10.5 %collective-permute-start.4 = (bf16[736,128]{1,0:T(8,128)(2,1)S(1)}, bf16[736,128]{1,0:T(8,128)(2,1)S(1)}, u32[]{:S(2)}, u32[]{:S(2)}) collective-permute-start(bf16[736,128]{1,0:T(8,128)(2,1)S(1)} %regroup.1.refs_0_), channel_id=1, source_target_pairs={{0,4},{1,5},{2,6},{3,7},{4,0},{5,1},{6,2},{7,3},{8,12},{9,13},{10,... | collective-permute-start | bytes 565256 | tf_op jit(solution)/shard_map/ppermute | solution.py:464
  26.3 1.0 %copy-start.9 = (bf16[5,5,25,256]{3,2,1,0:T(8,128)(2,1)S(1)}, bf16[5,5,25,256]{3,2,1,0:T(8,128)(2,1)}, u32[]{:S(2)}) copy-start(bf16[5,5,25,256]{3,2,1,0:T(8,128)(2,1)} %weight_ref) | copy-start | bytes 960004
  32.8 1.4 %collective-permute-start.6 = (bf16[736,128]{1,0:T(8,128)(2,1)S(1)}, bf16[736,128]{1,0:T(8,128)(2,1)S(1)}, u32[]{:S(2)}, u32[]{:S(2)}) collective-permute-start(bf16[736,128]{1,0:T(8,128)(2,1)S(1)} %collective-permute-done.2.refs_0_), channel_id=1, source_target_pairs={{0,1},{1,0},{2,3},{3,2},{4,5},{5,4},{6,7},{7,6},{8,9},{9,8},{10,11... | collective-permute-start | bytes 565256 | tf_op jit(solution)/shard_map/ppermute | solution.py:467
  32.8 1.7 %collective-permute-start.7 = (bf16[736,128]{1,0:T(8,128)(2,1)S(1)}, bf16[736,128]{1,0:T(8,128)(2,1)S(1)}, u32[]{:S(2)}, u32[]{:S(2)}) collective-permute-start(bf16[736,128]{1,0:T(8,128)(2,1)S(1)} %collective-permute-done.3.refs_1_), channel_id=1, source_target_pairs={{0,1},{1,0},{2,3},{3,2},{4,5},{5,4},{6,7},{7,6},{8,9},{9,8},{10,11... | collective-permute-start | bytes 565256 | tf_op jit(solution)/shard_map/ppermute | solution.py:467
  33.3 1.5 %collective-permute-start.8 = (bf16[736,128]{1,0:T(8,128)(2,1)S(1)}, bf16[736,128]{1,0:T(8,128)(2,1)S(1)}, u32[]{:S(2)}, u32[]{:S(2)}) collective-permute-start(bf16[736,128]{1,0:T(8,128)(2,1)S(1)} %collective-permute-done.4.refs_2_), channel_id=1, source_target_pairs={{0,1},{1,0},{2,3},{3,2},{4,5},{5,4},{6,7},{7,6},{8,9},{9,8},{10,11... | collective-permute-start | bytes 565256 | tf_op jit(solution)/shard_map/ppermute | solution.py:467
  35.3 7.8 %copy-start.8 = (f32[256]{0:T(256)S(1)}, f32[256]{0:T(256)}, u32[]{:S(2)}) copy-start(f32[256]{0:T(256)} %param.25) | copy-start | bytes 3076
  35.3 11.9 %collective-permute-start.9 = (bf16[720,128]{1,0:T(8,128)(2,1)S(1)}, bf16[720,128]{1,0:T(8,128)(2,1)S(1)}, u32[]{:S(2)}, u32[]{:S(2)}) collective-permute-start(bf16[720,128]{1,0:T(8,128)(2,1)S(1)} %edge_sums.1), channel_id=1, source_target_pairs={{4,8},{12,16},{20,24},{28,32},{36,40},{44,48},{52,56},{60,64},{68,... | collective-permute-start | bytes 552968 | tf_op jit(solution)/shard_map/ppermute | solution.py:528
  41.8 5.4 %copy-start.1 = (bf16[24,2048]{1,0:T(8,128)(2,1)S(1)}, bf16[24,2048]{1,0:T(8,128)(2,1)}, u32[]{:S(2)}) copy-start(bf16[24,2048]{1,0:T(8,128)(2,1)} %values_ref.1) | copy-start | bytes 294916
  41.9 5.4 %copy-start.2 = (s32[2048]{0:T(1024)S(1)}, s32[2048]{0:T(1024)}, u32[]{:S(2)}) copy-start(s32[2048]{0:T(1024)} %param.18) | copy-start | bytes 24580
  41.9 5.4 %copy-start.3 = (f32[2,2048]{1,0:T(2,128)S(1)}, f32[2,2048]{1,0:T(2,128)}, u32[]{:S(2)}) copy-start(f32[2,2048]{1,0:T(2,128)} %frac_ref.1) | copy-start | bytes 49156
  41.9 5.4 %copy-start.4 = (s32[2048]{0:T(1024)S(1)}, s32[2048]{0:T(1024)}, u32[]{:S(2)}) copy-start(s32[2048]{0:T(1024)} %param.19) | copy-start | bytes 24580
  41.9 5.4 %copy-start.5 = (s32[2048]{0:T(1024)S(1)}, s32[2048]{0:T(1024)}, u32[]{:S(2)}) copy-start(s32[2048]{0:T(1024)} %param.20) | copy-start | bytes 24580
  41.9 5.4 %copy-start.6 = (s32[256]{0:T(256)S(1)}, s32[256]{0:T(256)}, u32[]{:S(2)}) copy-start(s32[256]{0:T(256)} %param.22) | copy-start | bytes 3076
  48.1 0.9 %copy-start = (bf16[2,720,256]{2,1,0:T(8,128)(2,1)}, bf16[2,720,256]{2,1,0:T(8,128)(2,1)S(1)}, u32[]{:S(2)}) copy-start(bf16[2,720,256]{2,1,0:T(8,128)(2,1)S(1)} %get-tuple-element.425) | copy-start | bytes 2211844

commit v5 on v4

--- a/solution.py
+++ b/solution.py
@@ -75,7 +75,11 @@
     return high, middle, rest - middle
 
 
-def pack_kernel(values_ref, tile_ref, row_ref, col_ref, frac_ref, place_ref, out_ref, left_ref, right_ref):
+def pack_kernel(
+    values_ref, tile_ref, row_ref, col_ref, frac_ref, place_ref, scale_ref, out_ref, scales_ref, left_ref, right_ref
+):
+    scale = jnp.where(iota((8, 128), 0) == 0, scale_ref[0], scale_ref[1])
+    scales_ref[...] = (-0.5 * LOG2E) / (scale * scale)
     chunks = tile_ref.shape[0] * 128 // BOX
 
     def wide(ref, k):
@@ -213,10 +217,7 @@
         rows_in, first_row = 2, jnp.where(shard == SENDS_DOWN, LAT_BAND - 2, 0)
     else:
         rows_in, first_row = ROWS_IN, shard * ROWS_DEV - 2
-    scale = jnp.full((8, 128), 1.0, F32)
-    lat_scale = (-0.5 * LOG2E) / (scale * scale_ref[0] * scale_ref[0])
-    lon_scale = (-0.5 * LOG2E) / (scale * scale_ref[1] * scale_ref[1])
-    lat_scale, lon_scale = lat_scale[0:1], lon_scale[0:1]
+    lat_scale, lon_scale = scale_ref[0:1, :], scale_ref[1:2, :]
     row_mid = ((iota((8, 128), 0) + first_row) & (LAT_BAND - 1)).astype(F32) + 0.5
     line = iota((2 * HALF_PAD, 128), 0)
     past = (line >= HALF_PAD).astype(jnp.int32)
@@ -423,11 +424,11 @@
 
 def fast_features(values, tile, row, col, frac, place, scale, conv_weight):
     arrivals = tile.shape[0]
-    sent = pl.pallas_call(
+    sent, scales = pl.pallas_call(
         pack_kernel,
-        out_shape=jax.ShapeDtypeStruct((BANDS * PAY, BOX), BF16),
-        in_specs=[vmem()] * 6,
-        out_specs=vmem(),
+        out_shape=(jax.ShapeDtypeStruct((BANDS * PAY, BOX), BF16), jax.ShapeDtypeStruct((8, 128), F32)),
+        in_specs=[vmem()] * 6 + [pl.BlockSpec(memory_space=pltpu.SMEM)],
+        out_specs=(vmem(), vmem()),
         scratch_shapes=[
             pltpu.VMEM((BANDS * PAY, arrivals), BF16),
             pltpu.VMEM((BOX, arrivals), BF16),
@@ -441,6 +442,7 @@
         col.reshape(-1, 128),
         frac,
         place.reshape(2, 128),
+        scale,
     )
     came = lax.all_to_all(sent, "band", split_axis=0, concat_axis=0, tiled=True)
     groups = BANDS + EXTRA
@@ -494,7 +496,7 @@
         return pl.pallas_call(
             functools.partial(sums_kernel, len(blocks), kind),
             out_shape=out_shape,
-            in_specs=[pl.BlockSpec(memory_space=pltpu.SMEM)] + [vmem()] * (len(blocks) + len(before)),
+            in_specs=[vmem()] * (1 + len(blocks) + len(before)),
             out_specs=(vmem(),) * len(out_shape),
             scratch_shapes=scratch,
             compiler_params=params(32),
@@ -502,7 +504,7 @@
                 flops=len(blocks) * 1_200_000_000, bytes_accessed=len(blocks) * 200_000, transcendentals=0
             ),
             name=kind + "_sums",
-        )(scale, *blocks, *before)
+        )(scales, *blocks, *before)
 
     far, after, ahead = (along(own, steps) for steps in (2, 1, -1))
     near = [own, across(own)]

time: 49.2 us -> 48.7 us (0.990)
  Pallas kernels: 14.6 us -> 12.2 us
  waiting for transfers between devices: 9.36 us -> 10.7 us
  local copies, waits for them, and re-layouts: 1.85 us -> 2.39 us
    pallas_call x4, Pallas kernels: 8.49 us -> 6.03 us  [sums(): pl.pallas_call(functools.partial(sums_kernel, len(blocks), kind), out_sha...]
    ppermute x3, waiting for transfers between devices: 5.39 us -> 6.11 us  [along(): return lax.ppermute(value, 'obs', order)]
    ppermute x1, waiting for transfers between devices: 2.51 us -> 3.09 us  [fast_features(): edge = lax.ppermute(edge, ('band', 'obs'), down + up)]
    unnamed x20, local copies, waits for them, and re-layouts: 1.33 us -> 1.87 us
  transfers between devices with their start and end apart: 8 -> 8, of which waited for: 7 -> 7; matrix products, arithmetic and copies ran while one was open for 1% -> 1% of each run, Pallas kernels for 20% -> 16%
where the time goes in v5:
time: 48.7 us; the launch traced here: 48.4 us
  blocking collectives  14.2 us (29%)
  Pallas kernels  12.2 us (25%)
  waiting for transfers between devices  10.7 us (22%)
  starting transfers between devices  7.85 us (16%)
  local copies, waits for them, and re-layouts  2.39 us (5%)
  between operations  0.86 us (2%)
    all_to_all x1, blocking collectives, fast_features(): came = lax.all_to_all(sent, 'band', split_axis=0, concat_axis=0, tiled=True)  14.2 us
    ppermute x3, waiting for transfers between devices, along(): return lax.ppermute(value, 'obs', order)  6.11 us
    pallas_call x4, Pallas kernels, sums(): pl.pallas_call(functools.partial(sums_kernel, len(blocks), kind), out_sha...  6.03 us
    ppermute x3, starting transfers between devices, along(): return lax.ppermute(value, 'obs', order)  5.97 us
    ppermute x1, waiting for transfers between devices, fast_features(): edge = lax.ppermute(edge, ('band', 'obs'), down + up)  3.09 us
    pallas_call x1, Pallas kernels, fast_features(): pl.pallas_call(pack_kernel, out_shape=(jax.ShapeDtypeStruct((BANDS * PAY,...  2.47 us
    unnamed x20, local copies, waits for them, and re-layouts  1.87 us
    pallas_call x1, Pallas kernels, body(): pl.pallas_call(local_conv_kernel, out_shape=jax.ShapeDtypeStruct((columns...  1.73 us
  transfers between devices with their start and end apart: 8, of which 7 were waited for; matrix products, arithmetic and copies ran while one was open for 1% of the time, Pallas kernels for 16%

profile of v5, /device:TPU:8, one launch (start us, length us, event | category | flops | bytes accessed | tf_op | source)
XLA Modules:
  0.0 48.4 jit_solution(2956191010969807559)
XLA Ops:
  0.0 2.5 %pack.1 = (bf16[512,256]{1,0:T(8,128)(2,1)S(1)}, f32[8,128]{1,0:T(8,128)S(1)}) custom-call(bf16[24,2048]{1,0:T(8,128)(2,1)} %values_ref.1, s32[16,128]{1,0:T(8,128)} %bitcast.90, s32[16,128]{1,0:T(8,128)} %bitcast.95, s32[16,128]{1,0:T(8,128)} %bitcast.96, f32[2,2048]{1,0:T(2,128)} %frac_ref.1, s32[2,128]{1,0:T(2,128)} %bitcast.99, f32[2]{0:T(128)} %scale_ref.1), custom_call_target="tpu_custom_call" | custom-call | tf_op jit(solution)/shard_map/pack/pallas_call | solution.py:427
  2.5 14.2 %all_to_all.24 = bf16[16,32,256]{2,1,0:T(8,128)(2,1)S(1)} all-to-all(bf16[16,32,256]{2,1,0:T(8,128)(2,1)S(1)} %bitcast.81), channel_id=1, replica_groups=mesh['band'=16,'obs'=8] {'band'}, dimensions={0} | all-to-all | bytes 524288 | tf_op jit(solution)/shard_map/all_to_all | solution.py:447
  16.6 1.4 %regroup.1.refs_0_ = bf16[736,128]{1,0:T(8,128)(2,1)S(1)} custom-call(bf16[512,256]{1,0:T(8,128)(2,1)S(1)} %bitcast.80), custom_call_target="tpu_custom_call" | custom-call | tf_op jit(solution)/shard_map/regroup/pallas_call | solution.py:449
  18.0 0.1 collective-permute-start.5
  18.1 2.0 %collective-permute-start.2 = (bf16[736,128]{1,0:T(8,128)(2,1)S(1)}, bf16[736,128]{1,0:T(8,128)(2,1)S(1)}, u32[]{:S(2)}, u32[]{:S(2)}) collective-permute-start(bf16[736,128]{1,0:T(8,128)(2,1)S(1)} %regroup.1.refs_0_), channel_id=1, source_target_pairs={{0,2},{1,3},{2,4},{3,5},{4,6},{5,7},{6,0},{7,1},{8,10},{9,11},{10,... | collective-permute-start | bytes 565256 | tf_op jit(solution)/shard_map/ppermute | solution.py:466
  20.1 2.2 %collective-permute-start.3 = (bf16[736,128]{1,0:T(8,128)(2,1)S(1)}, bf16[736,128]{1,0:T(8,128)(2,1)S(1)}, u32[]{:S(2)}, u32[]{:S(2)}) collective-permute-start(bf16[736,128]{1,0:T(8,128)(2,1)S(1)} %regroup.1.refs_0_), channel_id=1, source_target_pairs={{0,6},{1,7},{2,0},{3,1},{4,2},{5,3},{6,4},{7,5},{8,14},{9,15},{10,... | collective-permute-start | bytes 565256 | tf_op jit(solution)/shard_map/ppermute | solution.py:466
  22.3 1.8 %collective-permute-start.4 = (bf16[736,128]{1,0:T(8,128)(2,1)S(1)}, bf16[736,128]{1,0:T(8,128)(2,1)S(1)}, u32[]{:S(2)}, u32[]{:S(2)}) collective-permute-start(bf16[736,128]{1,0:T(8,128)(2,1)S(1)} %regroup.1.refs_0_), channel_id=1, source_target_pairs={{0,4},{1,5},{2,6},{3,7},{4,0},{5,1},{6,2},{7,3},{8,12},{9,13},{10,... | collective-permute-start | bytes 565256 | tf_op jit(solution)/shard_map/ppermute | solution.py:466
  24.1 0.0 collective-permute-done.5.refs_1_
  24.1 1.5 %part_sums.1 = (f32[1632,256]{1,0:T(8,128)S(1)}, f32[8,128]{1,0:T(8,128)S(1)}) custom-call(f32[8,128]{1,0:T(8,128)S(1)} %get-tuple-element.222.scale_ref, bf16[736,128]{1,0:T(8,128)(2,1)S(1)} %regroup.1.refs_0_, bf16[736,128]{1,0:T(8,128)(2,1)S(1)} %collective-permute-done.5.refs_1_), custom_call_target="tpu_custom_call" | custom-call | flops 2400000000 | bytes 400000 | tf_op jit(solution)/shard_map/part_sums/pallas_call | solution.py:496
  25.6 0.0 copy-start.9
  25.6 1.0 %copy-done.9 = bf16[5,5,25,256]{3,2,1,0:T(8,128)(2,1)S(1)} copy-done((bf16[5,5,25,256]{3,2,1,0:T(8,128)(2,1)S(1)}, bf16[5,5,25,256]{3,2,1,0:T(8,128)(2,1)}, u32[]{:S(2)}) %copy-start.9) | copy-done | bytes 320024
  26.6 0.1 weights.1.w_ref
  26.7 0.9 %collective-permute-done.2.refs_0_ = bf16[736,128]{1,0:T(8,128)(2,1)S(1)} collective-permute-done((bf16[736,128]{1,0:T(8,128)(2,1)S(1)}, bf16[736,128]{1,0:T(8,128)(2,1)S(1)}, u32[]{:S(2)}, u32[]{:S(2)}) %collective-permute-start.2) | collective-permute-done | bytes 188448 | tf_op jit(solution)/shard_map/ppermute | solution.py:466
  27.5 3.3 %collective-permute-done.3.refs_1_ = bf16[736,128]{1,0:T(8,128)(2,1)S(1)} collective-permute-done((bf16[736,128]{1,0:T(8,128)(2,1)S(1)}, bf16[736,128]{1,0:T(8,128)(2,1)S(1)}, u32[]{:S(2)}, u32[]{:S(2)}) %collective-permute-start.3) | collective-permute-done | bytes 188448 | tf_op jit(solution)/shard_map/ppermute | solution.py:466
  30.9 1.9 %collective-permute-done.4.refs_2_ = bf16[736,128]{1,0:T(8,128)(2,1)S(1)} collective-permute-done((bf16[736,128]{1,0:T(8,128)(2,1)S(1)}, bf16[736,128]{1,0:T(8,128)(2,1)S(1)}, u32[]{:S(2)}, u32[]{:S(2)}) %collective-permute-start.4) | collective-permute-done | bytes 188448 | tf_op jit(solution)/shard_map/ppermute | solution.py:466
  32.8 0.0 collective-permute-start.6
  32.8 0.5 %collective-permute-start.7 = (bf16[736,128]{1,0:T(8,128)(2,1)S(1)}, bf16[736,128]{1,0:T(8,128)(2,1)S(1)}, u32[]{:S(2)}, u32[]{:S(2)}) collective-permute-start(bf16[736,128]{1,0:T(8,128)(2,1)S(1)} %collective-permute-done.3.refs_1_), channel_id=1, source_target_pairs={{0,1},{1,0},{2,3},{3,2},{4,5},{5,4},{6,7},{7,6},{8,9},{9,8},{10,11... | collective-permute-start | bytes 565256 | tf_op jit(solution)/shard_map/ppermute | solution.py:469
  33.3 0.0 collective-permute-start.8
  33.3 0.9 %collective-permute-done.6.refs_3_ = bf16[736,128]{1,0:T(8,128)(2,1)S(1)} collective-permute-done((bf16[736,128]{1,0:T(8,128)(2,1)S(1)}, bf16[736,128]{1,0:T(8,128)(2,1)S(1)}, u32[]{:S(2)}, u32[]{:S(2)}) %collective-permute-start.6) | collective-permute-done | bytes 188448 | tf_op jit(solution)/shard_map/ppermute | solution.py:469
  34.2 0.3 collective-permute-done.7.refs_4_
  34.5 0.3 collective-permute-done.8.refs_5_
  34.8 0.0 copy-start.8
  34.8 1.3 %collective-permute-start.9 = (bf16[720,128]{1,0:T(8,128)(2,1)S(1)}, bf16[720,128]{1,0:T(8,128)(2,1)S(1)}, u32[]{:S(2)}, u32[]{:S(2)}) collective-permute-start(bf16[720,128]{1,0:T(8,128)(2,1)S(1)} %edge_sums.1), channel_id=1, source_target_pairs={{4,8},{12,16},{20,24},{28,32},{36,40},{44,48},{52,56},{60,64},{68,... | collective-permute-start | bytes 552968 | tf_op jit(solution)/shard_map/ppermute | solution.py:530
  36.1 4.5 %last_sums.1 = (bf16[720,512]{1,0:T(8,128)(2,1)S(1)}, f32[8,128]{1,0:T(8,128)S(1)}) custom-call(f32[8,128]{1,0:T(8,128)S(1)} %get-tuple-element.222.scale_ref, bf16[736,128]{1,0:T(8,128)(2,1)S(1)} %collective-permute-done.2.refs_0_, bf16[736,128]{1,0:T(8,128)(2,1)S(1)} %collective-permute-done.3.refs_1_, ...), custom_call_target="tpu_custom_call" | custom-call | flops 7200000000 | bytes 1200000 | tf_op jit(solution)/shard_map/last_sums/pallas_call | solution.py:496
  40.6 0.0 copy-start.1
  40.6 0.0 copy-start.2
  40.7 0.0 copy-start.3
  40.7 0.0 copy-start.4
  40.7 0.0 copy-start.5
  40.7 0.0 copy-start.6
  40.7 0.0 copy-start.7
  40.7 0.5 %slice.89 = f32[1,1]{1,0:T(1,128)} slice(f32[8,128]{1,0:T(8,128)S(1)} %get-tuple-element.242), slice={[0:1], [0:1]} | slice | bytes 8 | tf_op jit(solution)/shard_map/slice | solution.py:693
  41.9 0.0 copy-done.8
  41.9 1.7 %local_conv.1 = f32[720,512]{1,0:T(8,128)S(1)} custom-call(bf16[720,512]{1,0:T(8,128)(2,1)S(1)} %get-tuple-element.244.feature_ref, bf16[3,512,512]{2,1,0:T(8,128)(2,1)S(1)} %weights.1.w_ref, f32[1,256]{1,0:T(1,128)S(1)} %bitcast.100), custom_call_target="tpu_custom_call" | custom-call | flops 2000000000 | bytes 4000000 | tf_op jit(solution)/shard_map/local_conv/pallas_call | solution.py:667
  43.6 3.1 %collective-permute-done.9 = bf16[720,128]{1,0:T(8,128)(2,1)S(1)} collective-permute-done((bf16[720,128]{1,0:T(8,128)(2,1)S(1)}, bf16[720,128]{1,0:T(8,128)(2,1)S(1)}, u32[]{:S(2)}, u32[]{:S(2)}) %collective-permute-start.9) | collective-permute-done | bytes 184352 | tf_op jit(solution)/shard_map/ppermute | solution.py:530
  46.7 0.0 copy-done.1
  46.7 0.0 copy-done.2
  46.7 0.0 copy-done.3
  46.7 0.0 copy-done.4
  46.7 0.0 copy-done.5
  46.7 0.0 copy-done.6
  46.8 0.0 copy-done.7
  46.8 0.8 %conditional.1 = (bf16[2,720,256]{2,1,0:T(8,128)(2,1)S(1)}) conditional(s32[]{:T(128)} %bitcast.23, (f32[720,512]{1,0:T(8,128)S(1)}, bf16[720,128]{1,0:T(8,128)(2,1)S(1)}, bf16[3,512,512]{2,1,0:T(8,128)(2,1)S(1)}) %tuple.38, (s32[2048]{0:T(1024)S(1)}, bf16[24,2048]{1,0:T(8,128)(2,1)S(1)}, s32[2048]{0:T(1024)S(1)}, f32[2,2048]{1,0:T(2,128)S(1)}, ...), branch_computations={%region_0.0_spmd, %region_1.13_spmd} | conditional | flops 1663610880 | bytes 171243296 | solution.py:693
  46.8 0.5 %conv.1 = bf16[2,720,256]{2,1,0:T(8,128)(2,1)S(1)} custom-call(f32[720,512]{1,0:T(8,128)S(1)} %get-tuple-element.174.part_ref, bf16[720,128]{1,0:T(8,128)(2,1)S(1)} %get-tuple-element.175.edge_ref, bf16[3,512,512]{2,1,0:T(8,128)(2,1)S(1)} %get-tuple-element.176.w_ref), custom_call_target="tpu_custom_call" | custom-call | tf_op jit(solution)/shard_map/cond/branch_0_fun/conv/pallas_call | solution.py:680
  47.6 0.0 copy-start
  47.6 0.9 %copy-done = bf16[2,720,256]{2,1,0:T(8,128)(2,1)} copy-done((bf16[2,720,256]{2,1,0:T(8,128)(2,1)}, bf16[2,720,256]{2,1,0:T(8,128)(2,1)S(1)}, u32[]{:S(2)}) %copy-start) | copy-done | bytes 737304
  (2 shorter events, 0.0 us)
Async XLA Ops:
  18.0 6.1 %collective-permute-start.5 = (bf16[736,128]{1,0:T(8,128)(2,1)S(1)}, bf16[736,128]{1,0:T(8,128)(2,1)S(1)}, u32[]{:S(2)}, u32[]{:S(2)}) collective-permute-start(bf16[736,128]{1,0:T(8,128)(2,1)S(1)} %regroup.1.refs_0_), channel_id=1, source_target_pairs={{0,1},{1,0},{2,3},{3,2},{4,5},{5,4},{6,7},{7,6},{8,9},{9,8},{10,11... | collective-permute-start | bytes 565256 | tf_op jit(solution)/shard_map/ppermute | solution.py:469
  18.1 9.4 %collective-permute-start.2 = (bf16[736,128]{1,0:T(8,128)(2,1)S(1)}, bf16[736,128]{1,0:T(8,128)(2,1)S(1)}, u32[]{:S(2)}, u32[]{:S(2)}) collective-permute-start(bf16[736,128]{1,0:T(8,128)(2,1)S(1)} %regroup.1.refs_0_), channel_id=1, source_target_pairs={{0,2},{1,3},{2,4},{3,5},{4,6},{5,7},{6,0},{7,1},{8,10},{9,11},{10,... | collective-permute-start | bytes 565256 | tf_op jit(solution)/shard_map/ppermute | solution.py:466
  20.1 10.8 %collective-permute-start.3 = (bf16[736,128]{1,0:T(8,128)(2,1)S(1)}, bf16[736,128]{1,0:T(8,128)(2,1)S(1)}, u32[]{:S(2)}, u32[]{:S(2)}) collective-permute-start(bf16[736,128]{1,0:T(8,128)(2,1)S(1)} %regroup.1.refs_0_), channel_id=1, source_target_pairs={{0,6},{1,7},{2,0},{3,1},{4,2},{5,3},{6,4},{7,5},{8,14},{9,15},{10,... | collective-permute-start | bytes 565256 | tf_op jit(solution)/shard_map/ppermute | solution.py:466
  22.3 10.5 %collective-permute-start.4 = (bf16[736,128]{1,0:T(8,128)(2,1)S(1)}, bf16[736,128]{1,0:T(8,128)(2,1)S(1)}, u32[]{:S(2)}, u32[]{:S(2)}) collective-permute-start(bf16[736,128]{1,0:T(8,128)(2,1)S(1)} %regroup.1.refs_0_), channel_id=1, source_target_pairs={{0,4},{1,5},{2,6},{3,7},{4,0},{5,1},{6,2},{7,3},{8,12},{9,13},{10,... | collective-permute-start | bytes 565256 | tf_op jit(solution)/shard_map/ppermute | solution.py:466
  25.6 1.0 %copy-start.9 = (bf16[5,5,25,256]{3,2,1,0:T(8,128)(2,1)S(1)}, bf16[5,5,25,256]{3,2,1,0:T(8,128)(2,1)}, u32[]{:S(2)}) copy-start(bf16[5,5,25,256]{3,2,1,0:T(8,128)(2,1)} %weight_ref) | copy-start | bytes 960004
  32.8 1.4 %collective-permute-start.6 = (bf16[736,128]{1,0:T(8,128)(2,1)S(1)}, bf16[736,128]{1,0:T(8,128)(2,1)S(1)}, u32[]{:S(2)}, u32[]{:S(2)}) collective-permute-start(bf16[736,128]{1,0:T(8,128)(2,1)S(1)} %collective-permute-done.2.refs_0_), channel_id=1, source_target_pairs={{0,1},{1,0},{2,3},{3,2},{4,5},{5,4},{6,7},{7,6},{8,9},{9,8},{10,11... | collective-permute-start | bytes 565256 | tf_op jit(solution)/shard_map/ppermute | solution.py:469
  32.8 1.7 %collective-permute-start.7 = (bf16[736,128]{1,0:T(8,128)(2,1)S(1)}, bf16[736,128]{1,0:T(8,128)(2,1)S(1)}, u32[]{:S(2)}, u32[]{:S(2)}) collective-permute-start(bf16[736,128]{1,0:T(8,128)(2,1)S(1)} %collective-permute-done.3.refs_1_), channel_id=1, source_target_pairs={{0,1},{1,0},{2,3},{3,2},{4,5},{5,4},{6,7},{7,6},{8,9},{9,8},{10,11... | collective-permute-start | bytes 565256 | tf_op jit(solution)/shard_map/ppermute | solution.py:469
  33.3 1.5 %collective-permute-start.8 = (bf16[736,128]{1,0:T(8,128)(2,1)S(1)}, bf16[736,128]{1,0:T(8,128)(2,1)S(1)}, u32[]{:S(2)}, u32[]{:S(2)}) collective-permute-start(bf16[736,128]{1,0:T(8,128)(2,1)S(1)} %collective-permute-done.4.refs_2_), channel_id=1, source_target_pairs={{0,1},{1,0},{2,3},{3,2},{4,5},{5,4},{6,7},{7,6},{8,9},{9,8},{10,11... | collective-permute-start | bytes 565256 | tf_op jit(solution)/shard_map/ppermute | solution.py:469
  34.8 7.1 %copy-start.8 = (f32[256]{0:T(256)S(1)}, f32[256]{0:T(256)}, u32[]{:S(2)}) copy-start(f32[256]{0:T(256)} %param.25) | copy-start | bytes 3076
  34.8 11.9 %collective-permute-start.9 = (bf16[720,128]{1,0:T(8,128)(2,1)S(1)}, bf16[720,128]{1,0:T(8,128)(2,1)S(1)}, u32[]{:S(2)}, u32[]{:S(2)}) collective-permute-start(bf16[720,128]{1,0:T(8,128)(2,1)S(1)} %edge_sums.1), channel_id=1, source_target_pairs={{4,8},{12,16},{20,24},{28,32},{36,40},{44,48},{52,56},{60,64},{68,... | collective-permute-start | bytes 552968 | tf_op jit(solution)/shard_map/ppermute | solution.py:530
  40.6 6.1 %copy-start.1 = (bf16[24,2048]{1,0:T(8,128)(2,1)S(1)}, bf16[24,2048]{1,0:T(8,128)(2,1)}, u32[]{:S(2)}) copy-start(bf16[24,2048]{1,0:T(8,128)(2,1)} %values_ref.1) | copy-start | bytes 294916
  40.6 6.1 %copy-start.2 = (s32[2048]{0:T(1024)S(1)}, s32[2048]{0:T(1024)}, u32[]{:S(2)}) copy-start(s32[2048]{0:T(1024)} %param.18) | copy-start | bytes 24580
  40.7 6.1 %copy-start.3 = (f32[2,2048]{1,0:T(2,128)S(1)}, f32[2,2048]{1,0:T(2,128)}, u32[]{:S(2)}) copy-start(f32[2,2048]{1,0:T(2,128)} %frac_ref.1) | copy-start | bytes 49156
  40.7 6.1 %copy-start.4 = (s32[2048]{0:T(1024)S(1)}, s32[2048]{0:T(1024)}, u32[]{:S(2)}) copy-start(s32[2048]{0:T(1024)} %param.19) | copy-start | bytes 24580
  40.7 6.1 %copy-start.5 = (s32[2048]{0:T(1024)S(1)}, s32[2048]{0:T(1024)}, u32[]{:S(2)}) copy-start(s32[2048]{0:T(1024)} %param.20) | copy-start | bytes 24580
  40.7 6.1 %copy-start.6 = (f32[2]{0:T(128)S(1)}, f32[2]{0:T(128)}, u32[]{:S(2)}) copy-start(f32[2]{0:T(128)} %scale_ref.1) | copy-start | bytes 28
  40.7 6.1 %copy-start.7 = (s32[256]{0:T(256)S(1)}, s32[256]{0:T(256)}, u32[]{:S(2)}) copy-start(s32[256]{0:T(256)} %param.22) | copy-start | bytes 3076
  47.6 0.9 %copy-start = (bf16[2,720,256]{2,1,0:T(8,128)(2,1)}, bf16[2,720,256]{2,1,0:T(8,128)(2,1)S(1)}, u32[]{:S(2)}) copy-start(bf16[2,720,256]{2,1,0:T(8,128)(2,1)S(1)} %get-tuple-element.429) | copy-start | bytes 2211844
